TPU v7x, 256 devices: a whole 4x4x8 slice. The times are simulated.
256 devices in a mesh: ax: 4 (over y), az: 64 (over x, z, core).
Axes of the slice: x: 4, y: 4, z: 8, core: 2. Of those that a mesh axis runs over, the one named last changes fastest.
Arguments:
- fraction: float32 [2048, 32, 512], P('az', 'ax'), may hold values from 0 to 1
- courant_axial: float32 [2048, 32, 512], P('az', 'ax'), may hold values from -0.45 to 0.45
- courant_azimuth: float32 [2048, 32, 512], P('az', 'ax'), may hold values from -0.45 to 0.45
- courant_radial: float32 [2048, 32, 512], P('az', 'ax'), may hold values from -0.45 to 0.45
- plane_code: int32 [2048, 512], P('az', 'ax'), may hold values from 0 to 4095
- strip_width: float32 [2048, 512], P('az', 'ax'), may hold values from 0.25 to 0.75
- tile_reader: int32 [2048, 32], P('az', 'ax'), may hold values from 0 to 63, as said below
- landing_column: int32 [2048, 32], P('az', 'ax'), may hold values from 0 to 31
Outputs:
- fraction_new: float32 [2048, 32, 512], P('az', 'ax')
Inputs may be any that keep to these rules, and one draw needn't show every extreme that they name: `tile_reader`: among the 32 x 8 rows (column, plane) of one device's block at most 8 name the same reader, and in every such block exactly 8 name some reader.
All inputs are finite; a program needn't handle non-finite values.
Results may differ from a plain program's by a relative error of at most 0.000057.
Values sent between devices are 32-bit elements; how exact they have to be, the bound alone decides.
No kernel may reach another device: no remote copies, remote signals or barrier semaphores. Data moves between devices by JAX's collectives and lax.ppermute only.
A program may use at most 64 MiB of HBM per device.

v0:
```python
import math

import jax
import jax.numpy as jnp
from jax import lax
from jax.sharding import PartitionSpec as P

R_AX = 64
XR = 16


highest = lax.Precision.HIGHEST


def extended_2(cells, sides, width):
    for axis, dim in sides:
        count = lax.axis_size(axis)
        head = lax.slice_in_dim(cells, 0, width, axis=dim)
        tail = lax.slice_in_dim(cells, cells.shape[dim] - width, cells.shape[dim], axis=dim)
        cells = jnp.concatenate(
            [
                lax.ppermute(tail, axis, [(i, (i + 1) % count) for i in range(count)]),
                cells,
                lax.ppermute(head, axis, [((i + 1) % count, i) for i in range(count)]),
            ],
            axis=dim,
        )
    return cells


def upwind(courant, below_cell, above_cell):
    return jnp.maximum(courant, 0.0) * below_cell + jnp.minimum(courant, 0.0) * above_cell


def valid_sweep(values, courant, sweep_axis):
    cell_count = values.shape[sweep_axis]
    face_flux = upwind(
        lax.slice_in_dim(courant, 0, cell_count - 1, axis=sweep_axis),
        lax.slice_in_dim(values, 0, cell_count - 1, axis=sweep_axis),
        lax.slice_in_dim(values, 1, cell_count, axis=sweep_axis),
    )
    middle = lax.slice_in_dim(values, 1, cell_count - 1, axis=sweep_axis)
    upper_flux = lax.slice_in_dim(face_flux, 1, cell_count - 1, axis=sweep_axis)
    lower_flux = lax.slice_in_dim(face_flux, 0, cell_count - 2, axis=sweep_axis)
    return middle - (upper_flux - lower_flux)


def radial_sweep(values, courant):
    above_cell = jnp.concatenate([values[:, :, 1:], jnp.zeros_like(values[:, :, :1])], axis=2)
    face_flux = upwind(courant, values, above_cell)
    radius = lax.iota(jnp.int32, values.shape[2]).astype(jnp.float32)
    outer_flux = (radius + 1.0) * face_flux
    inner_flux = jnp.concatenate(
        [jnp.zeros_like(outer_flux[:, :, :1]), outer_flux[:, :, :-1]], axis=2
    )
    return values - (outer_flux - inner_flux) / (radius + 0.5)


def axial_half(values, courant):
    extended = extended_2(jnp.stack([values, courant]), (("ax", 2),), 1)
    return valid_sweep(extended[0], extended[1], 1)


def sector_half(values, courant):
    extended = extended_2(jnp.stack([values, courant]), (("az", 1),), 1)
    return valid_sweep(extended[0], extended[1], 0)


def dft_tables(first_row, row_count, mode_count, column_count):
    row_index = first_row + lax.iota(jnp.int32, row_count)
    mode_index = lax.iota(jnp.int32, mode_count)
    phase = row_index[:, None] * mode_index[None, :] % column_count
    angle_table = phase.astype(jnp.float32) * (2.0 * math.pi / column_count)
    return (jnp.cos(angle_table), jnp.sin(angle_table))


def damping(cycle_count, mode_count, column_count):
    mode_index = lax.iota(jnp.int32, mode_count).astype(jnp.float32)[:, None]
    cycle_index = lax.iota(jnp.int32, cycle_count).astype(jnp.float32)[None, :]
    cutoff = (cycle_index + 1.0) * (column_count / 1024.0)
    weight = jnp.where(mode_index == 0.0, 1.0, 2.0) / column_count
    return weight * jnp.exp(-((mode_index / cutoff) ** 2))


def circulant_columns(first_column, column_share, gathered_cycles):
    column_count = gathered_cycles.shape[0]
    cycle_count = gathered_cycles.shape[2]
    scale = damping(cycle_count, column_count // 2, column_count)
    table_rows = column_count // 8

    def table_block(block_index):
        cos_table, sin_table = dft_tables(
            block_index * table_rows, table_rows, column_count // 2, column_count
        )
        return jnp.dot(cos_table, scale, precision=highest, preferred_element_type=jnp.float32)

    kernel = lax.map(table_block, lax.iota(jnp.int32, 8)).reshape(column_count, cycle_count)
    doubled = jnp.concatenate([kernel, kernel], axis=0)
    block_cols = math.gcd(column_share, 8)

    def column_block(block_index):
        first = first_column + block_index * block_cols
        picked = jnp.stack(
            [
                lax.dynamic_slice_in_dim(doubled, column_count - first - offset, column_count, 0)
                for offset in range(block_cols)
            ]
        )
        return jnp.einsum(
            "jnr,npr->jpr",
            picked,
            gathered_cycles,
            precision=highest,
            preferred_element_type=jnp.float32,
        )

    blocks_out = lax.map(column_block, lax.iota(jnp.int32, column_share // block_cols))
    return blocks_out.reshape(column_share, gathered_cycles.shape[1], cycle_count)


def plic_volume(plane_code, strip_width):
    normal = (plane_code // 64).astype(jnp.float32)
    offset = (plane_code % 64).astype(jnp.float32)
    plane_angle = math.pi / 16 + (normal + 0.5) * (3 * math.pi / 512)
    normal_along = jnp.cos(plane_angle)
    across = jnp.sin(plane_angle)
    plane_level = (offset + 0.5) * (normal_along + across) / 64.0
    strip_span = strip_width * normal_along

    def square(shift_value):
        return jnp.maximum(shift_value, 0.0) ** 2

    strip_area = (
        square(plane_level)
        - square(plane_level - strip_span)
        - square(plane_level - across)
        + square(plane_level - strip_span - across)
    ) / (2.0 * strip_span * across)
    return strip_width * strip_area


def local(
    fraction,
    courant_axial,
    courant_azimuth,
    courant_radial,
    plane_code,
    strip_width,
    tile_reader,
    landing_column,
):
    swept_field = axial_half(fraction, courant_axial)
    swept_field = sector_half(swept_field, courant_azimuth)
    swept_field = radial_sweep(swept_field, courant_radial)
    swept_field = sector_half(swept_field, courant_azimuth)
    swept_field = axial_half(swept_field, courant_axial)
    sector = fraction.shape[0]
    plane_count = fraction.shape[1]
    near_cycles = swept_field[:, :, :R_AX]
    gathered_cycles = lax.all_gather(near_cycles, "az", axis=0, tiled=True)
    filtered_near = circulant_columns(lax.axis_index("az") * sector, sector, gathered_cycles)
    filtered = jnp.concatenate([filtered_near, swept_field[:, :, R_AX:]], axis=2)
    volume = plic_volume(plane_code, strip_width)
    devices = lax.axis_size("az")
    row_count = sector * plane_count
    capacity = max(2, 2 * row_count // devices)
    volume_rows = volume.reshape(row_count, -1)
    reader = tile_reader.reshape(row_count)
    row_index = lax.iota(jnp.int32, row_count)
    target_row = landing_column.reshape(row_count) * plane_count + row_index % plane_count
    same_reader = reader[:, None] == reader[None, :]
    earlier = row_index[None, :] < row_index[:, None]
    rank = jnp.sum((same_reader & earlier).astype(jnp.int32), axis=1)
    slot_index = reader * capacity + rank
    slot_match = slot_index[None, :] == lax.iota(jnp.int32, devices * capacity)[:, None]
    send_volume = jnp.dot(
        slot_match.astype(jnp.float32),
        volume_rows,
        precision=highest,
        preferred_element_type=jnp.float32,
    )
    send_target = jnp.sum(slot_match.astype(jnp.int32) * (target_row + 1)[None, :], axis=1) - 1
    got_volume, got_target = (
        lax.all_to_all(
            send_volume.reshape(devices, capacity, -1),
            "az",
            split_axis=0,
            concat_axis=0,
            tiled=True,
        ),
        lax.all_to_all(
            send_target.reshape(devices, capacity), "az", split_axis=0, concat_axis=0, tiled=True
        ),
    )
    arrive_table = (got_target.reshape(-1)[None, :] == row_index[:, None]).astype(jnp.float32)
    arrived = jnp.dot(
        arrive_table,
        got_volume.reshape(devices * capacity, -1),
        precision=highest,
        preferred_element_type=jnp.float32,
    ).reshape(sector, -1)
    inner_cycles = filtered[:, :, :XR].reshape(sector, -1) - volume + arrived
    return jnp.concatenate([inner_cycles.reshape(sector, -1, XR), filtered[:, :, XR:]], axis=2)


def solution(mesh):
    return jax.shard_map(
        local,
        mesh=mesh,
        in_specs=(
            P("az", "ax", None),
            P("az", "ax", None),
            P("az", "ax", None),
            P("az", "ax", None),
            P("az", "ax"),
            P("az", "ax"),
            P("az", "ax"),
            P("az", "ax"),
        ),
        out_specs=P("az", "ax", None),
        check_vma=False,
    )
```

profile of v0, /device:TPU:1, one launch (start us, length us, event | category | flops | bytes accessed | tf_op | source)
XLA Modules:
  0.0 280.9 jit_solution(18038076299585697154)
XLA Ops:
  17.8 3.7 %collective-permute-start.2 = (f32[2,1,8,512]{3,2,1,0:T(8,128)S(1)}, f32[2,1,8,512]{3,2,1,0:T(8,128)S(1)}, u32[]{:S(2)}, u32[]{:S(2)}) collective-permute-start(f32[2,1,8,512]{3,2,1,0:T(8,128)S(1)} %get-tuple-element.287), channel_id=1, source_target_pairs={{0,1},{1,2},{2,3},{3,4},{4,5},{5,6},{6,7},{7,8},{8,9},{9,10},{10,1... | collective-permute-start | bytes 98312 | tf_op jit(solution)/shard_map/ppermute | solution.py:22
  26.7 3.5 %collective-permute-start.5 = (f32[2,1,8,512]{3,2,1,0:T(8,128)S(1)}, f32[2,1,8,512]{3,2,1,0:T(8,128)S(1)}, u32[]{:S(2)}, u32[]{:S(2)}) collective-permute-start(f32[2,1,8,512]{3,2,1,0:T(8,128)S(1)} %get-tuple-element.286), channel_id=1, source_target_pairs={{1,0},{2,1},{3,2},{4,3},{5,4},{6,5},{7,6},{8,7},{9,8},{10,9},{11,1... | collective-permute-start | bytes 98312 | tf_op jit(solution)/shard_map/ppermute | solution.py:24
  40.7 13.1 %all-to-all-start = ((s32[64,1,8]{2,1,0:T(1,128)}), s32[64,1,8]{2,1,0:T(1,128)S(1)}, u32[]{:S(2)}, u32[]{:S(2)}) async-start(s32[64,1,8]{2,1,0:T(1,128)} %bitcast.17), calls=%async_computation | async-start | bytes 65536 | tf_op jit(solution)/shard_map/all_to_all | solution.py:191
  54.1 57.7 %while.28 = (s32[]{:T(128)}, f32[8,256,64]{1,0,2:T(8,128)S(1)}, s32[8]{0:T(128)S(1)}, f32[64]{0:T(128)S(1)}, f32[1024]{0:T(1024)S(1)}, /*index=5*/f32[1024]{0:T(1024)S(1)}, s32[]{:T(128)}, s32[1]{0:T(128)}, s32[]{:T(128)}) while((s32[]{:T(128)}, f32[8,256,64]{1,0,2:T(8,128)S(1)}, s32[8]{0:T(128)S(1)}, f32[64]{0:T(128)S(1)}, ...), condition=%wide.region_1.2_spmd.clone, body=%wide.region_0.1_spmd.clone.sunk | while | flops 205259008 | bytes 338301 | solution.py:97
  55.3 5.1 %convolution_bitcast_fusion.5 = f32[1,256,64]{1,2,0:T(8,128)S(1)} fusion(s32[256]{0:T(256)S(1)} %iota_add_fusion.2, f32[64]{0:T(128)S(1)} %get-tuple-element.402, f32[1024]{0:T(1024)S(1)} %get-tuple-element.403, f32[1024]{0:T(1024)S(1)} %get-tuple-element.404), kind=kOutput, calls=%fused_computation.14.clone.1 | convolution fusion | flops 205258752 | bytes 75008 | tf_op jit(solution)/shard_map/while/body/eval_jaxpr/dot_general | solution.py:95
  62.5 5.1 %convolution_bitcast_fusion.5 = f32[1,256,64]{1,2,0:T(8,128)S(1)} fusion(s32[256]{0:T(256)S(1)} %iota_add_fusion.2, f32[64]{0:T(128)S(1)} %get-tuple-element.402, f32[1024]{0:T(1024)S(1)} %get-tuple-element.403, f32[1024]{0:T(1024)S(1)} %get-tuple-element.404), kind=kOutput, calls=%fused_computation.14.clone.1 | convolution fusion | flops 205258752 | bytes 75008 | tf_op jit(solution)/shard_map/while/body/eval_jaxpr/dot_general | solution.py:95
  69.7 5.1 %convolution_bitcast_fusion.5 = f32[1,256,64]{1,2,0:T(8,128)S(1)} fusion(s32[256]{0:T(256)S(1)} %iota_add_fusion.2, f32[64]{0:T(128)S(1)} %get-tuple-element.402, f32[1024]{0:T(1024)S(1)} %get-tuple-element.403, f32[1024]{0:T(1024)S(1)} %get-tuple-element.404), kind=kOutput, calls=%fused_computation.14.clone.1 | convolution fusion | flops 205258752 | bytes 75008 | tf_op jit(solution)/shard_map/while/body/eval_jaxpr/dot_general | solution.py:95
  77.0 5.1 %convolution_bitcast_fusion.5 = f32[1,256,64]{1,2,0:T(8,128)S(1)} fusion(s32[256]{0:T(256)S(1)} %iota_add_fusion.2, f32[64]{0:T(128)S(1)} %get-tuple-element.402, f32[1024]{0:T(1024)S(1)} %get-tuple-element.403, f32[1024]{0:T(1024)S(1)} %get-tuple-element.404), kind=kOutput, calls=%fused_computation.14.clone.1 | convolution fusion | flops 205258752 | bytes 75008 | tf_op jit(solution)/shard_map/while/body/eval_jaxpr/dot_general | solution.py:95
  84.2 5.1 %convolution_bitcast_fusion.5 = f32[1,256,64]{1,2,0:T(8,128)S(1)} fusion(s32[256]{0:T(256)S(1)} %iota_add_fusion.2, f32[64]{0:T(128)S(1)} %get-tuple-element.402, f32[1024]{0:T(1024)S(1)} %get-tuple-element.403, f32[1024]{0:T(1024)S(1)} %get-tuple-element.404), kind=kOutput, calls=%fused_computation.14.clone.1 | convolution fusion | flops 205258752 | bytes 75008 | tf_op jit(solution)/shard_map/while/body/eval_jaxpr/dot_general | solution.py:95
  91.4 5.1 %convolution_bitcast_fusion.5 = f32[1,256,64]{1,2,0:T(8,128)S(1)} fusion(s32[256]{0:T(256)S(1)} %iota_add_fusion.2, f32[64]{0:T(128)S(1)} %get-tuple-element.402, f32[1024]{0:T(1024)S(1)} %get-tuple-element.403, f32[1024]{0:T(1024)S(1)} %get-tuple-element.404), kind=kOutput, calls=%fused_computation.14.clone.1 | convolution fusion | flops 205258752 | bytes 75008 | tf_op jit(solution)/shard_map/while/body/eval_jaxpr/dot_general | solution.py:95
  98.6 5.1 %convolution_bitcast_fusion.5 = f32[1,256,64]{1,2,0:T(8,128)S(1)} fusion(s32[256]{0:T(256)S(1)} %iota_add_fusion.2, f32[64]{0:T(128)S(1)} %get-tuple-element.402, f32[1024]{0:T(1024)S(1)} %get-tuple-element.403, f32[1024]{0:T(1024)S(1)} %get-tuple-element.404), kind=kOutput, calls=%fused_computation.14.clone.1 | convolution fusion | flops 205258752 | bytes 75008 | tf_op jit(solution)/shard_map/while/body/eval_jaxpr/dot_general | solution.py:95
  105.8 5.1 %convolution_bitcast_fusion.5 = f32[1,256,64]{1,2,0:T(8,128)S(1)} fusion(s32[256]{0:T(256)S(1)} %iota_add_fusion.2, f32[64]{0:T(128)S(1)} %get-tuple-element.402, f32[1024]{0:T(1024)S(1)} %get-tuple-element.403, f32[1024]{0:T(1024)S(1)} %get-tuple-element.404), kind=kOutput, calls=%fused_computation.14.clone.1 | convolution fusion | flops 205258752 | bytes 75008 | tf_op jit(solution)/shard_map/while/body/eval_jaxpr/dot_general | solution.py:95
  113.3 10.3 %all-to-all-start.1 = ((f32[64,1,128]{2,1,0:T(1,128)}), f32[64,1,128]{2,1,0:T(1,128)S(1)}, u32[]{:S(2)}, u32[]{:S(2)}) async-start(f32[64,1,128]{2,1,0:T(1,128)} %reshape.174), calls=%async_computation.1 | async-start | bytes 65536 | tf_op jit(solution)/shard_map/all_to_all | solution.py:184
  125.1 7.8 %all-to-all-done.1 = f32[64,1,128]{2,1,0:T(1,128)S(1)} async-done(((f32[64,1,128]{2,1,0:T(1,128)}), f32[64,1,128]{2,1,0:T(1,128)S(1)}, u32[]{:S(2)}, u32[]{:S(2)}) %all-to-all-start.1) | async-done | bytes 32800 | tf_op jit(solution)/shard_map/all_to_all | solution.py:184
  135.8 7.7 %copy.66 = f32[2048,8,64]{0,1,2:T(8,128)} copy(f32[2048,8,64]{2,1,0:T(8,128)} %all-gather.2.cloned.1.call-done) | data formatting | bytes 8388608 | tf_op jit(solution)/shard_map/while | solution.py:117
  143.6 128.0 %while.27 = (s32[]{:T(128)}, f32[4,8,8,64]{3,2,1,0:T(8,128)S(1)}, s32[4]{0:T(128)S(1)}, s32[]{:T(128)}, f32[4096,64]{0,1:T(8,128)S(1)}, /*index=5*/f32[2048,8,64...) while((s32[]{:T(128)}, f32[4,8,8,64]{3,2,1,0:T(8,128)S(1)}, ...), condition=%wide.region_3.4_spmd, body=%wide.region_2.3_spmd.sunk | while | flops 100663328 | bytes 33669780 | solution.py:117
  152.2 11.5 %stack.140 = f32[8,2048,64]{1,0,2:T(8,128)} concatenate(f32[1,2048,64]{1,0,2:T(1,128)S(1)} %stack.132, f32[1,2048,64]{1,0,2:T(1,128)S(1)} %stack.133, f32[1,2048,64]{1,0,2:T(1,128)S(1)} %stack.134, f32[1,2048,64]{1,0,2:T(1,128)S(1)} %stack.135, f32[1,2048,64]{1,0,2:T(1,128)} %stack.136, f32[1,2048,64]{1,0,2:T(1,128)} %stack.137, f32[1,2048,64]{1,0,2:T(1,128)} %stack.138, ...), dimensions={0} | concatenate | bytes 8388608 | tf_op jit(solution)/shard_map/while/body/eval_jaxpr/stack | solution.py:103
  163.6 11.8 %convolution_bitcast_fusion.4 = f32[1,8,8,64]{2,1,3,0:T(8,128)S(1)} fusion(f32[8,2048,64]{1,0,2:T(8,128)} %stack.140, f32[2048,8,64]{0,1,2:T(8,128)} %get-tuple-element.463), kind=kOutput, calls=%fused_computation.1.clone.1 | convolution fusion | flops 100663296 | bytes 8404992 | tf_op jit(solution)/shard_map/while/body/eval_jaxpr/jnr,npr->jpr/dot_general | solution.py:109
  184.2 11.5 %stack.140 = f32[8,2048,64]{1,0,2:T(8,128)} concatenate(f32[1,2048,64]{1,0,2:T(1,128)S(1)} %stack.132, f32[1,2048,64]{1,0,2:T(1,128)S(1)} %stack.133, f32[1,2048,64]{1,0,2:T(1,128)S(1)} %stack.134, f32[1,2048,64]{1,0,2:T(1,128)S(1)} %stack.135, f32[1,2048,64]{1,0,2:T(1,128)} %stack.136, f32[1,2048,64]{1,0,2:T(1,128)} %stack.137, f32[1,2048,64]{1,0,2:T(1,128)} %stack.138, ...), dimensions={0} | concatenate | bytes 8388608 | tf_op jit(solution)/shard_map/while/body/eval_jaxpr/stack | solution.py:103
  195.6 11.8 %convolution_bitcast_fusion.4 = f32[1,8,8,64]{2,1,3,0:T(8,128)S(1)} fusion(f32[8,2048,64]{1,0,2:T(8,128)} %stack.140, f32[2048,8,64]{0,1,2:T(8,128)} %get-tuple-element.463), kind=kOutput, calls=%fused_computation.1.clone.1 | convolution fusion | flops 100663296 | bytes 8404992 | tf_op jit(solution)/shard_map/while/body/eval_jaxpr/jnr,npr->jpr/dot_general | solution.py:109
  216.2 11.5 %stack.140 = f32[8,2048,64]{1,0,2:T(8,128)} concatenate(f32[1,2048,64]{1,0,2:T(1,128)S(1)} %stack.132, f32[1,2048,64]{1,0,2:T(1,128)S(1)} %stack.133, f32[1,2048,64]{1,0,2:T(1,128)S(1)} %stack.134, f32[1,2048,64]{1,0,2:T(1,128)S(1)} %stack.135, f32[1,2048,64]{1,0,2:T(1,128)} %stack.136, f32[1,2048,64]{1,0,2:T(1,128)} %stack.137, f32[1,2048,64]{1,0,2:T(1,128)} %stack.138, ...), dimensions={0} | concatenate | bytes 8388608 | tf_op jit(solution)/shard_map/while/body/eval_jaxpr/stack | solution.py:103
  227.6 11.8 %convolution_bitcast_fusion.4 = f32[1,8,8,64]{2,1,3,0:T(8,128)S(1)} fusion(f32[8,2048,64]{1,0,2:T(8,128)} %stack.140, f32[2048,8,64]{0,1,2:T(8,128)} %get-tuple-element.463), kind=kOutput, calls=%fused_computation.1.clone.1 | convolution fusion | flops 100663296 | bytes 8404992 | tf_op jit(solution)/shard_map/while/body/eval_jaxpr/jnr,npr->jpr/dot_general | solution.py:109
  248.2 11.5 %stack.140 = f32[8,2048,64]{1,0,2:T(8,128)} concatenate(f32[1,2048,64]{1,0,2:T(1,128)S(1)} %stack.132, f32[1,2048,64]{1,0,2:T(1,128)S(1)} %stack.133, f32[1,2048,64]{1,0,2:T(1,128)S(1)} %stack.134, f32[1,2048,64]{1,0,2:T(1,128)S(1)} %stack.135, f32[1,2048,64]{1,0,2:T(1,128)} %stack.136, f32[1,2048,64]{1,0,2:T(1,128)} %stack.137, f32[1,2048,64]{1,0,2:T(1,128)} %stack.138, ...), dimensions={0} | concatenate | bytes 8388608 | tf_op jit(solution)/shard_map/while/body/eval_jaxpr/stack | solution.py:103
  259.7 11.8 %convolution_bitcast_fusion.4 = f32[1,8,8,64]{2,1,3,0:T(8,128)S(1)} fusion(f32[8,2048,64]{1,0,2:T(8,128)} %stack.140, f32[2048,8,64]{0,1,2:T(8,128)} %get-tuple-element.463), kind=kOutput, calls=%fused_computation.1.clone.1 | convolution fusion | flops 100663296 | bytes 8404992 | tf_op jit(solution)/shard_map/while/body/eval_jaxpr/jnr,npr->jpr/dot_general | solution.py:109
  (175 shorter events, 79.6 us)
Async XLA Ops:
  6.5 129.3 %all-gather.2.cloned.1.call-start = ((), (), s32[]{:S(2)}) async-start(), calls=%async_computation.2 | async-start | bytes 8519680 | tf_op jit(solution)/shard_map/all_gather | solution.py:160
  8.5 6.0 %collective-permute-start = (f32[2,32,1,512]{3,2,1,0:T(1,128)S(1)}, f32[2,32,1,512]{3,2,1,0:T(1,128)S(1)}, u32[]{:S(2)}, u32[]{:S(2)}) collective-permute-start(f32[2,32,1,512]{3,2,1,0:T(1,128)S(1)} %get-tuple-element.288), channel_id=1, source_target_pairs={{0,64},{64,128},{128,192},{192,0},{1,65},{65,129},{129,193},{193,1... | collective-permute-start | bytes 393224 | tf_op jit(solution)/shard_map/ppermute | solution.py:22
  10.7 3.8 %collective-permute-start.1 = (f32[2,32,1,512]{3,2,1,0:T(1,128)S(1)}, f32[2,32,1,512]{3,2,1,0:T(1,128)S(1)}, u32[]{:S(2)}, u32[]{:S(2)}) collective-permute-start(f32[2,32,1,512]{3,2,1,0:T(1,128)S(1)} %get-tuple-element.269), channel_id=1, source_target_pairs={{64,0},{128,64},{192,128},{0,192},{65,1},{129,65},{193,129},{1,193... | collective-permute-start | bytes 393224 | tf_op jit(solution)/shard_map/ppermute | solution.py:24
  16.8 1.0 copy-start
  17.8 4.7 %collective-permute-start.2 = (f32[2,1,8,512]{3,2,1,0:T(8,128)S(1)}, f32[2,1,8,512]{3,2,1,0:T(8,128)S(1)}, u32[]{:S(2)}, u32[]{:S(2)}) collective-permute-start(f32[2,1,8,512]{3,2,1,0:T(8,128)S(1)} %get-tuple-element.287), channel_id=1, source_target_pairs={{0,1},{1,2},{2,3},{3,4},{4,5},{5,6},{6,7},{7,8},{8,9},{9,10},{10,1... | collective-permute-start | bytes 98312 | tf_op jit(solution)/shard_map/ppermute | solution.py:22
  21.5 3.3 %collective-permute-start.3 = (f32[2,1,8,512]{3,2,1,0:T(8,128)S(1)}, f32[2,1,8,512]{3,2,1,0:T(8,128)S(1)}, u32[]{:S(2)}, u32[]{:S(2)}) collective-permute-start(f32[2,1,8,512]{3,2,1,0:T(8,128)S(1)} %get-tuple-element.267), channel_id=1, source_target_pairs={{1,0},{2,1},{3,2},{4,3},{5,4},{6,5},{7,6},{8,7},{9,8},{10,9},{11,1... | collective-permute-start | bytes 98312 | tf_op jit(solution)/shard_map/ppermute | solution.py:24
  25.0 1.0 copy-start.2
  26.5 4.3 %collective-permute-start.4 = (f32[2,1,8,512]{3,2,1,0:T(8,128)S(1)}, f32[2,1,8,512]{3,2,1,0:T(8,128)S(1)}, u32[]{:S(2)}, u32[]{:S(2)}) collective-permute-start(f32[2,1,8,512]{3,2,1,0:T(8,128)S(1)} %get-tuple-element.285), channel_id=1, source_target_pairs={{0,1},{1,2},{2,3},{3,4},{4,5},{5,6},{6,7},{7,8},{8,9},{9,10},{10,1... | collective-permute-start | bytes 98312 | tf_op jit(solution)/shard_map/ppermute | solution.py:22
  26.7 4.3 %collective-permute-start.5 = (f32[2,1,8,512]{3,2,1,0:T(8,128)S(1)}, f32[2,1,8,512]{3,2,1,0:T(8,128)S(1)}, u32[]{:S(2)}, u32[]{:S(2)}) collective-permute-start(f32[2,1,8,512]{3,2,1,0:T(8,128)S(1)} %get-tuple-element.286), channel_id=1, source_target_pairs={{1,0},{2,1},{3,2},{4,3},{5,4},{6,5},{7,6},{8,7},{9,8},{10,9},{11,1... | collective-permute-start | bytes 98312 | tf_op jit(solution)/shard_map/ppermute | solution.py:24
  30.9 1.0 copy-start.1
  32.1 5.2 %collective-permute-start.6 = (f32[2,32,1,512]{3,2,1,0:T(1,128)S(1)}, f32[2,32,1,512]{3,2,1,0:T(1,128)S(1)}, u32[]{:S(2)}, u32[]{:S(2)}) collective-permute-start(f32[2,32,1,512]{3,2,1,0:T(1,128)S(1)} %get-tuple-element.283), channel_id=1, source_target_pairs={{0,64},{64,128},{128,192},{192,0},{1,65},{65,129},{129,193},{193,1... | collective-permute-start | bytes 393224 | tf_op jit(solution)/shard_map/ppermute | solution.py:22
  33.2 4.1 %collective-permute-start.7 = (f32[2,32,1,512]{3,2,1,0:T(1,128)S(1)}, f32[2,32,1,512]{3,2,1,0:T(1,128)S(1)}, u32[]{:S(2)}, u32[]{:S(2)}) collective-permute-start(f32[2,32,1,512]{3,2,1,0:T(1,128)S(1)} %get-tuple-element.284), channel_id=1, source_target_pairs={{64,0},{128,64},{192,128},{0,192},{65,1},{129,65},{193,129},{1,193... | collective-permute-start | bytes 393224 | tf_op jit(solution)/shard_map/ppermute | solution.py:24
  38.3 1.0 copy-start.5
  38.4 1.1 copy-start.6
  38.4 15.5 %copy-start.3 = (f32[32,128]{1,0:T(8,128)S(1)}, f32[32,128]{1,0:T(8,128)}, u32[]{:S(2)}) copy-start(f32[32,128]{1,0:T(8,128)} %param.17) | copy-start | bytes 49156
  38.4 15.5 %copy-start.4 = (s32[32,128]{1,0:T(8,128)S(1)}, s32[32,128]{1,0:T(8,128)}, u32[]{:S(2)}) copy-start(s32[32,128]{1,0:T(8,128)} %param.16) | copy-start | bytes 49156
  40.7 72.5 %all-to-all-start = ((s32[64,1,8]{2,1,0:T(1,128)}), s32[64,1,8]{2,1,0:T(1,128)S(1)}, u32[]{:S(2)}, u32[]{:S(2)}) async-start(s32[64,1,8]{2,1,0:T(1,128)} %bitcast.17), calls=%async_computation | async-start | bytes 65536 | tf_op jit(solution)/shard_map/all_to_all | solution.py:191
  113.3 19.6 %all-to-all-start.1 = ((f32[64,1,128]{2,1,0:T(1,128)}), f32[64,1,128]{2,1,0:T(1,128)S(1)}, u32[]{:S(2)}, u32[]{:S(2)}) async-start(f32[64,1,128]{2,1,0:T(1,128)} %reshape.174), calls=%async_computation.1 | async-start | bytes 65536 | tf_op jit(solution)/shard_map/all_to_all | solution.py:184
Sparse Core Ops, SparseCore 0:
  39.4 87.0 all-gather.1
where the time goes:
time: 286 us; the launch traced here: 281 us
  local copies, waits for them, and re-layouts  106 us (37%)
  matrix products  88.7 us (31%)
  starting transfers between devices  37.4 us (13%)
  waiting for transfers between devices  16.3 us (6%)
  between operations  13.8 us (5%)
  other arithmetic  10.7 us (4%)
  loops' own time  7.76 us (3%)
    another operation x36, local copies, waits for them, and re-layouts, column_block(): jnp.stack([lax.dynamic_slice_in_dim(doubled, column_count - first - offse...  70.2 us
    dot_general x4, matrix products, column_block(): jnp.einsum('jnr,npr->jpr', picked, gathered_cycles, precision=highest, pr...  47.2 us
    dot_general x8, matrix products, table_block(): jnp.dot(cos_table, scale, precision=highest, preferred_element_type=jnp.f...  40.6 us
    all_to_all x1, starting transfers between devices, local(): lax.all_to_all(send_target.reshape(devices, capacity), 'az', split_axis=0...  13.1 us
    all_to_all x1, starting transfers between devices, local(): lax.all_to_all(send_volume.reshape(devices, capacity, -1), 'az', split_ax...  10.3 us
    all_to_all x1, waiting for transfers between devices, local(): lax.all_to_all(send_volume.reshape(devices, capacity, -1), 'az', split_ax...  7.78 us
    while x1, local copies, waits for them, and re-layouts, circulant_columns(): lax.map(column_block, lax.iota(jnp.int32, column_share // block_cols))  7.72 us
    dynamic_update_slice x16, local copies, waits for them, and re-layouts, circulant_columns(): lax.map(table_block, lax.iota(jnp.int32, 8))  7.63 us
  transfers between devices with their start and end apart: 11, of which 7 were waited for; matrix products, arithmetic and copies ran while one was open for 22% of the time, Pallas kernels for 0%

commit v1 on v0

v1 whole, which is shorter than its diff:
```python
import functools
import math

import jax
import jax.numpy as jnp
import ml_dtypes
import numpy as np
from jax import lax
from jax.experimental import pallas as pl
from jax.experimental.pallas import tpu as pltpu
from jax.sharding import PartitionSpec as P

R_AX = 64
XR = 16
COLS = 32
PLANES = 8
ROWS = COLS * PLANES
NR = 512
SLOTS = 8
KD = 40

F32 = jnp.float32
BF16 = jnp.bfloat16

BELOW = ((0, -2), (0, -1), (1, -2), (1, -1), (2, -1), (3, -1))
ABOVE = ((0, 8), (0, 9), (1, 8), (2, 8), (3, 8))
LEFT = ((0, -2), (0, -1), (1, -2), (1, -1), (2, -2), (2, -1), (3, -1))
RIGHT = ((0, 32), (0, 33), (1, 32), (1, 33), (2, 32), (3, 32))
HALO_PLANES = ((-2, -1, 8, 9), (-2, -1, 8), (-1, 8), (-1, 8))


def corner_list(columns):
    return [(f, c, p) for f, c in columns for p in HALO_PLANES[f]]


LEFT_ROWS = 80
RIGHT_ROWS = 72


def plane_slot(plane):
    return plane % 16 - 8


def pack_planes(f, ca, ct, cr, up, down):
    fields = (f, ca, ct, cr)
    for k, (field, plane) in enumerate(BELOW):
        up[k * COLS : (k + 1) * COLS, :] = fields[field][pl.ds(plane + PLANES, COLS, stride=PLANES), :]
    for k, (field, plane) in enumerate(ABOVE):
        down[k * COLS : (k + 1) * COLS, :] = fields[field][pl.ds(plane - PLANES, COLS, stride=PLANES), :]


def pack_columns(f0, c0, t0, r0, f1, c1, t1, r1, below, above, right, left):
    low = (f0, c0, t0, r0)
    high = (f1, c1, t1, r1)

    def corner(field, column, plane):
        if plane < 0:
            return below, BELOW.index((field, plane)) * COLS + column
        return above, ABOVE.index((field, plane)) * COLS + column

    for k, (field, column) in enumerate(LEFT):
        right[k * 8 : k * 8 + 8, :] = high[field][(column + 2) * 8 : (column + 2) * 8 + 8, :]
    for k, (field, column, plane) in enumerate(corner_list(LEFT)):
        source, row = corner(field, column + COLS, plane)
        at = len(LEFT) * 8 + k
        right[at : at + 1, :] = source[row : row + 1, :]
    for k, (field, column) in enumerate(RIGHT):
        left[k * 8 : k * 8 + 8, :] = low[field][(column - 32) * 8 : (column - 32) * 8 + 8, :]
    for k, (field, column, plane) in enumerate(corner_list(RIGHT)):
        source, row = corner(field, column - COLS, plane)
        at = len(RIGHT) * 8 + k
        left[at : at + 1, :] = source[row : row + 1, :]


def upwind(courant, below_cell, above_cell):
    return courant * jnp.where(courant > 0.0, below_cell, above_cell)


def sweep(fields, below, above, left, right, halos, store, lanes, unrolled):
    for tile in range(lanes // 128):
        at_lanes = pl.ds(tile * 128, 128)
        for planes, source in ((BELOW, below), (ABOVE, above)):
            for k, (field, plane) in enumerate(planes):
                at_rows = pl.ds(16 + plane_slot(plane), COLS, stride=8)
                halos[field].at[tile][at_rows, :] = source[k * COLS : (k + 1) * COLS, at_lanes]
        for columns, source in ((LEFT, left), (RIGHT, right)):
            for k, (field, column, plane) in enumerate(corner_list(columns)):
                at = (column + 2) * 8 + plane_slot(plane)
                row = len(columns) * 8 + k
                halos[field].at[tile][at : at + 1, :] = source[row : row + 1, at_lanes]

    plane = lax.broadcasted_iota(jnp.int32, (8, lanes), 0)
    cycle = lax.broadcasted_iota(jnp.int32, (8, lanes), 1)
    first, last = plane == 0, plane == 7
    radius = cycle.astype(F32)
    outer_radius = radius + 1.0
    inverse = 1.0 / (radius + 0.5)
    axis_cell, rim_cell = cycle == 0, cycle == NR - 1

    def load(field, column):
        if isinstance(column, int) and (column, field) in [(c, f) for f, c in LEFT]:
            at = LEFT.index((field, column)) * 8
            own = left[at : at + 8, :]
        elif isinstance(column, int) and (column, field) in [(c, f) for f, c in RIGHT]:
            at = RIGHT.index((field, column)) * 8
            own = right[at : at + 8, :]
        elif isinstance(column, int):
            own = fields[field][column * 8 : column * 8 + 8, :]
        else:
            own = fields[field][pl.ds(pl.multiple_of(column * 8, 8), 8), :]
        if isinstance(column, int):
            at_rows = pl.ds((column + 2) * 8, 8)
        else:
            at_rows = pl.ds(pl.multiple_of(column * 8 + 16, 8), 8)
        tiles = [halos[field].at[tile][at_rows, :] for tile in range(lanes // 128)]
        return own, jnp.concatenate(tiles, axis=1) if len(tiles) > 1 else tiles[0]

    def next_plane(pair):
        own, halo = (pltpu.roll(a, 7, 0) for a in pair)
        return jnp.where(last, halo, own), jnp.where(last, own, halo)

    def previous_plane(pair):
        own, halo = (pltpu.roll(a, 1, 0) for a in pair)
        return jnp.where(first, halo, own), jnp.where(first, own, halo)

    def flux(courant, low, high):
        return tuple(upwind(c, a, b) for c, a, b in zip(courant, low, high))

    def update(values, upper, lower):
        return tuple(v - (a - b) for v, a, b in zip(values, upper, lower))

    def axial(values, courant):
        face = flux(courant, values, next_plane(values))
        return update(values, face, previous_plane(face))

    def axial_own(values, courant):
        own, halo = flux(courant, values, next_plane(values))
        lower = jnp.where(first, pltpu.roll(halo, 1, 0), pltpu.roll(own, 1, 0))
        return values[0] - (own - lower)

    def radial_one(values, courant):
        above_cell = jnp.where(rim_cell, 0.0, pltpu.roll(values, lanes - 1, 1))
        outer = outer_radius * upwind(courant, values, above_cell)
        inner = jnp.where(axis_cell, 0.0, pltpu.roll(outer, 1, 1))
        return values - (outer - inner) * inverse

    def radial(values, courant):
        return tuple(radial_one(v, c) for v, c in zip(values, courant))

    def step(column, state, stage):
        v1_old, face_a_old, v3_old, face_b_old = state
        v1 = axial(load(0, column), load(1, column)) if stage < 6 else None
        face_a = v3 = face_b = None
        if stage >= 1:
            face_a = flux(load(2, column - 1), v1_old, v1)
        if stage >= 2:
            v2 = update(v1_old, face_a, face_a_old)
            v3 = radial(v2, load(3, column - 1))
        if stage >= 3:
            face_b = flux(load(2, column - 2), v3_old, v3)
        if stage >= 4:
            v4 = update(v3_old, face_b, face_b_old)
            store(column - 2, axial_own(v4, load(1, column - 2)))
        return v1, face_a, v3, face_b

    state = (None, None, None, None)
    for stage, column in enumerate(range(-2, 4)):
        state = step(column, state, stage if stage < 4 else 4)
    if unrolled:
        for column in range(4, 32):
            state = step(column, state, 4)
    else:
        state = lax.fori_loop(4, 32, lambda column, s: step(column, s, 4), state)
    for column in (32, 33):
        state = step(column, state, 4)


def near_kernel(f, ca, ct, cr, below, above, left, right, crossing, out, h0, h1, h2, h3, swept):
    def store(column, values):
        swept[column * 8 : column * 8 + 8, :] = values

    sweep((f, ca, ct, cr), below, above, left, right, (h0, h1, h2, h3), store, 128, True)
    turned = swept[...].T
    out[pl.ds(0, R_AX, stride=4), :] = turned[:R_AX, :128]
    out[pl.ds(1, R_AX, stride=4), :] = turned[:R_AX, 128:]
    out[pl.ds(2, R_AX, stride=4), :] = crossing[:R_AX, :]
    out[pl.ds(3, R_AX, stride=4), :] = crossing[R_AX:, :]


def far_kernel(f, ca, ct, cr, below, above, left, right, out, h0, h1, h2, h3):
    def store(column, values):
        if isinstance(column, int):
            out[column * 8 : column * 8 + 8, :] = values
        else:
            out[pl.ds(pl.multiple_of(column * 8, 8), 8), :] = values

    sweep((f, ca, ct, cr), below, above, left, right, (h0, h1, h2, h3), store, NR, False)


def pieces(values, count):
    out = []
    for _ in range(count):
        piece = values.astype(BF16)
        out.append(piece)
        values = values - piece.astype(F32)
    return out


def mm(a, b, dims=((1,), (0,))):
    return lax.dot_general(a, b, (dims, ((), ())), preferred_element_type=F32)


def plic_volume(plane_code, strip_width):
    normal = lax.shift_right_logical(plane_code, 6).astype(F32)
    offset = lax.bitwise_and(plane_code, 63).astype(F32)
    plane_angle = math.pi / 16 + (normal + 0.5) * (3 * math.pi / 512)
    normal_along = jnp.cos(plane_angle)
    across = jnp.sin(plane_angle)
    plane_level = (offset + 0.5) * (normal_along + across) / 64.0
    strip_span = strip_width * normal_along

    def square(shift_value):
        positive = jnp.maximum(shift_value, 0.0)
        return positive * positive

    strip_area = (
        square(plane_level)
        - square(plane_level - strip_span)
        - square(plane_level - across)
        + square(plane_level - strip_span - across)
    ) / (2.0 * strip_span * across)
    return strip_width * strip_area


def crossing_kernel(code, width, reader, landing, out, volume_out):
    iota = functools.partial(lax.broadcasted_iota, jnp.int32)
    volume = plic_volume(code[...], width[...])
    both = jnp.concatenate([reader[...].astype(F32), landing[...].astype(F32)], axis=0).astype(BF16)
    column_of_row = (iota((ROWS, COLS), 0) // 8 == iota((ROWS, COLS), 1)).astype(F32).astype(BF16)
    spread = mm(column_of_row, both, ((1,), (1,)))
    row16, lane16 = iota((ROWS, 16), 0), iota((ROWS, 16), 1)
    reader_rows = jnp.sum(jnp.where(lane16 == row16 % 8, spread, 0.0), axis=1, keepdims=True)
    landing_rows = jnp.sum(jnp.where(lane16 == row16 % 8 + 8, spread, 0.0), axis=1, keepdims=True)
    across = mm(both, column_of_row, ((1,), (1,)))
    reader_lanes = jnp.sum(
        jnp.where(iota((16, ROWS), 0) == iota((16, ROWS), 1) % 8, across, 0.0), axis=0, keepdims=True
    )
    same = (reader_rows == reader_lanes) & (iota((ROWS, ROWS), 1) < iota((ROWS, ROWS), 0))
    rank = jnp.sum(jnp.where(same, 1.0, 0.0), axis=1, keepdims=True)

    row, lane = iota((ROWS, 128), 0), iota((ROWS, 128), 1)
    wide = jnp.broadcast_to(volume[:, None, :], (COLS, PLANES, 128)).reshape(ROWS, 128)
    own = jnp.where(lane // 16 == row % 8, wide, 0.0)
    repeat = (iota((128, 128), 0) % 16 == iota((128, 128), 1) % 16).astype(F32).astype(BF16)
    rows_of_volume = sum(mm(piece, repeat) for piece in pieces(own, 3))
    volume_out[...] = rows_of_volume.T[:XR, :]
    chosen = (reader_lanes == iota((R_AX, ROWS), 0).astype(F32)).astype(F32).astype(BF16)
    slotted = jnp.where((lane // 16).astype(F32) == rank, rows_of_volume, 0.0)
    out[:R_AX, :] = sum(mm(chosen, piece) for piece in pieces(slotted, 3))
    target = landing_rows * 8.0 + (row % 8).astype(F32) + 1.0
    marked = jnp.where(lane.astype(F32) == rank, target, 0.0)
    out[R_AX:, :] = mm(chosen, marked.astype(BF16))


def arrival_kernel(received, volume, out):
    values = received[pl.ds(2, R_AX, stride=4), :]
    targets = received[pl.ds(3, R_AX, stride=4), :]
    turned = values.T
    row = lax.broadcasted_iota(jnp.int32, (R_AX, ROWS), 1).astype(F32) + 1.0
    total = -volume[...]
    for slot in range(SLOTS):
        chosen = (targets[:, slot : slot + 1] == row).astype(F32).astype(BF16)
        for piece in pieces(turned[slot * XR : (slot + 1) * XR, :], 3):
            total += mm(piece, chosen)
    out[...] = total


def halves(table):
    high = table.astype(ml_dtypes.bfloat16)
    low = (table - high.astype(np.float64)).astype(ml_dtypes.bfloat16)
    return high, low


def filter_tables():
    outer, sector = np.arange(33)[:, None], np.arange(64)[None, :]
    phase = 2 * np.pi * (outer * sector % 64) / 64
    first = np.zeros((2 * KD, 64))
    first[:33], first[KD : KD + 33] = np.cos(phase), -np.sin(phase)
    weight = np.where((outer == 0) | (outer == 32), 1.0, 2.0) / 2048
    last = np.zeros((64, 2 * KD))
    last[:, :33], last[:, KD : KD + 33] = (weight * np.cos(phase)).T, (-weight * np.sin(phase)).T
    column, plane = np.arange(ROWS) // PLANES, np.arange(ROWS) % PLANES
    inner = 2 * np.pi * (column[:, None] * column[None, :] % 32) / 32
    same = plane[:, None] == plane[None, :]
    block = np.concatenate([np.where(same, np.cos(inner), 0.0), np.where(same, -np.sin(inner), 0.0)], axis=1)
    turn = 2 * np.pi * np.arange(KD)[:, None] * column[None, :] / 2048
    twiddle = np.concatenate([np.cos(turn), -np.sin(turn)], axis=0).astype(np.float32)
    return (*halves(first), *halves(block), twiddle, *halves(last))


def dot3(a, b):
    (ah, al), (bh, bl) = a, b
    return mm(ah, bh) + (mm(al, bh) + mm(ah, bl))


def filter_kernel(received, first_h, first_l, block_h, block_l, twiddle, last_h, last_l, out):
    sectors = jnp.concatenate(
        [received[pl.ds(0, R_AX, stride=4), :], received[pl.ds(1, R_AX, stride=4), :]], axis=1
    )
    outer = dot3((first_h[...], first_l[...]), pieces(sectors, 2))
    re, im = outer[:KD], outer[KD:]
    t_re, t_im = twiddle[:KD, :], twiddle[KD:, :]
    turned = jnp.concatenate([re * t_re - im * t_im, re * t_im + im * t_re], axis=0)
    block = (block_h[...], block_l[...])
    inner = dot3(pieces(turned, 2), block)
    re = inner[:KD, :ROWS] - inner[KD:, ROWS:]
    im = inner[:KD, ROWS:] + inner[KD:, :ROWS]
    mode = lax.broadcasted_iota(jnp.int32, (KD, ROWS), 0) + 64 * (
        lax.broadcasted_iota(jnp.int32, (KD, ROWS), 1) // PLANES
    )
    folded = jnp.minimum(mode, 2048 - mode).astype(F32)
    cutoff = (lax.axis_index("az") + 1).astype(F32) * 2.0
    scaled = folded / cutoff
    damped = jnp.exp(-(scaled * scaled))
    back = dot3(pieces(jnp.concatenate([re * damped, im * damped], axis=0), 2), block)
    re = back[:KD, :ROWS] + back[KD:, ROWS:]
    im = back[KD:, :ROWS] - back[:KD, ROWS:]
    turned = jnp.concatenate([re * t_re + im * t_im, im * t_re - re * t_im], axis=0)
    result = dot3((last_h[...], last_l[...]), pieces(turned, 2))
    out[pl.ds(0, R_AX, stride=2), :] = result[:, :128]
    out[pl.ds(1, R_AX, stride=2), :] = result[:, 128:]


def final_kernel(received, delta, swept, out):
    near = jnp.concatenate(
        [received[pl.ds(0, R_AX, stride=2), :], received[pl.ds(1, R_AX, stride=2), :]], axis=1
    )
    near = jnp.concatenate([near[:XR] + delta[...], near[XR:], jnp.zeros((R_AX, ROWS), F32)], axis=0)
    cycle = lax.broadcasted_iota(jnp.int32, (ROWS, 128), 1)
    out[...] = jnp.where(cycle < R_AX, near.T, swept[...])


def block(rows, lanes, row=0):
    return pl.BlockSpec((rows, lanes), lambda i: (row, 0))


def lane_tile(rows):
    return pl.BlockSpec((rows, 128), lambda i: (0, i))


def call(kernel, inputs, specs, out_shapes, out_specs, scratch=(), cost=1.0, steps=1, **options):
    return pl.pallas_call(
        kernel,
        grid=(steps,),
        in_specs=list(specs),
        out_specs=out_specs,
        out_shape=out_shapes,
        scratch_shapes=list(scratch),
        cost_estimate=pl.CostEstimate(flops=int(cost * 1e6), bytes_accessed=int(cost * 3e6), transcendentals=0),
        compiler_params=pltpu.CompilerParams(vmem_limit_bytes=32 * 1024 * 1024),
        **options,
    )(*inputs)


def shape(*dims):
    return jax.ShapeDtypeStruct(dims, F32)


def local(
    fraction,
    courant_axial,
    courant_azimuth,
    courant_radial,
    plane_code,
    strip_width,
    tile_reader,
    landing_column,
):
    ax_count, az_count = lax.axis_size("ax"), lax.axis_size("az")
    fields = [a.reshape(ROWS, NR) for a in (fraction, courant_axial, courant_azimuth, courant_radial)]
    n_below, n_above = len(BELOW) * COLS, len(ABOVE) * COLS

    up, down = call(
        pack_planes,
        fields,
        [lane_tile(ROWS)] * 4,
        (shape(n_below, NR), shape(n_above, NR)),
        (lane_tile(n_below), lane_tile(n_above)),
        steps=NR // 128,
    )
    below = lax.ppermute(up, "ax", [(i, (i + 1) % ax_count) for i in range(ax_count)])
    above = lax.ppermute(down, "ax", [((i + 1) % ax_count, i) for i in range(ax_count)])

    crossing, volume = call(
        crossing_kernel,
        (plane_code, strip_width, tile_reader.T, landing_column.T),
        [block(COLS, 128), block(COLS, 128), block(PLANES, COLS), block(PLANES, COLS)],
        (shape(2 * R_AX, 128), shape(XR, ROWS)),
        (block(2 * R_AX, 128), block(XR, ROWS)),
    )

    to_right, to_left = call(
        pack_columns,
        (*fields, *fields, below, above),
        [block(16, NR)] * 4 + [block(16, NR, 15)] * 4 + [block(n_below, NR), block(n_above, NR)],
        (shape(LEFT_ROWS, NR), shape(RIGHT_ROWS, NR)),
        (block(LEFT_ROWS, NR), block(RIGHT_ROWS, NR)),
    )
    left = lax.ppermute(to_right, "az", [(i, (i + 1) % az_count) for i in range(az_count)])
    right = lax.ppermute(to_left, "az", [((i + 1) % az_count, i) for i in range(az_count)])

    parts = (*fields, below, above, left, right)

    def part_specs(lanes):
        return [block(ROWS, lanes)] * 4 + [block(a.shape[0], lanes) for a in (below, above, left, right)]

    def halo_scratch(lanes):
        return [pltpu.VMEM((lanes // 128, (COLS + 4) * 8, 128), F32)] * 4

    send = call(
        near_kernel,
        (*parts, crossing),
        part_specs(128) + [block(2 * R_AX, 128)],
        shape(4 * R_AX, 128),
        block(4 * R_AX, 128),
        halo_scratch(128) + [pltpu.VMEM((ROWS, 128), F32)],
    )
    got = lax.all_to_all(send.reshape(R_AX, 4, 128), "az", 0, 0, tiled=True).reshape(4 * R_AX, 128)
    swept = call(far_kernel, parts, part_specs(NR), shape(ROWS, NR), block(ROWS, NR), halo_scratch(NR), cost=4.0)

    tables = filter_tables()
    back = call(
        filter_kernel,
        (got, *tables),
        [block(4 * R_AX, 128)] + [block(*t.shape) for t in tables],
        shape(2 * R_AX, 128),
        block(2 * R_AX, 128),
    )
    returned = lax.all_to_all(back.reshape(R_AX, 2, 128), "az", 0, 0, tiled=True).reshape(2 * R_AX, 128)
    delta = call(
        arrival_kernel,
        (got, volume),
        [block(4 * R_AX, 128), block(XR, ROWS)],
        shape(XR, ROWS),
        block(XR, ROWS),
    )
    out = call(
        final_kernel,
        (returned, delta, swept),
        [block(2 * R_AX, 128), block(XR, ROWS), block(ROWS, 128)],
        shape(ROWS, NR),
        block(ROWS, 128),
        input_output_aliases={2: 0},
    )
    return out.reshape(COLS, PLANES, NR)


def solution(mesh):
    return jax.shard_map(
        local,
        mesh=mesh,
        in_specs=(
            P("az", "ax", None),
            P("az", "ax", None),
            P("az", "ax", None),
            P("az", "ax", None),
            P("az", "ax"),
            P("az", "ax"),
            P("az", "ax"),
            P("az", "ax"),
        ),
        out_specs=P("az", "ax", None),
        check_vma=False,
    )
```

time: 286 us -> 65.4 us (0.23); the launches traced: 281 us -> 65 us
  local copies, waits for them, and re-layouts: 106 us -> 4.25 us
  matrix products: 88.7 us -> 0 us
  starting transfers between devices: 37.4 us -> 13.5 us
  blocking collectives: 0 us -> 21.7 us
  between operations: 13.8 us -> 0.2 us
  Pallas kernels: 0 us -> 11.9 us
  other arithmetic: 10.7 us -> 0 us
  loops' own time: 7.76 us -> 0 us
  waiting for transfers between devices: 16.3 us -> 13.4 us
    dot_general x14 -> x0, matrix products: 88.7 us -> none  [the longest x4 47.2 us: column_block(): jnp.einsum('jnr,npr->jpr', picked, gathered_cycles, precision=highest, pr...]
    another operation x36 -> x0, local copies, waits for them, and re-layouts: 70.2 us -> none  [column_block(): jnp.stack([lax.dynamic_slice_in_dim(doubled, column_count - first - offse...]
    all_to_all x0 -> x1, blocking collectives: none -> 21.7 us  [local(): lax.all_to_all(send.reshape(R_AX, 4, 128), 'az', 0, 0, tiled=True)]
    all_to_all x2 -> x1, starting transfers between devices: 23.4 us -> 4.88 us  [local(): lax.all_to_all(back.reshape(R_AX, 2, 128), 'az', 0, 0, tiled=True)]
    pallas_call x0 -> x8, Pallas kernels: none -> 11.9 us  [call(): pl.pallas_call(kernel, grid=(steps,), in_specs=list(specs), out_specs=out...]
    dynamic_slice x16 -> x0, local copies, waits for them, and re-layouts: 11.8 us -> none  [the longest x4 4.73 us: column_block(): lax.dynamic_slice_in_dim(doubled, column_count - first - offset, column_c...]
    dynamic_update_slice x24 -> x0, local copies, waits for them, and re-layouts: 8.18 us -> none  [the longest x16 7.63 us: circulant_columns(): lax.map(table_block, lax.iota(jnp.int32, 8))]
    another operation x2 -> x0, loops' own time: 7.76 us -> none  [the longest x1 4.82 us: circulant_columns(): lax.map(table_block, lax.iota(jnp.int32, 8))]
  transfers between devices with their start and end apart: 11 -> 5, of which waited for: 7 -> 4; matrix products, arithmetic and copies ran while one was open for 22% -> 0% of each run, Pallas kernels for 0% -> 12%
where the time goes in v1:
time: 65.4 us; the launch traced here: 65 us
  blocking collectives  21.7 us (33%)
  starting transfers between devices  13.5 us (21%)
  waiting for transfers between devices  13.4 us (20%)
  Pallas kernels  11.9 us (18%)
  local copies, waits for them, and re-layouts  4.25 us (6%)
    all_to_all x1, blocking collectives, local(): lax.all_to_all(send.reshape(R_AX, 4, 128), 'az', 0, 0, tiled=True)  21.7 us
    pallas_call x8, Pallas kernels, call(): pl.pallas_call(kernel, grid=(steps,), in_specs=list(specs), out_specs=out...  11.9 us
    ppermute x1, waiting for transfers between devices, local(): lax.ppermute(down, 'ax', [((i + 1) % ax_count, i) for i in range(ax_count)])  6.45 us
    all_to_all x1, starting transfers between devices, local(): lax.all_to_all(back.reshape(R_AX, 2, 128), 'az', 0, 0, tiled=True)  4.88 us
    ppermute x1, starting transfers between devices, local(): lax.ppermute(to_right, 'az', [(i, (i + 1) % az_count) for i in range(az_c...  4.87 us
    unnamed x38, local copies, waits for them, and re-layouts  4.25 us
    ppermute x1, waiting for transfers between devices, local(): lax.ppermute(to_left, 'az', [((i + 1) % az_count, i) for i in range(az_co...  3.97 us
    all_to_all x1, waiting for transfers between devices, local(): lax.all_to_all(back.reshape(R_AX, 2, 128), 'az', 0, 0, tiled=True)  2.71 us
  transfers between devices with their start and end apart: 5, of which 4 were waited for; matrix products, arithmetic and copies ran while one was open for 0% of the time, Pallas kernels for 12%

profile of v1, /device:TPU:1, one launch (start us, length us, event | category | flops | bytes accessed | tf_op | source)
XLA Modules:
  0.0 65.0 jit_solution(10782651427729394280)
XLA Ops:
  0.0 1.0 %copy-done = f32[32,8,512]{2,1,0:T(8,128)S(1)} copy-done((f32[32,8,512]{2,1,0:T(8,128)S(1)}, f32[32,8,512]{2,1,0:T(8,128)}, u32[]{:S(2)}) %copy-start) | copy-done | bytes 524312
  1.0 1.0 %copy-done.2 = f32[32,8,512]{2,1,0:T(8,128)S(1)} copy-done((f32[32,8,512]{2,1,0:T(8,128)S(1)}, f32[32,8,512]{2,1,0:T(8,128)}, u32[]{:S(2)}) %copy-start.2) | copy-done | bytes 524312
  2.1 1.0 %copy-done.4 = f32[32,8,512]{2,1,0:T(8,128)S(1)} copy-done((f32[32,8,512]{2,1,0:T(8,128)S(1)}, f32[32,8,512]{2,1,0:T(8,128)}, u32[]{:S(2)}) %copy-start.4) | copy-done | bytes 524312
  3.1 1.0 %copy-done.6 = f32[32,8,512]{2,1,0:T(8,128)S(1)} copy-done((f32[32,8,512]{2,1,0:T(8,128)S(1)}, f32[32,8,512]{2,1,0:T(8,128)}, u32[]{:S(2)}) %copy-start.6) | copy-done | bytes 524312
  4.2 0.6 shard_map.145
  4.8 2.2 %collective-permute-start = (f32[192,512]{1,0:T(8,128)S(1)}, f32[192,512]{1,0:T(8,128)S(1)}, u32[]{:S(2)}, u32[]{:S(2)}) collective-permute-start(f32[192,512]{1,0:T(8,128)S(1)} %get-tuple-element.11), channel_id=1, source_target_pairs={{0,64},{64,128},{128,192},{192,0},{1,65},{65,129},{129,193},{193,1... | collective-permute-start | bytes 1179656 | tf_op jit(solution)/shard_map/ppermute | solution.py:391
  7.0 1.5 %collective-permute-start.1 = (f32[160,512]{1,0:T(8,128)S(1)}, f32[160,512]{1,0:T(8,128)S(1)}, u32[]{:S(2)}, u32[]{:S(2)}) collective-permute-start(f32[160,512]{1,0:T(8,128)S(1)} %get-tuple-element.12), channel_id=1, source_target_pairs={{64,0},{128,64},{192,128},{0,192},{65,1},{129,65},{193,129},{1,193... | collective-permute-start | bytes 983048 | tf_op jit(solution)/shard_map/ppermute | solution.py:392
  8.5 6.4 %collective-permute-done.1.above = f32[160,512]{1,0:T(8,128)S(1)} collective-permute-done((f32[160,512]{1,0:T(8,128)S(1)}, f32[160,512]{1,0:T(8,128)S(1)}, u32[]{:S(2)}, u32[]{:S(2)}) %collective-permute-start.1) | collective-permute-done | bytes 327712 | tf_op jit(solution)/shard_map/ppermute | solution.py:392
  14.9 0.2 collective-permute-done.below
  15.2 4.9 %collective-permute-start.2 = (f32[80,512]{1,0:T(8,128)S(1)}, f32[80,512]{1,0:T(8,128)S(1)}, u32[]{:S(2)}, u32[]{:S(2)}) collective-permute-start(f32[80,512]{1,0:T(8,128)S(1)} %get-tuple-element.13), channel_id=1, source_target_pairs={{0,1},{1,2},{2,3},{3,4},{4,5},{5,6},{6,7},{7,8},{8,9},{9,10},{10,1... | collective-permute-start | bytes 491528 | tf_op jit(solution)/shard_map/ppermute | solution.py:409
  20.1 0.6 shard_map.147
  20.7 4.0 %collective-permute-done.3.right = f32[72,512]{1,0:T(8,128)S(1)} collective-permute-done((f32[72,512]{1,0:T(8,128)S(1)}, f32[72,512]{1,0:T(8,128)S(1)}, u32[]{:S(2)}, u32[]{:S(2)}) %collective-permute-start.3) | collective-permute-done | bytes 147488 | tf_op jit(solution)/shard_map/ppermute | solution.py:410
  24.7 0.0 copy-start.9
  24.7 0.0 copy-start.11
  24.7 0.0 copy-start.12
  24.7 0.0 copy-start.13
  24.8 0.4 shard_map.148
  25.2 21.7 %all_to_all.10 = f32[64,4,128]{2,1,0:T(4,128)S(1)} all-to-all(f32[64,4,128]{2,1,0:T(4,128)S(1)} %bitcast.33), channel_id=1, replica_groups=mesh['ax'=4,'az'=64] {'az'}, dimensions={0} | all-to-all | bytes 262144 | tf_op jit(solution)/shard_map/all_to_all | solution.py:428
  47.0 1.6 %shard_map.149 = f32[128,128]{1,0:T(8,128)} custom-call(f32[256,128]{1,0:T(8,128)S(1)} %bitcast.31, bf16[80,64]{1,0:T(8,128)(2,1)S(1)} %copy-done.11, bf16[80,64]{1,0:T(8,128)(2,1)S(1)} %copy-done.12, bf16[256,512]{1,0:T(8,128)(2,1)S(1)} %copy-done.8, bf16[256,512]{1,0:T(8,128)(2,1)S(1)} %copy-done.9, f32[80,256]{1,0:T(8,128)S(1)} %copy-done.10, ...), custom_call_target="tpu_custom_call" | custom-call | flops 1000000 | bytes 3000000 | tf_op jit(solution)/shard_map/pallas_call | solution.py:352
  48.7 4.9 %all-to-all-start.1 = ((f32[64,2,128]{2,1,0:T(2,128)}), f32[64,2,128]{2,1,0:T(2,128)S(1)}, u32[]{:S(2)}, u32[]{:S(2)}) async-start(f32[64,2,128]{2,1,0:T(2,128)} %bitcast.8), calls=%async_computation.1 | async-start | bytes 131072 | tf_op jit(solution)/shard_map/all_to_all | solution.py:439
  53.6 6.7 %shard_map.151.swept = f32[256,512]{1,0:T(8,128)} custom-call(f32[256,512]{1,0:T(8,128)S(1)} %bitcast.15, f32[256,512]{1,0:T(8,128)S(1)} %bitcast.20, f32[256,512]{1,0:T(8,128)S(1)} %bitcast.25, f32[256,512]{1,0:T(8,128)S(1)} %bitcast.30, f32[192,512]{1,0:T(8,128)S(1)} %collective-permute-done.below, f32[160,512]{1,0:T(8,128)S(1)} %collective-permute-done.1.above, ...), custom_call_target="tpu_custom_call" | custom-call | flops 4000000 | bytes 12000000 | tf_op jit(solution)/shard_map/pallas_call | solution.py:352
  60.3 0.4 shard_map.150.delta
  60.6 2.7 %all-to-all-done.1 = f32[64,2,128]{2,1,0:T(2,128)S(1)} async-done(((f32[64,2,128]{2,1,0:T(2,128)}), f32[64,2,128]{2,1,0:T(2,128)S(1)}, u32[]{:S(2)}, u32[]{:S(2)}) %all-to-all-start.1) | async-done | bytes 65568 | tf_op jit(solution)/shard_map/all_to_all | solution.py:439
  63.3 1.7 %shard_map.152 = f32[256,512]{1,0:T(8,128)} custom-call(f32[128,128]{1,0:T(8,128)S(1)} %bitcast.34, f32[16,256]{1,0:T(8,128)S(1)} %shard_map.150.delta, f32[256,512]{1,0:T(8,128)} %shard_map.151.swept), custom_call_target="tpu_custom_call", output_to_operand_aliasing={{}: (2, {})} | custom-call | flops 1000000 | bytes 3000000 | tf_op jit(solution)/shard_map/pallas_call | solution.py:352
  (33 shorter events, 0.1 us)
Async XLA Ops:
  0.0 1.0 %copy-start = (f32[32,8,512]{2,1,0:T(8,128)S(1)}, f32[32,8,512]{2,1,0:T(8,128)}, u32[]{:S(2)}) copy-start(f32[32,8,512]{2,1,0:T(8,128)} %param.15) | copy-start | bytes 1572868
  1.0 1.0 %copy-start.2 = (f32[32,8,512]{2,1,0:T(8,128)S(1)}, f32[32,8,512]{2,1,0:T(8,128)}, u32[]{:S(2)}) copy-start(f32[32,8,512]{2,1,0:T(8,128)} %param.16) | copy-start | bytes 1572868
  2.1 1.0 %copy-start.4 = (f32[32,8,512]{2,1,0:T(8,128)S(1)}, f32[32,8,512]{2,1,0:T(8,128)}, u32[]{:S(2)}) copy-start(f32[32,8,512]{2,1,0:T(8,128)} %param.17) | copy-start | bytes 1572868
  3.1 1.0 %copy-start.6 = (f32[32,8,512]{2,1,0:T(8,128)S(1)}, f32[32,8,512]{2,1,0:T(8,128)}, u32[]{:S(2)}) copy-start(f32[32,8,512]{2,1,0:T(8,128)} %param.18) | copy-start | bytes 1572868
  4.8 10.4 %collective-permute-start = (f32[192,512]{1,0:T(8,128)S(1)}, f32[192,512]{1,0:T(8,128)S(1)}, u32[]{:S(2)}, u32[]{:S(2)}) collective-permute-start(f32[192,512]{1,0:T(8,128)S(1)} %get-tuple-element.11), channel_id=1, source_target_pairs={{0,64},{64,128},{128,192},{192,0},{1,65},{65,129},{129,193},{193,1... | collective-permute-start | bytes 1179656 | tf_op jit(solution)/shard_map/ppermute | solution.py:391
  7.0 17.7 %copy-start.1 = (f32[32,8,512]{2,1,0:T(8,128)S(1)}, f32[32,8,512]{2,1,0:T(8,128)}, u32[]{:S(2)}) copy-start(f32[32,8,512]{2,1,0:T(8,128)} %param.15) | copy-start | bytes 1572868
  7.0 8.0 %collective-permute-start.1 = (f32[160,512]{1,0:T(8,128)S(1)}, f32[160,512]{1,0:T(8,128)S(1)}, u32[]{:S(2)}, u32[]{:S(2)}) collective-permute-start(f32[160,512]{1,0:T(8,128)S(1)} %get-tuple-element.12), channel_id=1, source_target_pairs={{64,0},{128,64},{192,128},{0,192},{65,1},{129,65},{193,129},{1,193... | collective-permute-start | bytes 983048 | tf_op jit(solution)/shard_map/ppermute | solution.py:392
  15.2 4.9 %copy-start.15 = (s32[32,128]{1,0:T(8,128)S(1)}, s32[32,128]{1,0:T(8,128)}, u32[]{:S(2)}) copy-start(s32[32,128]{1,0:T(8,128)} %code.1) | copy-start | bytes 49156
  15.2 4.9 %copy-start.16 = (f32[32,128]{1,0:T(8,128)S(1)}, f32[32,128]{1,0:T(8,128)}, u32[]{:S(2)}) copy-start(f32[32,128]{1,0:T(8,128)} %width.1) | copy-start | bytes 49156
  15.2 4.9 %copy-start.18 = (s32[32,8]{0,1:T(8,128)S(1)}, s32[32,8]{0,1:T(8,128)}, u32[]{:S(2)}) copy-start(s32[32,8]{0,1:T(8,128)} %param.22) | copy-start | bytes 3076
  15.2 4.9 %copy-start.17 = (s32[32,8]{0,1:T(8,128)S(1)}, s32[32,8]{0,1:T(8,128)}, u32[]{:S(2)}) copy-start(s32[32,8]{0,1:T(8,128)} %param.21) | copy-start | bytes 3076
  15.2 9.4 %collective-permute-start.2 = (f32[80,512]{1,0:T(8,128)S(1)}, f32[80,512]{1,0:T(8,128)S(1)}, u32[]{:S(2)}, u32[]{:S(2)}) collective-permute-start(f32[80,512]{1,0:T(8,128)S(1)} %get-tuple-element.13), channel_id=1, source_target_pairs={{0,1},{1,2},{2,3},{3,4},{4,5},{5,6},{6,7},{7,8},{8,9},{9,10},{10,1... | collective-permute-start | bytes 491528 | tf_op jit(solution)/shard_map/ppermute | solution.py:409
  20.1 4.6 %collective-permute-start.3 = (f32[72,512]{1,0:T(8,128)S(1)}, f32[72,512]{1,0:T(8,128)S(1)}, u32[]{:S(2)}, u32[]{:S(2)}) collective-permute-start(f32[72,512]{1,0:T(8,128)S(1)} %get-tuple-element.14), channel_id=1, source_target_pairs={{1,0},{2,1},{3,2},{4,3},{5,4},{6,5},{7,6},{8,7},{9,8},{10,9},{11,1... | collective-permute-start | bytes 442376 | tf_op jit(solution)/shard_map/ppermute | solution.py:410
  24.7 22.3 %copy-start.8 = (bf16[256,512]{1,0:T(8,128)(2,1)S(1)}, bf16[256,512]{1,0:T(8,128)(2,1)}, u32[]{:S(2)}) copy-start(bf16[256,512]{1,0:T(8,128)(2,1)} %constant.16.clone.block_h) | copy-start | bytes 786436
  24.7 22.3 %copy-start.9 = (bf16[256,512]{1,0:T(8,128)(2,1)S(1)}, bf16[256,512]{1,0:T(8,128)(2,1)}, u32[]{:S(2)}) copy-start(bf16[256,512]{1,0:T(8,128)(2,1)} %constant.17.clone.block_l) | copy-start | bytes 786436
  24.7 22.3 %copy-start.10 = (f32[80,256]{1,0:T(8,128)S(1)}, f32[80,256]{1,0:T(8,128)}, u32[]{:S(2)}) copy-start(f32[80,256]{1,0:T(8,128)} %constant.18.clone.twiddle) | copy-start | bytes 245764
  24.7 22.3 %copy-start.11 = (bf16[80,64]{1,0:T(8,128)(2,1)S(1)}, bf16[80,64]{1,0:T(8,128)(2,1)}, u32[]{:S(2)}) copy-start(bf16[80,64]{1,0:T(8,128)(2,1)} %constant.14.clone.first_h) | copy-start | bytes 30724
  24.7 22.3 %copy-start.12 = (bf16[80,64]{1,0:T(8,128)(2,1)S(1)}, bf16[80,64]{1,0:T(8,128)(2,1)}, u32[]{:S(2)}) copy-start(bf16[80,64]{1,0:T(8,128)(2,1)} %constant.15.clone.first_l) | copy-start | bytes 30724
  24.7 22.3 %copy-start.13 = (bf16[64,80]{1,0:T(8,128)(2,1)S(1)}, bf16[64,80]{1,0:T(8,128)(2,1)}, u32[]{:S(2)}) copy-start(bf16[64,80]{1,0:T(8,128)(2,1)} %constant.19.clone.last_h) | copy-start | bytes 30724
  24.8 22.3 %copy-start.14 = (bf16[64,80]{1,0:T(8,128)(2,1)S(1)}, bf16[64,80]{1,0:T(8,128)(2,1)}, u32[]{:S(2)}) copy-start(bf16[64,80]{1,0:T(8,128)(2,1)} %constant.20.clone.last_l) | copy-start | bytes 30724
  24.8 28.8 %copy-start.7 = (f32[32,8,512]{2,1,0:T(8,128)S(1)}, f32[32,8,512]{2,1,0:T(8,128)}, u32[]{:S(2)}) copy-start(f32[32,8,512]{2,1,0:T(8,128)} %param.18) | copy-start | bytes 1572868
  25.2 28.3 %copy-start.5 = (f32[32,8,512]{2,1,0:T(8,128)S(1)}, f32[32,8,512]{2,1,0:T(8,128)}, u32[]{:S(2)}) copy-start(f32[32,8,512]{2,1,0:T(8,128)} %param.17) | copy-start | bytes 1572868
  47.0 6.6 %copy-start.3 = (f32[32,8,512]{2,1,0:T(8,128)S(1)}, f32[32,8,512]{2,1,0:T(8,128)}, u32[]{:S(2)}) copy-start(f32[32,8,512]{2,1,0:T(8,128)} %param.16) | copy-start | bytes 1572868
  48.7 14.7 %all-to-all-start.1 = ((f32[64,2,128]{2,1,0:T(2,128)}), f32[64,2,128]{2,1,0:T(2,128)S(1)}, u32[]{:S(2)}, u32[]{:S(2)}) async-start(f32[64,2,128]{2,1,0:T(2,128)} %bitcast.8), calls=%async_computation.1 | async-start | bytes 131072 | tf_op jit(solution)/shard_map/all_to_all | solution.py:439

commit v2 on v1

--- a/solution.py
+++ b/solution.py
@@ -24,71 +24,84 @@
 
 BELOW = ((0, -2), (0, -1), (1, -2), (1, -1), (2, -1), (3, -1))
 ABOVE = ((0, 8), (0, 9), (1, 8), (2, 8), (3, 8))
+HALO_PLANES = ((-2, -1, 8, 9), (-2, -1, 8), (-1, 8), (-1, 8))
+
+NEAR_LEFT = tuple((f, c) for f in range(3) for c in range(-4, 0)) + tuple((3, c) for c in range(-3, 0))
+NEAR_CORNERS = tuple((f, c, p) for f, c in NEAR_LEFT for p in HALO_PLANES[f])
+NEAR_ROWS = 8 * len(NEAR_LEFT) + 48
 LEFT = ((0, -2), (0, -1), (1, -2), (1, -1), (2, -2), (2, -1), (3, -1))
 RIGHT = ((0, 32), (0, 33), (1, 32), (1, 33), (2, 32), (3, 32))
-HALO_PLANES = ((-2, -1, 8, 9), (-2, -1, 8), (-1, 8), (-1, 8))
-
-
-def corner_list(columns):
-    return [(f, c, p) for f, c in columns for p in HALO_PLANES[f]]
-
-
-LEFT_ROWS = 80
-RIGHT_ROWS = 72
+TILES = NR // 128
+
+
+def far_layout(planes):
+    entries, row = [], 0
+    for tile in range(TILES):
+        for field, plane in planes:
+            left = sum(f == field for f, _ in LEFT)
+            right = sum(f == field for f, _ in RIGHT)
+            if tile:
+                runs = ((-left, left + COLS + right),)
+            else:
+                runs = ((-left, left), (COLS, right))
+            for column, count in runs:
+                entries.append((tile, field, plane, column, count, row))
+                row += count
+    return entries, -(-row // 8) * 8
+
+
+FAR_BELOW, FAR_BELOW_ROWS = far_layout(BELOW)
+FAR_ABOVE, FAR_ABOVE_ROWS = far_layout(ABOVE)
 
 
 def plane_slot(plane):
     return plane % 16 - 8
 
 
-def pack_planes(f, ca, ct, cr, up, down):
-    fields = (f, ca, ct, cr)
+def pack_first(*refs):
+    near, low, high, (up, down, right, left) = refs[:4], refs[4:8], refs[8:12], refs[12:]
     for k, (field, plane) in enumerate(BELOW):
-        up[k * COLS : (k + 1) * COLS, :] = fields[field][pl.ds(plane + PLANES, COLS, stride=PLANES), :]
+        up[k * COLS : (k + 1) * COLS, :] = near[field][pl.ds(plane + PLANES, COLS, stride=PLANES), :]
     for k, (field, plane) in enumerate(ABOVE):
-        down[k * COLS : (k + 1) * COLS, :] = fields[field][pl.ds(plane - PLANES, COLS, stride=PLANES), :]
-
-
-def pack_columns(f0, c0, t0, r0, f1, c1, t1, r1, below, above, right, left):
-    low = (f0, c0, t0, r0)
-    high = (f1, c1, t1, r1)
-
-    def corner(field, column, plane):
-        if plane < 0:
-            return below, BELOW.index((field, plane)) * COLS + column
-        return above, ABOVE.index((field, plane)) * COLS + column
-
+        down[k * COLS : (k + 1) * COLS, :] = near[field][pl.ds(plane - PLANES, COLS, stride=PLANES), :]
     for k, (field, column) in enumerate(LEFT):
-        right[k * 8 : k * 8 + 8, :] = high[field][(column + 2) * 8 : (column + 2) * 8 + 8, :]
-    for k, (field, column, plane) in enumerate(corner_list(LEFT)):
-        source, row = corner(field, column + COLS, plane)
-        at = len(LEFT) * 8 + k
+        right[k * 8 : k * 8 + 8, :] = high[field][(column + 2) * 8 : (column + 3) * 8, :]
+    for k, (field, column) in enumerate(RIGHT):
+        left[k * 8 : k * 8 + 8, :] = low[field][(column - COLS) * 8 : (column - COLS + 1) * 8, :]
+
+
+def pack_near_columns(*refs):
+    high, (below, above, right) = refs[:4], refs[4:]
+    for k, (field, column) in enumerate(NEAR_LEFT):
+        right[k * 8 : k * 8 + 8, :] = high[field][(column + 4) * 8 : (column + 5) * 8, :]
+    right[len(NEAR_LEFT) * 8 :, :] = jnp.zeros((48, 128), F32)
+    for k, (field, column, plane) in enumerate(NEAR_CORNERS):
+        planes, source = (BELOW, below) if plane < 0 else (ABOVE, above)
+        row = planes.index((field, plane)) * COLS + column + COLS
+        at = len(NEAR_LEFT) * 8 + k
         right[at : at + 1, :] = source[row : row + 1, :]
-    for k, (field, column) in enumerate(RIGHT):
-        left[k * 8 : k * 8 + 8, :] = low[field][(column - 32) * 8 : (column - 32) * 8 + 8, :]
-    for k, (field, column, plane) in enumerate(corner_list(RIGHT)):
-        source, row = corner(field, column - COLS, plane)
-        at = len(RIGHT) * 8 + k
-        left[at : at + 1, :] = source[row : row + 1, :]
+
+
+def pack_far_planes(*refs):
+    own, (left, right, up, down) = refs[: 4 * (TILES - 1)], refs[4 * (TILES - 1) :]
+    for entries, out, shift in ((FAR_BELOW, up, PLANES), (FAR_ABOVE, down, -PLANES)):
+        for tile, field, plane, column, count, row in entries:
+            lanes = pl.ds(tile * 128, 128)
+            for at in range(count):
+                for columns, source in ((LEFT, left), (RIGHT, right)):
+                    if (field, column + at) in columns:
+                        origin = columns.index((field, column + at)) * 8 + plane + shift
+                        out[row + at : row + at + 1, :] = source[origin : origin + 1, lanes]
+            if tile:
+                source = own[field * (TILES - 1) + tile - 1]
+                out[row - column : row - column + COLS, :] = source[pl.ds(plane + shift, COLS, stride=PLANES), :]
 
 
 def upwind(courant, below_cell, above_cell):
     return courant * jnp.where(courant > 0.0, below_cell, above_cell)
 
 
-def sweep(fields, below, above, left, right, halos, store, lanes, unrolled):
-    for tile in range(lanes // 128):
-        at_lanes = pl.ds(tile * 128, 128)
-        for planes, source in ((BELOW, below), (ABOVE, above)):
-            for k, (field, plane) in enumerate(planes):
-                at_rows = pl.ds(16 + plane_slot(plane), COLS, stride=8)
-                halos[field].at[tile][at_rows, :] = source[k * COLS : (k + 1) * COLS, at_lanes]
-        for columns, source in ((LEFT, left), (RIGHT, right)):
-            for k, (field, column, plane) in enumerate(corner_list(columns)):
-                at = (column + 2) * 8 + plane_slot(plane)
-                row = len(columns) * 8 + k
-                halos[field].at[tile][at : at + 1, :] = source[row : row + 1, at_lanes]
-
+def sweep(lowest, load_own, load_halo, store, lanes, unrolled):
     plane = lax.broadcasted_iota(jnp.int32, (8, lanes), 0)
     cycle = lax.broadcasted_iota(jnp.int32, (8, lanes), 1)
     first, last = plane == 0, plane == 7
@@ -98,22 +111,7 @@
     axis_cell, rim_cell = cycle == 0, cycle == NR - 1
 
     def load(field, column):
-        if isinstance(column, int) and (column, field) in [(c, f) for f, c in LEFT]:
-            at = LEFT.index((field, column)) * 8
-            own = left[at : at + 8, :]
-        elif isinstance(column, int) and (column, field) in [(c, f) for f, c in RIGHT]:
-            at = RIGHT.index((field, column)) * 8
-            own = right[at : at + 8, :]
-        elif isinstance(column, int):
-            own = fields[field][column * 8 : column * 8 + 8, :]
-        else:
-            own = fields[field][pl.ds(pl.multiple_of(column * 8, 8), 8), :]
-        if isinstance(column, int):
-            at_rows = pl.ds((column + 2) * 8, 8)
-        else:
-            at_rows = pl.ds(pl.multiple_of(column * 8 + 16, 8), 8)
-        tiles = [halos[field].at[tile][at_rows, :] for tile in range(lanes // 128)]
-        return own, jnp.concatenate(tiles, axis=1) if len(tiles) > 1 else tiles[0]
+        return load_own(field, column), load_halo(field, column)
 
     def next_plane(pair):
         own, halo = (pltpu.roll(a, 7, 0) for a in pair)
@@ -149,7 +147,7 @@
 
     def step(column, state, stage):
         v1_old, face_a_old, v3_old, face_b_old = state
-        v1 = axial(load(0, column), load(1, column)) if stage < 6 else None
+        v1 = axial(load(0, column), load(1, column))
         face_a = v3 = face_b = None
         if stage >= 1:
             face_a = flux(load(2, column - 1), v1_old, v1)
@@ -164,22 +162,42 @@
         return v1, face_a, v3, face_b
 
     state = (None, None, None, None)
-    for stage, column in enumerate(range(-2, 4)):
-        state = step(column, state, stage if stage < 4 else 4)
+    for stage in range(6):
+        state = step(lowest + stage, state, stage)
     if unrolled:
-        for column in range(4, 32):
-            state = step(column, state, 4)
+        for stage in range(6, 34):
+            state = step(lowest + stage, state, stage)
     else:
-        state = lax.fori_loop(4, 32, lambda column, s: step(column, s, 4), state)
-    for column in (32, 33):
-        state = step(column, state, 4)
-
-
-def near_kernel(f, ca, ct, cr, below, above, left, right, crossing, out, h0, h1, h2, h3, swept):
+        state = lax.fori_loop(lowest + 6, lowest + 34, lambda column, s: step(column, s, 6), state, unroll=4)
+    for stage in (34, 35):
+        state = step(lowest + stage, state, stage)
+
+
+def near_kernel(*refs):
+    fields, (below, above, left, crossing, out), halos, swept = refs[:4], refs[4:9], refs[9:13], refs[13]
+    lowest = -4
+    for planes, source in ((BELOW, below), (ABOVE, above)):
+        for k, (field, plane) in enumerate(planes):
+            rows = pl.ds(-lowest * 8 + plane_slot(plane), COLS, stride=8)
+            halos[field][rows, :] = source[k * COLS : (k + 1) * COLS, :]
+    for k, (field, column, plane) in enumerate(NEAR_CORNERS):
+        at = (column - lowest) * 8 + plane_slot(plane)
+        row = len(NEAR_LEFT) * 8 + k
+        halos[field][at : at + 1, :] = left[row : row + 1, :]
+
+    def load_own(field, column):
+        if column < 0:
+            at = NEAR_LEFT.index((field, column)) * 8
+            return left[at : at + 8, :]
+        return fields[field][column * 8 : column * 8 + 8, :]
+
+    def load_halo(field, column):
+        return halos[field][(column - lowest) * 8 : (column - lowest + 1) * 8, :]
+
     def store(column, values):
-        swept[column * 8 : column * 8 + 8, :] = values
-
-    sweep((f, ca, ct, cr), below, above, left, right, (h0, h1, h2, h3), store, 128, True)
+        swept[(column + 2) * 8 : (column + 3) * 8, :] = values
+
+    sweep(lowest, load_own, load_halo, store, 128, True)
     turned = swept[...].T
     out[pl.ds(0, R_AX, stride=4), :] = turned[:R_AX, :128]
     out[pl.ds(1, R_AX, stride=4), :] = turned[:R_AX, 128:]
@@ -187,14 +205,38 @@
     out[pl.ds(3, R_AX, stride=4), :] = crossing[R_AX:, :]
 
 
-def far_kernel(f, ca, ct, cr, below, above, left, right, out, h0, h1, h2, h3):
+def far_kernel(*refs):
+    fields, (near_below, near_above, below, above, left, right, out, first_tile) = refs[:4], refs[4:12]
+    halos = refs[12:]
+    lowest = -2
+    for planes, near, entries, far in ((BELOW, near_below, FAR_BELOW, below), (ABOVE, near_above, FAR_ABOVE, above)):
+        for k, (field, plane) in enumerate(planes):
+            rows = pl.ds(-lowest * 8 + plane_slot(plane), COLS, stride=8)
+            halos[field].at[0][rows, :] = near[k * COLS : (k + 1) * COLS, :]
+        for tile, field, plane, column, count, row in entries:
+            rows = pl.ds((column - lowest) * 8 + plane_slot(plane), count, stride=8)
+            halos[field].at[tile][rows, :] = far[row : row + count, :]
+
+    def load_own(field, column):
+        if not isinstance(column, int):
+            return fields[field][pl.ds(pl.multiple_of(column * 8, 8), 8), :]
+        for columns, source in ((LEFT, left), (RIGHT, right)):
+            if (field, column) in columns:
+                at = columns.index((field, column)) * 8
+                return source[at : at + 8, :]
+        return fields[field][column * 8 : column * 8 + 8, :]
+
+    def load_halo(field, column):
+        at = (column - lowest) * 8
+        rows = pl.ds(at if isinstance(at, int) else pl.multiple_of(at, 8), 8)
+        return jnp.concatenate([halos[field].at[tile][rows, :] for tile in range(TILES)], axis=1)
+
     def store(column, values):
-        if isinstance(column, int):
-            out[column * 8 : column * 8 + 8, :] = values
-        else:
-            out[pl.ds(pl.multiple_of(column * 8, 8), 8), :] = values
-
-    sweep((f, ca, ct, cr), below, above, left, right, (h0, h1, h2, h3), store, NR, False)
+        rows = pl.ds(column * 8 if isinstance(column, int) else pl.multiple_of(column * 8, 8), 8)
+        out[rows, :] = values
+        first_tile[rows, :] = values[:, :128]
+
+    sweep(lowest, load_own, load_halo, store, NR, False)
 
 
 def pieces(values, count):
@@ -294,7 +336,10 @@
     same = plane[:, None] == plane[None, :]
     block = np.concatenate([np.where(same, np.cos(inner), 0.0), np.where(same, -np.sin(inner), 0.0)], axis=1)
     turn = 2 * np.pi * np.arange(KD)[:, None] * column[None, :] / 2048
-    twiddle = np.concatenate([np.cos(turn), -np.sin(turn)], axis=0).astype(np.float32)
+    mode = np.arange(KD)[:, None] + 64 * column[None, :]
+    shift = 2 * np.pi * (2 * mode % 2048) / 2048
+    turns = [np.cos(turn), -np.sin(turn), np.cos(shift), np.sin(shift)]
+    twiddle = np.concatenate(turns, axis=0).astype(np.float32)
     return (*halves(first), *halves(block), twiddle, *halves(last))
 
 
@@ -309,12 +354,13 @@
     )
     outer = dot3((first_h[...], first_l[...]), pieces(sectors, 2))
     re, im = outer[:KD], outer[KD:]
-    t_re, t_im = twiddle[:KD, :], twiddle[KD:, :]
+    t_re, t_im, s_re, s_im = (twiddle[k * KD : (k + 1) * KD, :] for k in range(4))
     turned = jnp.concatenate([re * t_re - im * t_im, re * t_im + im * t_re], axis=0)
     block = (block_h[...], block_l[...])
     inner = dot3(pieces(turned, 2), block)
     re = inner[:KD, :ROWS] - inner[KD:, ROWS:]
     im = inner[:KD, ROWS:] + inner[KD:, :ROWS]
+    re, im = re * s_re - im * s_im, re * s_im + im * s_re
     mode = lax.broadcasted_iota(jnp.int32, (KD, ROWS), 0) + 64 * (
         lax.broadcasted_iota(jnp.int32, (KD, ROWS), 1) // PLANES
     )
@@ -331,7 +377,7 @@
     out[pl.ds(1, R_AX, stride=2), :] = result[:, 128:]
 
 
-def final_kernel(received, delta, swept, out):
+def final_kernel(received, delta, swept, _, out):
     near = jnp.concatenate(
         [received[pl.ds(0, R_AX, stride=2), :], received[pl.ds(1, R_AX, stride=2), :]], axis=1
     )
@@ -340,24 +386,26 @@
     out[...] = jnp.where(cycle < R_AX, near.T, swept[...])
 
 
-def block(rows, lanes, row=0):
-    return pl.BlockSpec((rows, lanes), lambda i: (row, 0))
-
-
-def lane_tile(rows):
-    return pl.BlockSpec((rows, 128), lambda i: (0, i))
-
-
-def call(kernel, inputs, specs, out_shapes, out_specs, scratch=(), cost=1.0, steps=1, **options):
+def block(rows, lanes, row=0, lane=0):
+    return pl.BlockSpec((rows, lanes), lambda i: (row, lane))
+
+
+def whole(array):
+    return block(*array.shape)
+
+
+def call(kernel, inputs, specs, out_shapes, out_specs=None, scratch=(), cost=1.0, vmem=32, **options):
+    if out_specs is None:
+        out_specs = jax.tree.map(whole, out_shapes)
     return pl.pallas_call(
         kernel,
-        grid=(steps,),
+        grid=(1,),
         in_specs=list(specs),
         out_specs=out_specs,
         out_shape=out_shapes,
         scratch_shapes=list(scratch),
         cost_estimate=pl.CostEstimate(flops=int(cost * 1e6), bytes_accessed=int(cost * 3e6), transcendentals=0),
-        compiler_params=pltpu.CompilerParams(vmem_limit_bytes=32 * 1024 * 1024),
+        compiler_params=pltpu.CompilerParams(vmem_limit_bytes=vmem * 1024 * 1024),
         **options,
     )(*inputs)
 
@@ -377,80 +425,81 @@
     landing_column,
 ):
     ax_count, az_count = lax.axis_size("ax"), lax.axis_size("az")
+    higher_ax, higher_az = ([(i, (i + 1) % n) for i in range(n)] for n in (ax_count, az_count))
+    lower_ax, lower_az = ([(j, i) for i, j in pairs] for pairs in (higher_ax, higher_az))
     fields = [a.reshape(ROWS, NR) for a in (fraction, courant_axial, courant_azimuth, courant_radial)]
-    n_below, n_above = len(BELOW) * COLS, len(ABOVE) * COLS
-
-    up, down = call(
-        pack_planes,
-        fields,
-        [lane_tile(ROWS)] * 4,
-        (shape(n_below, NR), shape(n_above, NR)),
-        (lane_tile(n_below), lane_tile(n_above)),
-        steps=NR // 128,
-    )
-    below = lax.ppermute(up, "ax", [(i, (i + 1) % ax_count) for i in range(ax_count)])
-    above = lax.ppermute(down, "ax", [((i + 1) % ax_count, i) for i in range(ax_count)])
+
+    near_up, near_down, far_right, far_left = call(
+        pack_first,
+        fields * 3,
+        [block(ROWS, 128)] * 4 + [block(16, NR)] * 4 + [block(16, NR, 15)] * 4,
+        (
+            shape(len(BELOW) * COLS, 128),
+            shape(len(ABOVE) * COLS, 128),
+            shape(len(LEFT) * 8, NR),
+            shape(len(RIGHT) * 8, NR),
+        ),
+        vmem=60,
+    )
+    near_below = lax.ppermute(near_up, "ax", higher_ax)
+    near_above = lax.ppermute(near_down, "ax", lower_ax)
+    left = lax.ppermute(far_right, "az", higher_az)
+    right = lax.ppermute(far_left, "az", lower_az)
 
     crossing, volume = call(
         crossing_kernel,
         (plane_code, strip_width, tile_reader.T, landing_column.T),
         [block(COLS, 128), block(COLS, 128), block(PLANES, COLS), block(PLANES, COLS)],
         (shape(2 * R_AX, 128), shape(XR, ROWS)),
-        (block(2 * R_AX, 128), block(XR, ROWS)),
-    )
-
-    to_right, to_left = call(
-        pack_columns,
-        (*fields, *fields, below, above),
-        [block(16, NR)] * 4 + [block(16, NR, 15)] * 4 + [block(n_below, NR), block(n_above, NR)],
-        (shape(LEFT_ROWS, NR), shape(RIGHT_ROWS, NR)),
-        (block(LEFT_ROWS, NR), block(RIGHT_ROWS, NR)),
-    )
-    left = lax.ppermute(to_right, "az", [(i, (i + 1) % az_count) for i in range(az_count)])
-    right = lax.ppermute(to_left, "az", [((i + 1) % az_count, i) for i in range(az_count)])
-
-    parts = (*fields, below, above, left, right)
-
-    def part_specs(lanes):
-        return [block(ROWS, lanes)] * 4 + [block(a.shape[0], lanes) for a in (below, above, left, right)]
-
-    def halo_scratch(lanes):
-        return [pltpu.VMEM((lanes // 128, (COLS + 4) * 8, 128), F32)] * 4
+    )
+
+    near_right = call(
+        pack_near_columns,
+        (*fields, near_below, near_above),
+        [block(32, 128, 7)] * 4 + [whole(near_below), whole(near_above)],
+        shape(NEAR_ROWS, 128),
+    )
+    near_left = lax.ppermute(near_right, "az", higher_az)
+
+    far_up, far_down = call(
+        pack_far_planes,
+        (*(f for f in fields for _ in range(TILES - 1)), left, right),
+        [block(ROWS, 128, 0, tile) for _ in fields for tile in range(1, TILES)] + [whole(left), whole(right)],
+        (shape(FAR_BELOW_ROWS, 128), shape(FAR_ABOVE_ROWS, 128)),
+    )
+    far_below = lax.ppermute(far_up, "ax", higher_ax)
+    far_above = lax.ppermute(far_down, "ax", lower_ax)
 
     send = call(
         near_kernel,
-        (*parts, crossing),
-        part_specs(128) + [block(2 * R_AX, 128)],
+        (*fields, near_below, near_above, near_left, crossing),
+        [block(ROWS, 128)] * 4 + [whole(a) for a in (near_below, near_above, near_left, crossing)],
         shape(4 * R_AX, 128),
-        block(4 * R_AX, 128),
-        halo_scratch(128) + [pltpu.VMEM((ROWS, 128), F32)],
+        scratch=[pltpu.VMEM((36 * 8, 128), F32)] * 4 + [pltpu.VMEM((ROWS, 128), F32)],
     )
     got = lax.all_to_all(send.reshape(R_AX, 4, 128), "az", 0, 0, tiled=True).reshape(4 * R_AX, 128)
-    swept = call(far_kernel, parts, part_specs(NR), shape(ROWS, NR), block(ROWS, NR), halo_scratch(NR), cost=4.0)
+
+    halos = (near_below, near_above, far_below, far_above, left, right)
+    swept, first_tile = call(
+        far_kernel,
+        (*fields, *halos),
+        [whole(a) for a in (*fields, *halos)],
+        (shape(ROWS, NR), shape(ROWS, 128)),
+        scratch=[pltpu.VMEM((TILES, 36 * 8, 128), F32)] * 4,
+        cost=4.0,
+    )
 
     tables = filter_tables()
-    back = call(
-        filter_kernel,
-        (got, *tables),
-        [block(4 * R_AX, 128)] + [block(*t.shape) for t in tables],
-        shape(2 * R_AX, 128),
-        block(2 * R_AX, 128),
-    )
+    back = call(filter_kernel, (got, *tables), [whole(a) for a in (got, *tables)], shape(2 * R_AX, 128))
     returned = lax.all_to_all(back.reshape(R_AX, 2, 128), "az", 0, 0, tiled=True).reshape(2 * R_AX, 128)
-    delta = call(
-        arrival_kernel,
-        (got, volume),
-        [block(4 * R_AX, 128), block(XR, ROWS)],
-        shape(XR, ROWS),
-        block(XR, ROWS),
-    )
+    delta = call(arrival_kernel, (got, volume), [whole(got), whole(volume)], shape(XR, ROWS))
     out = call(
         final_kernel,
-        (returned, delta, swept),
-        [block(2 * R_AX, 128), block(XR, ROWS), block(ROWS, 128)],
+        (returned, delta, first_tile, swept),
+        [whole(returned), whole(delta), whole(first_tile), pl.BlockSpec(memory_space=pl.ANY)],
         shape(ROWS, NR),
         block(ROWS, 128),
-        input_output_aliases={2: 0},
+        input_output_aliases={3: 0},
     )
     return out.reshape(COLS, PLANES, NR)
 

time: 65.4 us -> 59 us (0.902)
  blocking collectives: 21.7 us -> 0 us
  starting transfers between devices: 13.5 us -> 28.8 us
  Pallas kernels: 11.9 us -> 10 us
  waiting for transfers between devices: 13.4 us -> 14.9 us
    all_to_all x1 -> x0, blocking collectives: 21.7 us -> none  [local(): lax.all_to_all(send.reshape(R_AX, 4, 128), 'az', 0, 0, tiled=True)]
    all_to_all x0 -> x1, starting transfers between devices: none -> 13.4 us  [local(): lax.all_to_all(send.reshape(R_AX, 4, 128), 'az', 0, 0, tiled=True)]
    ppermute x4 -> x7, waiting for transfers between devices: 10.7 us -> 2.13 us  [the longest x1 1.97 us: local(): near_above = lax.ppermute(near_down, 'ax', lower_ax)]
    all_to_all x0 -> x1, waiting for transfers between devices: none -> 6.56 us  [local(): lax.all_to_all(send.reshape(R_AX, 4, 128), 'az', 0, 0, tiled=True)]
    all_to_all x1, waiting for transfers between devices: 2.71 us -> 6.24 us  [local(): lax.all_to_all(back.reshape(R_AX, 2, 128), 'az', 0, 0, tiled=True)]
    pallas_call x8 -> x9, Pallas kernels: 11.9 us -> 10 us  [call(): pl.pallas_call(kernel, grid=(1,), in_specs=list(specs), out_specs=out_spe...]
    ppermute x4 -> x7, starting transfers between devices: 8.61 us -> 10.4 us  [the longest x1 3.57 us: local(): near_left = lax.ppermute(near_right, 'az', higher_az)]
    unnamed x38 -> x40, local copies, waits for them, and re-layouts: 4.25 us -> 4.6 us
  transfers between devices with their start and end apart: 5 -> 9, of which waited for: 4 -> 4; matrix products, arithmetic and copies ran while one was open for 0% -> 0% of each run, Pallas kernels for 12% -> 12%
where the time goes in v2:
time: 59 us; the launch traced here: 58.5 us
  starting transfers between devices  28.8 us (49%)
  waiting for transfers between devices  14.9 us (25%)
  Pallas kernels  10 us (17%)
  local copies, waits for them, and re-layouts  4.6 us (8%)
    all_to_all x1, starting transfers between devices, local(): lax.all_to_all(send.reshape(R_AX, 4, 128), 'az', 0, 0, tiled=True)  13.4 us
    pallas_call x9, Pallas kernels, call(): pl.pallas_call(kernel, grid=(1,), in_specs=list(specs), out_specs=out_spe...  10 us
    all_to_all x1, waiting for transfers between devices, local(): lax.all_to_all(send.reshape(R_AX, 4, 128), 'az', 0, 0, tiled=True)  6.56 us
    all_to_all x1, waiting for transfers between devices, local(): lax.all_to_all(back.reshape(R_AX, 2, 128), 'az', 0, 0, tiled=True)  6.24 us
    all_to_all x1, starting transfers between devices, local(): lax.all_to_all(back.reshape(R_AX, 2, 128), 'az', 0, 0, tiled=True)  5.01 us
    unnamed x40, local copies, waits for them, and re-layouts  4.6 us
    ppermute x1, starting transfers between devices, local(): near_left = lax.ppermute(near_right, 'az', higher_az)  3.57 us
    ppermute x1, starting transfers between devices, local(): near_below = lax.ppermute(near_up, 'ax', higher_ax)  2.13 us
  transfers between devices with their start and end apart: 9, of which 4 were waited for; matrix products, arithmetic and copies ran while one was open for 0% of the time, Pallas kernels for 12%

profile of v2, /device:TPU:1, one launch (start us, length us, event | category | flops | bytes accessed | tf_op | source)
XLA Modules:
  0.0 58.5 jit_solution(15809106500570339035)
XLA Ops:
  0.0 2.1 %shard_map.145 = (f32[192,128]{1,0:T(8,128)}, f32[160,128]{1,0:T(8,128)}, f32[56,512]{1,0:T(8,128)}, f32[48,512]{1,0:T(8,128)}) custom-call(f32[256,512]{1,0:T(8,128)} %bitcast.11, f32[256,512]{1,0:T(8,128)} %bitcast.20, f32[256,512]{1,0:T(8,128)} %bitcast.29, f32[256,512]{1,0:T(8,128)} %bitcast.38, f32[256,512]{1,0:T(8,128)} %bitcast.12, ...), custom_call_target="tpu_custom_call" | custom-call | flops 1000000 | bytes 3000000 | tf_op jit(solution)/shard_map/pallas_call | solution.py:400
  2.1 2.1 %collective-permute-start = (f32[192,128]{1,0:T(8,128)}, f32[192,128]{1,0:T(8,128)S(1)}, u32[]{:S(2)}, u32[]{:S(2)}) collective-permute-start(f32[192,128]{1,0:T(8,128)} %get-tuple-element.15), channel_id=1, source_target_pairs={{0,64},{64,128},{128,192},{192,0},{1,65},{65,129},{129,193},{193,1... | collective-permute-start | bytes 294920 | tf_op jit(solution)/shard_map/ppermute | solution.py:444
  4.2 1.5 %collective-permute-start.1 = (f32[160,128]{1,0:T(8,128)}, f32[160,128]{1,0:T(8,128)S(1)}, u32[]{:S(2)}, u32[]{:S(2)}) collective-permute-start(f32[160,128]{1,0:T(8,128)} %get-tuple-element.16), channel_id=1, source_target_pairs={{64,0},{128,64},{192,128},{0,192},{65,1},{129,65},{193,129},{1,193... | collective-permute-start | bytes 245768 | tf_op jit(solution)/shard_map/ppermute | solution.py:445
  5.7 2.0 %collective-permute-done.1.refs_5_ = f32[160,128]{1,0:T(8,128)S(1)} collective-permute-done((f32[160,128]{1,0:T(8,128)}, f32[160,128]{1,0:T(8,128)S(1)}, u32[]{:S(2)}, u32[]{:S(2)}) %collective-permute-start.1) | collective-permute-done | bytes 81952 | tf_op jit(solution)/shard_map/ppermute | solution.py:445
  8.0 3.6 %collective-permute-start.2 = (f32[168,128]{1,0:T(8,128)S(1)}, f32[168,128]{1,0:T(8,128)S(1)}, u32[]{:S(2)}, u32[]{:S(2)}) collective-permute-start(f32[168,128]{1,0:T(8,128)S(1)} %shard_map.146), channel_id=1, source_target_pairs={{0,1},{1,2},{2,3},{3,4},{4,5},{5,6},{6,7},{7,8},{8,9},{9,10},{10,1... | collective-permute-start | bytes 258056 | tf_op jit(solution)/shard_map/ppermute | solution.py:462
  11.6 0.4 collective-permute-start.4
  12.1 0.6 shard_map.147
  12.6 0.6 %copy-done.10 = f32[16,256]{1,0:T(8,128)} copy-done((f32[16,256]{1,0:T(8,128)}, f32[16,256]{1,0:T(8,128)S(1)}, u32[]{:S(2)}) %copy-start.10) | copy-done | bytes 16408
  13.2 1.1 %shard_map.148 = f32[256,128]{1,0:T(8,128)} custom-call(f32[256,512]{1,0:T(8,128)S(1)} %bitcast.15, f32[256,512]{1,0:T(8,128)S(1)} %bitcast.24, f32[256,512]{1,0:T(8,128)S(1)} %bitcast.33, f32[256,512]{1,0:T(8,128)S(1)} %bitcast.42, f32[192,128]{1,0:T(8,128)S(1)} %collective-permute-done.refs_4_, f32[160,128]{1,0:T(8,128)S(1)} %collective-permute-done.1.refs_5_, ...), custom_call_target="tpu_custom_call" | custom-call | flops 1000000 | bytes 3000000 | tf_op jit(solution)/shard_map/pallas_call | solution.py:400
  14.3 13.4 %all-to-all-start = ((f32[64,4,128]{2,1,0:T(4,128)}), f32[64,4,128]{2,1,0:T(4,128)S(1)}, u32[]{:S(2)}, u32[]{:S(2)}) async-start(f32[64,4,128]{2,1,0:T(4,128)} %bitcast.6), calls=%async_computation | async-start | bytes 262144 | tf_op jit(solution)/shard_map/all_to_all | solution.py:480
  27.7 1.1 %shard_map.151 = (f32[664,128]{1,0:T(8,128)}, f32[552,128]{1,0:T(8,128)}) custom-call(f32[256,512]{1,0:T(8,128)S(1)} %bitcast.16, f32[256,512]{1,0:T(8,128)S(1)} %bitcast.17, f32[256,512]{1,0:T(8,128)S(1)} %bitcast.18, f32[256,512]{1,0:T(8,128)S(1)} %bitcast.25, f32[256,512]{1,0:T(8,128)S(1)} %bitcast.26, f32[256,512]{1,0:T(8,128)S(1)} %bitcast.27, ...), custom_call_target="tpu_custom_call" | custom-call | flops 1000000 | bytes 3000000 | tf_op jit(solution)/shard_map/pallas_call | solution.py:400
  28.8 1.3 %collective-permute-start.5 = (f32[664,128]{1,0:T(8,128)}, f32[664,128]{1,0:T(8,128)S(1)}, u32[]{:S(2)}, u32[]{:S(2)}) collective-permute-start(f32[664,128]{1,0:T(8,128)} %get-tuple-element.21), channel_id=1, source_target_pairs={{0,64},{64,128},{128,192},{192,0},{1,65},{65,129},{129,193},{193,1... | collective-permute-start | bytes 1019912 | tf_op jit(solution)/shard_map/ppermute | solution.py:470
  30.1 1.4 %collective-permute-start.6 = (f32[552,128]{1,0:T(8,128)}, f32[552,128]{1,0:T(8,128)S(1)}, u32[]{:S(2)}, u32[]{:S(2)}) collective-permute-start(f32[552,128]{1,0:T(8,128)} %get-tuple-element.22), channel_id=1, source_target_pairs={{64,0},{128,64},{192,128},{0,192},{65,1},{129,65},{193,129},{1,193... | collective-permute-start | bytes 847880 | tf_op jit(solution)/shard_map/ppermute | solution.py:471
  31.5 6.6 %all-to-all-done = f32[64,4,128]{2,1,0:T(4,128)S(1)} async-done(((f32[64,4,128]{2,1,0:T(4,128)}), f32[64,4,128]{2,1,0:T(4,128)S(1)}, u32[]{:S(2)}, u32[]{:S(2)}) %all-to-all-start) | async-done | bytes 131104 | tf_op jit(solution)/shard_map/all_to_all | solution.py:480
  38.1 0.9 %copy-done.5 = bf16[256,512]{1,0:T(8,128)(2,1)S(1)} copy-done((bf16[256,512]{1,0:T(8,128)(2,1)S(1)}, bf16[256,512]{1,0:T(8,128)(2,1)}, u32[]{:S(2)}) %copy-start.5) | copy-done | bytes 262168
  39.0 0.9 %copy-done.7 = f32[160,256]{1,0:T(8,128)S(1)} copy-done((f32[160,256]{1,0:T(8,128)S(1)}, f32[160,256]{1,0:T(8,128)}, u32[]{:S(2)}) %copy-start.7) | copy-done | bytes 163864
  39.9 0.7 %copy-done.14 = bf16[64,80]{1,0:T(8,128)(2,1)S(1)} copy-done((bf16[64,80]{1,0:T(8,128)(2,1)S(1)}, bf16[64,80]{1,0:T(8,128)(2,1)}, u32[]{:S(2)}) %copy-start.14) | copy-done | bytes 10264
  40.7 0.7 %copy-done.15 = bf16[64,80]{1,0:T(8,128)(2,1)S(1)} copy-done((bf16[64,80]{1,0:T(8,128)(2,1)S(1)}, bf16[64,80]{1,0:T(8,128)(2,1)}, u32[]{:S(2)}) %copy-start.15) | copy-done | bytes 10264
  41.4 1.0 %shard_map.149 = f32[128,128]{1,0:T(8,128)S(1)} custom-call(f32[256,128]{1,0:T(8,128)S(1)} %bitcast.47, bf16[80,64]{1,0:T(8,128)(2,1)S(1)} %copy-done.8, bf16[80,64]{1,0:T(8,128)(2,1)S(1)} %copy-done.9, bf16[256,512]{1,0:T(8,128)(2,1)S(1)} %copy-done.4, bf16[256,512]{1,0:T(8,128)(2,1)S(1)} %copy-done.5, f32[160,256]{1,0:T(8,128)S(1)} %copy-done.7, ...), custom_call_target="tpu_custom_call" | custom-call | flops 1000000 | bytes 3000000 | tf_op jit(solution)/shard_map/pallas_call | solution.py:400
  42.4 0.6 %copy-done.6 = f32[128,128]{1,0:T(8,128)} copy-done((f32[128,128]{1,0:T(8,128)}, f32[128,128]{1,0:T(8,128)S(1)}, u32[]{:S(2)}) %copy-start.6) | copy-done | bytes 65560
  43.0 5.0 %all-to-all-start.1 = ((f32[64,2,128]{2,1,0:T(2,128)}), f32[64,2,128]{2,1,0:T(2,128)S(1)}, u32[]{:S(2)}, u32[]{:S(2)}) async-start(f32[64,2,128]{2,1,0:T(2,128)} %bitcast.50), calls=%async_computation.1 | async-start | bytes 131072 | tf_op jit(solution)/shard_map/all_to_all | solution.py:494
  48.4 3.2 %shard_map.152 = (f32[256,512]{1,0:T(8,128)}, f32[256,128]{1,0:T(8,128)S(1)}) custom-call(f32[256,512]{1,0:T(8,128)S(1)} %bitcast.19, f32[256,512]{1,0:T(8,128)S(1)} %bitcast.28, f32[256,512]{1,0:T(8,128)S(1)} %bitcast.37, f32[256,512]{1,0:T(8,128)S(1)} %bitcast.46, f32[192,128]{1,0:T(8,128)S(1)} %collective-permute-done.refs_4_, ...), custom_call_target="tpu_custom_call" | custom-call | flops 4000000 | bytes 12000000 | tf_op jit(solution)/shard_map/pallas_call | solution.py:400
  51.5 6.2 %all-to-all-done.1 = f32[64,2,128]{2,1,0:T(2,128)S(1)} async-done(((f32[64,2,128]{2,1,0:T(2,128)}), f32[64,2,128]{2,1,0:T(2,128)S(1)}, u32[]{:S(2)}, u32[]{:S(2)}) %all-to-all-start.1) | async-done | bytes 65568 | tf_op jit(solution)/shard_map/all_to_all | solution.py:494
  57.8 0.8 %shard_map.153 = f32[256,512]{1,0:T(8,128)} custom-call(f32[128,128]{1,0:T(8,128)S(1)} %bitcast.49, f32[16,256]{1,0:T(8,128)S(1)} %shard_map.150.delta, f32[256,128]{1,0:T(8,128)S(1)} %get-tuple-element.23.swept, f32[256,512]{1,0:T(8,128)} %get-tuple-element.24._), custom_call_target="tpu_custom_call", output_to_operand_aliasing={{}: (3, {})} | custom-call | flops 1000000 | bytes 3000000 | tf_op jit(solution)/shard_map/pallas_call | solution.py:400
  (43 shorter events, 0.7 us)
Async XLA Ops:
  0.0 7.9 %copy-start = (f32[32,8,512]{2,1,0:T(8,128)S(1)}, f32[32,8,512]{2,1,0:T(8,128)}, u32[]{:S(2)}) copy-start(f32[32,8,512]{2,1,0:T(8,128)} %param.15) | copy-start | bytes 1572868
  0.0 7.9 %copy-start.1 = (f32[32,8,512]{2,1,0:T(8,128)S(1)}, f32[32,8,512]{2,1,0:T(8,128)}, u32[]{:S(2)}) copy-start(f32[32,8,512]{2,1,0:T(8,128)} %param.16) | copy-start | bytes 1572868
  0.0 7.9 %copy-start.2 = (f32[32,8,512]{2,1,0:T(8,128)S(1)}, f32[32,8,512]{2,1,0:T(8,128)}, u32[]{:S(2)}) copy-start(f32[32,8,512]{2,1,0:T(8,128)} %param.17) | copy-start | bytes 1572868
  0.0 7.9 %copy-start.3 = (f32[32,8,512]{2,1,0:T(8,128)S(1)}, f32[32,8,512]{2,1,0:T(8,128)}, u32[]{:S(2)}) copy-start(f32[32,8,512]{2,1,0:T(8,128)} %param.18) | copy-start | bytes 1572868
  2.1 5.8 %collective-permute-start = (f32[192,128]{1,0:T(8,128)}, f32[192,128]{1,0:T(8,128)S(1)}, u32[]{:S(2)}, u32[]{:S(2)}) collective-permute-start(f32[192,128]{1,0:T(8,128)} %get-tuple-element.15), channel_id=1, source_target_pairs={{0,64},{64,128},{128,192},{192,0},{1,65},{65,129},{129,193},{193,1... | collective-permute-start | bytes 294920 | tf_op jit(solution)/shard_map/ppermute | solution.py:444
  4.2 7.3 %copy-start.18 = (f32[56,512]{1,0:T(8,128)S(1)}, f32[56,512]{1,0:T(8,128)}, u32[]{:S(2)}) copy-start(f32[56,512]{1,0:T(8,128)} %get-tuple-element.19) | copy-start | bytes 344068
  4.2 7.4 %copy-start.19 = (f32[48,512]{1,0:T(8,128)S(1)}, f32[48,512]{1,0:T(8,128)}, u32[]{:S(2)}) copy-start(f32[48,512]{1,0:T(8,128)} %get-tuple-element.20) | copy-start | bytes 294916
  4.2 3.5 %collective-permute-start.1 = (f32[160,128]{1,0:T(8,128)}, f32[160,128]{1,0:T(8,128)S(1)}, u32[]{:S(2)}, u32[]{:S(2)}) collective-permute-start(f32[160,128]{1,0:T(8,128)} %get-tuple-element.16), channel_id=1, source_target_pairs={{64,0},{128,64},{192,128},{0,192},{65,1},{129,65},{193,129},{1,193... | collective-permute-start | bytes 245768 | tf_op jit(solution)/shard_map/ppermute | solution.py:445
  7.9 4.2 %copy-start.12 = (s32[32,128]{1,0:T(8,128)S(1)}, s32[32,128]{1,0:T(8,128)}, u32[]{:S(2)}) copy-start(s32[32,128]{1,0:T(8,128)} %code.1) | copy-start | bytes 49156
  7.9 4.2 %copy-start.13 = (f32[32,128]{1,0:T(8,128)S(1)}, f32[32,128]{1,0:T(8,128)}, u32[]{:S(2)}) copy-start(f32[32,128]{1,0:T(8,128)} %width.1) | copy-start | bytes 49156
  7.9 4.1 %copy-start.17 = (s32[32,8]{0,1:T(8,128)S(1)}, s32[32,8]{0,1:T(8,128)}, u32[]{:S(2)}) copy-start(s32[32,8]{0,1:T(8,128)} %param.22) | copy-start | bytes 3076
  7.9 4.1 %copy-start.16 = (s32[32,8]{0,1:T(8,128)S(1)}, s32[32,8]{0,1:T(8,128)}, u32[]{:S(2)}) copy-start(s32[32,8]{0,1:T(8,128)} %param.21) | copy-start | bytes 3076
  8.0 5.3 %collective-permute-start.2 = (f32[168,128]{1,0:T(8,128)S(1)}, f32[168,128]{1,0:T(8,128)S(1)}, u32[]{:S(2)}, u32[]{:S(2)}) collective-permute-start(f32[168,128]{1,0:T(8,128)S(1)} %shard_map.146), channel_id=1, source_target_pairs={{0,1},{1,2},{2,3},{3,4},{4,5},{5,6},{6,7},{7,8},{8,9},{9,10},{10,1... | collective-permute-start | bytes 258056 | tf_op jit(solution)/shard_map/ppermute | solution.py:462
  11.5 16.2 %collective-permute-start.3 = (f32[56,512]{1,0:T(8,128)S(1)}, f32[56,512]{1,0:T(8,128)S(1)}, u32[]{:S(2)}, u32[]{:S(2)}) collective-permute-start(f32[56,512]{1,0:T(8,128)S(1)} %copy-done.18), channel_id=1, source_target_pairs={{0,1},{1,2},{2,3},{3,4},{4,5},{5,6},{6,7},{7,8},{8,9},{9,10},{10,1... | collective-permute-start | bytes 344072 | tf_op jit(solution)/shard_map/ppermute | solution.py:446
  11.6 16.1 %collective-permute-start.4 = (f32[48,512]{1,0:T(8,128)S(1)}, f32[48,512]{1,0:T(8,128)S(1)}, u32[]{:S(2)}, u32[]{:S(2)}) collective-permute-start(f32[48,512]{1,0:T(8,128)S(1)} %copy-done.19), channel_id=1, source_target_pairs={{1,0},{2,1},{3,2},{4,3},{5,4},{6,5},{7,6},{8,7},{9,8},{10,9},{11,1... | collective-permute-start | bytes 294920 | tf_op jit(solution)/shard_map/ppermute | solution.py:447
  14.3 23.7 %all-to-all-start = ((f32[64,4,128]{2,1,0:T(4,128)}), f32[64,4,128]{2,1,0:T(4,128)S(1)}, u32[]{:S(2)}, u32[]{:S(2)}) async-start(f32[64,4,128]{2,1,0:T(4,128)} %bitcast.6), calls=%async_computation | async-start | bytes 262144 | tf_op jit(solution)/shard_map/all_to_all | solution.py:480
  27.7 10.4 %copy-start.4 = (bf16[256,512]{1,0:T(8,128)(2,1)S(1)}, bf16[256,512]{1,0:T(8,128)(2,1)}, u32[]{:S(2)}) copy-start(bf16[256,512]{1,0:T(8,128)(2,1)} %constant.16.clone.block_h) | copy-start | bytes 786436
  27.7 10.4 %copy-start.8 = (bf16[80,64]{1,0:T(8,128)(2,1)S(1)}, bf16[80,64]{1,0:T(8,128)(2,1)}, u32[]{:S(2)}) copy-start(bf16[80,64]{1,0:T(8,128)(2,1)} %constant.14.clone.first_h) | copy-start | bytes 30724
  27.7 10.3 %copy-start.9 = (bf16[80,64]{1,0:T(8,128)(2,1)S(1)}, bf16[80,64]{1,0:T(8,128)(2,1)}, u32[]{:S(2)}) copy-start(bf16[80,64]{1,0:T(8,128)(2,1)} %constant.15.clone.first_l) | copy-start | bytes 30724
  28.8 19.6 %collective-permute-start.5 = (f32[664,128]{1,0:T(8,128)}, f32[664,128]{1,0:T(8,128)S(1)}, u32[]{:S(2)}, u32[]{:S(2)}) collective-permute-start(f32[664,128]{1,0:T(8,128)} %get-tuple-element.21), channel_id=1, source_target_pairs={{0,64},{64,128},{128,192},{192,0},{1,65},{65,129},{129,193},{193,1... | collective-permute-start | bytes 1019912 | tf_op jit(solution)/shard_map/ppermute | solution.py:470
  30.1 18.3 %collective-permute-start.6 = (f32[552,128]{1,0:T(8,128)}, f32[552,128]{1,0:T(8,128)S(1)}, u32[]{:S(2)}, u32[]{:S(2)}) collective-permute-start(f32[552,128]{1,0:T(8,128)} %get-tuple-element.22), channel_id=1, source_target_pairs={{64,0},{128,64},{192,128},{0,192},{65,1},{129,65},{193,129},{1,193... | collective-permute-start | bytes 847880 | tf_op jit(solution)/shard_map/ppermute | solution.py:471
  38.1 1.0 %copy-start.5 = (bf16[256,512]{1,0:T(8,128)(2,1)S(1)}, bf16[256,512]{1,0:T(8,128)(2,1)}, u32[]{:S(2)}) copy-start(bf16[256,512]{1,0:T(8,128)(2,1)} %constant.17.clone.block_l) | copy-start | bytes 786436
  43.0 5.0 %copy-start.11 = (f32[16,256]{1,0:T(8,128)S(1)}, f32[16,256]{1,0:T(8,128)}, u32[]{:S(2)}) copy-start(f32[16,256]{1,0:T(8,128)} %copy-done.10) | copy-start | bytes 49156
  43.0 14.8 %all-to-all-start.1 = ((f32[64,2,128]{2,1,0:T(2,128)}), f32[64,2,128]{2,1,0:T(2,128)S(1)}, u32[]{:S(2)}, u32[]{:S(2)}) async-start(f32[64,2,128]{2,1,0:T(2,128)} %bitcast.50), calls=%async_computation.1 | async-start | bytes 131072 | tf_op jit(solution)/shard_map/all_to_all | solution.py:494
  (5 other events, 3.6 us)

commit v3 on v2

--- a/solution.py
+++ b/solution.py
@@ -58,22 +58,34 @@
     return plane % 16 - 8
 
 
+def copy_all(pairs, semaphores, first=0):
+    copies = [pltpu.make_async_copy(a, b, semaphores.at[first + k]) for k, (a, b) in enumerate(pairs)]
+    for copy in copies:
+        copy.start()
+    return copies
+
+
+def copy_out(source, target, semaphore):
+    copy = pltpu.make_async_copy(source, target, semaphore)
+    copy.start()
+    copy.wait()
+
+
 def pack_first(*refs):
-    near, low, high, (up, down, right, left) = refs[:4], refs[4:8], refs[8:12], refs[12:]
-    for k, (field, plane) in enumerate(BELOW):
-        up[k * COLS : (k + 1) * COLS, :] = near[field][pl.ds(plane + PLANES, COLS, stride=PLANES), :]
-    for k, (field, plane) in enumerate(ABOVE):
-        down[k * COLS : (k + 1) * COLS, :] = near[field][pl.ds(plane - PLANES, COLS, stride=PLANES), :]
-    for k, (field, column) in enumerate(LEFT):
-        right[k * 8 : k * 8 + 8, :] = high[field][(column + 2) * 8 : (column + 3) * 8, :]
-    for k, (field, column) in enumerate(RIGHT):
-        left[k * 8 : k * 8 + 8, :] = low[field][(column - COLS) * 8 : (column - COLS + 1) * 8, :]
+    fields, tiles, (up, down, semaphores) = refs[:4], refs[4:8], refs[8:]
+    copies = copy_all([(f.at[:, pl.ds(0, 128)], tile) for f, tile in zip(fields, tiles)], semaphores)
+    for field, copy in enumerate(copies):
+        copy.wait()
+        for planes, out, shift in ((BELOW, up, PLANES), (ABOVE, down, -PLANES)):
+            for k, (of, plane) in enumerate(planes):
+                if of == field:
+                    out[k * COLS : (k + 1) * COLS, :] = tiles[field][pl.ds(plane + shift, COLS, stride=PLANES), :]
 
 
 def pack_near_columns(*refs):
-    high, (below, above, right) = refs[:4], refs[4:]
+    tiles, (below, above, right) = refs[:4], refs[4:]
     for k, (field, column) in enumerate(NEAR_LEFT):
-        right[k * 8 : k * 8 + 8, :] = high[field][(column + 4) * 8 : (column + 5) * 8, :]
+        right[k * 8 : k * 8 + 8, :] = tiles[field][(column + COLS) * 8 : (column + COLS + 1) * 8, :]
     right[len(NEAR_LEFT) * 8 :, :] = jnp.zeros((48, 128), F32)
     for k, (field, column, plane) in enumerate(NEAR_CORNERS):
         planes, source = (BELOW, below) if plane < 0 else (ABOVE, above)
@@ -82,8 +94,20 @@
         right[at : at + 1, :] = source[row : row + 1, :]
 
 
+def pack_far_columns(*refs):
+    fields, (_, right, left, semaphores) = refs[:4], refs[4:]
+    pairs = []
+    for columns, out, shift in ((LEFT, right, COLS), (RIGHT, left, -COLS)):
+        for field in range(4):
+            at = [k for k, (f, _) in enumerate(columns) if f == field]
+            source = fields[field].at[pl.ds((columns[at[0]][1] + shift) * 8, len(at) * 8), :]
+            pairs.append((source, out.at[pl.ds(at[0] * 8, len(at) * 8), :]))
+    for copy in copy_all(pairs, semaphores):
+        copy.wait()
+
+
 def pack_far_planes(*refs):
-    own, (left, right, up, down) = refs[: 4 * (TILES - 1)], refs[4 * (TILES - 1) :]
+    tiles, (left, right, up, down) = refs[:4], refs[4:]
     for entries, out, shift in ((FAR_BELOW, up, PLANES), (FAR_ABOVE, down, -PLANES)):
         for tile, field, plane, column, count, row in entries:
             lanes = pl.ds(tile * 128, 128)
@@ -93,8 +117,11 @@
                         origin = columns.index((field, column + at)) * 8 + plane + shift
                         out[row + at : row + at + 1, :] = source[origin : origin + 1, lanes]
             if tile:
-                source = own[field * (TILES - 1) + tile - 1]
-                out[row - column : row - column + COLS, :] = source[pl.ds(plane + shift, COLS, stride=PLANES), :]
+                rows = pl.ds((tile - 1) * ROWS + plane + shift, COLS, stride=PLANES)
+                out[row - column : row - column + COLS, :] = tiles[field][rows, :]
+        used = sum(e[4] for e in entries)
+        if used < out.shape[0]:
+            out[used:, :] = jnp.zeros((out.shape[0] - used, 128), F32)
 
 
 def upwind(courant, below_cell, above_cell):
@@ -174,7 +201,8 @@
 
 
 def near_kernel(*refs):
-    fields, (below, above, left, crossing, out), halos, swept = refs[:4], refs[4:9], refs[9:13], refs[13]
+    fields, (below, above, left, crossing, send) = refs[:4], refs[4:9]
+    halos, (swept, out, semaphore) = refs[9:13], refs[13:]
     lowest = -4
     for planes, source in ((BELOW, below), (ABOVE, above)):
         for k, (field, plane) in enumerate(planes):
@@ -203,11 +231,12 @@
     out[pl.ds(1, R_AX, stride=4), :] = turned[:R_AX, 128:]
     out[pl.ds(2, R_AX, stride=4), :] = crossing[:R_AX, :]
     out[pl.ds(3, R_AX, stride=4), :] = crossing[R_AX:, :]
+    copy_out(out, send, semaphore)
 
 
 def far_kernel(*refs):
-    fields, (near_below, near_above, below, above, left, right, out, first_tile) = refs[:4], refs[4:12]
-    halos = refs[12:]
+    near_tiles, tiles, (near_below, near_above, below, above, left, right) = refs[:4], refs[4:8], refs[8:14]
+    result, first_tile, *halos, out, semaphore = refs[14:]
     lowest = -2
     for planes, near, entries, far in ((BELOW, near_below, FAR_BELOW, below), (ABOVE, near_above, FAR_ABOVE, above)):
         for k, (field, plane) in enumerate(planes):
@@ -218,13 +247,14 @@
             halos[field].at[tile][rows, :] = far[row : row + count, :]
 
     def load_own(field, column):
-        if not isinstance(column, int):
-            return fields[field][pl.ds(pl.multiple_of(column * 8, 8), 8), :]
         for columns, source in ((LEFT, left), (RIGHT, right)):
-            if (field, column) in columns:
+            if isinstance(column, int) and (field, column) in columns:
                 at = columns.index((field, column)) * 8
                 return source[at : at + 8, :]
-        return fields[field][column * 8 : column * 8 + 8, :]
+        at = column * 8 if isinstance(column, int) else pl.multiple_of(column * 8, 8)
+        parts = [near_tiles[field][pl.ds(at, 8), :]]
+        parts += [tiles[field][pl.ds(tile * ROWS + at, 8), :] for tile in range(TILES - 1)]
+        return jnp.concatenate(parts, axis=1)
 
     def load_halo(field, column):
         at = (column - lowest) * 8
@@ -237,6 +267,7 @@
         first_tile[rows, :] = values[:, :128]
 
     sweep(lowest, load_own, load_halo, store, NR, False)
+    copy_out(out, result, semaphore)
 
 
 def pieces(values, count):
@@ -274,7 +305,14 @@
     return strip_width * strip_area
 
 
-def crossing_kernel(code, width, reader, landing, out, volume_out):
+def crossing_kernel(*refs):
+    (code, width, reader, landing), fields, tables = refs[:4], refs[4:8], refs[8:15]
+    (out, volume_out), tiles, held, semaphores = refs[15:17], refs[17:21], refs[21:28], refs[28]
+    pairs = list(zip(tables, held))
+    for field, tile in zip(fields, tiles):
+        for k in range(1, TILES):
+            pairs.append((field.at[:, pl.ds(k * 128, 128)], tile.at[pl.ds((k - 1) * ROWS, ROWS), :]))
+    copies = copy_all(pairs, semaphores)
     iota = functools.partial(lax.broadcasted_iota, jnp.int32)
     volume = plic_volume(code[...], width[...])
     both = jnp.concatenate([reader[...].astype(F32), landing[...].astype(F32)], axis=0).astype(BF16)
@@ -302,6 +340,8 @@
     target = landing_rows * 8.0 + (row % 8).astype(F32) + 1.0
     marked = jnp.where(lane.astype(F32) == rank, target, 0.0)
     out[R_AX:, :] = mm(chosen, marked.astype(BF16))
+    for copy in copies:
+        copy.wait()
 
 
 def arrival_kernel(received, volume, out):
@@ -348,7 +388,7 @@
     return mm(ah, bh) + (mm(al, bh) + mm(ah, bl))
 
 
-def filter_kernel(received, first_h, first_l, block_h, block_l, twiddle, last_h, last_l, out):
+def filter_kernel(received, first_h, first_l, block_h, block_l, twiddle, last_h, last_l, send, out, semaphore):
     sectors = jnp.concatenate(
         [received[pl.ds(0, R_AX, stride=4), :], received[pl.ds(1, R_AX, stride=4), :]], axis=1
     )
@@ -375,43 +415,40 @@
     result = dot3((last_h[...], last_l[...]), pieces(turned, 2))
     out[pl.ds(0, R_AX, stride=2), :] = result[:, :128]
     out[pl.ds(1, R_AX, stride=2), :] = result[:, 128:]
-
-
-def final_kernel(received, delta, swept, _, out):
+    copy_out(out, send, semaphore)
+
+
+def final_kernel(received, delta, swept, _, result, out, semaphore):
     near = jnp.concatenate(
         [received[pl.ds(0, R_AX, stride=2), :], received[pl.ds(1, R_AX, stride=2), :]], axis=1
     )
     near = jnp.concatenate([near[:XR] + delta[...], near[XR:], jnp.zeros((R_AX, ROWS), F32)], axis=0)
     cycle = lax.broadcasted_iota(jnp.int32, (ROWS, 128), 1)
     out[...] = jnp.where(cycle < R_AX, near.T, swept[...])
-
-
-def block(rows, lanes, row=0, lane=0):
-    return pl.BlockSpec((rows, lanes), lambda i: (row, lane))
-
-
-def whole(array):
-    return block(*array.shape)
-
-
-def call(kernel, inputs, specs, out_shapes, out_specs=None, scratch=(), cost=1.0, vmem=32, **options):
-    if out_specs is None:
-        out_specs = jax.tree.map(whole, out_shapes)
+    copy_out(out, result.at[:, pl.ds(0, 128)], semaphore)
+
+
+VMEM, HBM = pltpu.VMEM, pltpu.HBM
+DMA = pltpu.SemaphoreType.DMA
+
+
+def call(kernel, inputs, outputs, scratch=(), cost=1.0, aliases=None):
+    arrays, specs = [], []
+    for given in inputs:
+        array, space = given if isinstance(given, tuple) else (given, VMEM)
+        arrays.append(pltpu.with_memory_space_constraint(array, HBM) if space is HBM else array)
+        specs.append(pl.BlockSpec(memory_space=space))
+    out_specs = [pl.BlockSpec(memory_space=o.memory_space) for o in outputs]
     return pl.pallas_call(
         kernel,
-        grid=(1,),
-        in_specs=list(specs),
+        in_specs=specs,
         out_specs=out_specs,
-        out_shape=out_shapes,
+        out_shape=list(outputs),
         scratch_shapes=list(scratch),
+        input_output_aliases=aliases or {},
         cost_estimate=pl.CostEstimate(flops=int(cost * 1e6), bytes_accessed=int(cost * 3e6), transcendentals=0),
-        compiler_params=pltpu.CompilerParams(vmem_limit_bytes=vmem * 1024 * 1024),
-        **options,
-    )(*inputs)
-
-
-def shape(*dims):
-    return jax.ShapeDtypeStruct(dims, F32)
+        compiler_params=pltpu.CompilerParams(vmem_limit_bytes=16 * 1024 * 1024),
+    )(*arrays)
 
 
 def local(
@@ -427,79 +464,73 @@
     ax_count, az_count = lax.axis_size("ax"), lax.axis_size("az")
     higher_ax, higher_az = ([(i, (i + 1) % n) for i in range(n)] for n in (ax_count, az_count))
     lower_ax, lower_az = ([(j, i) for i, j in pairs] for pairs in (higher_ax, higher_az))
-    fields = [a.reshape(ROWS, NR) for a in (fraction, courant_axial, courant_azimuth, courant_radial)]
-
-    near_up, near_down, far_right, far_left = call(
+    fields = [(a.reshape(ROWS, NR), HBM) for a in (fraction, courant_axial, courant_azimuth, courant_radial)]
+
+    *near_tiles, near_up, near_down = call(
         pack_first,
-        fields * 3,
-        [block(ROWS, 128)] * 4 + [block(16, NR)] * 4 + [block(16, NR, 15)] * 4,
-        (
-            shape(len(BELOW) * COLS, 128),
-            shape(len(ABOVE) * COLS, 128),
-            shape(len(LEFT) * 8, NR),
-            shape(len(RIGHT) * 8, NR),
-        ),
-        vmem=60,
+        fields,
+        [VMEM((ROWS, 128), F32)] * 4 + [VMEM((len(BELOW) * COLS, 128), F32), VMEM((len(ABOVE) * COLS, 128), F32)],
+        [DMA((4,))],
     )
     near_below = lax.ppermute(near_up, "ax", higher_ax)
     near_above = lax.ppermute(near_down, "ax", lower_ax)
+
+    tables = filter_tables()
+    results = call(
+        crossing_kernel,
+        [plane_code, strip_width, tile_reader.T, landing_column.T, *fields, *((t, HBM) for t in map(jnp.asarray, tables))],
+        [VMEM((2 * R_AX, 128), F32), VMEM((XR, ROWS), F32)]
+        + [VMEM(((TILES - 1) * ROWS, 128), F32)] * 4
+        + [VMEM(t.shape, t.dtype) for t in tables],
+        [DMA((len(tables) + 4 * (TILES - 1),))],
+    )
+    (crossing, volume), tiles, held_tables = results[:2], results[2:6], results[6:]
+
+    (near_right,) = call(pack_near_columns, [*near_tiles, near_below, near_above], [VMEM((NEAR_ROWS, 128), F32)])
+    near_left = lax.ppermute(near_right, "az", higher_az)
+    (send,) = call(
+        near_kernel,
+        [*near_tiles, near_below, near_above, near_left, crossing],
+        [HBM((4 * R_AX, 128), F32)],
+        [VMEM((36 * 8, 128), F32)] * 4 + [VMEM((ROWS, 128), F32), VMEM((4 * R_AX, 128), F32), DMA],
+    )
+    got = lax.all_to_all(send.reshape(R_AX, 4, 128), "az", 0, 0, tiled=True).reshape(4 * R_AX, 128)
+
+    far_right, far_left = call(
+        pack_far_columns,
+        [*fields, (send, HBM)],
+        [VMEM((len(LEFT) * 8, NR), F32), VMEM((len(RIGHT) * 8, NR), F32)],
+        [DMA((8,))],
+    )
     left = lax.ppermute(far_right, "az", higher_az)
     right = lax.ppermute(far_left, "az", lower_az)
-
-    crossing, volume = call(
-        crossing_kernel,
-        (plane_code, strip_width, tile_reader.T, landing_column.T),
-        [block(COLS, 128), block(COLS, 128), block(PLANES, COLS), block(PLANES, COLS)],
-        (shape(2 * R_AX, 128), shape(XR, ROWS)),
-    )
-
-    near_right = call(
-        pack_near_columns,
-        (*fields, near_below, near_above),
-        [block(32, 128, 7)] * 4 + [whole(near_below), whole(near_above)],
-        shape(NEAR_ROWS, 128),
-    )
-    near_left = lax.ppermute(near_right, "az", higher_az)
-
     far_up, far_down = call(
         pack_far_planes,
-        (*(f for f in fields for _ in range(TILES - 1)), left, right),
-        [block(ROWS, 128, 0, tile) for _ in fields for tile in range(1, TILES)] + [whole(left), whole(right)],
-        (shape(FAR_BELOW_ROWS, 128), shape(FAR_ABOVE_ROWS, 128)),
+        [*tiles, left, right],
+        [VMEM((FAR_BELOW_ROWS, 128), F32), VMEM((FAR_ABOVE_ROWS, 128), F32)],
     )
     far_below = lax.ppermute(far_up, "ax", higher_ax)
     far_above = lax.ppermute(far_down, "ax", lower_ax)
 
-    send = call(
-        near_kernel,
-        (*fields, near_below, near_above, near_left, crossing),
-        [block(ROWS, 128)] * 4 + [whole(a) for a in (near_below, near_above, near_left, crossing)],
-        shape(4 * R_AX, 128),
-        scratch=[pltpu.VMEM((36 * 8, 128), F32)] * 4 + [pltpu.VMEM((ROWS, 128), F32)],
-    )
-    got = lax.all_to_all(send.reshape(R_AX, 4, 128), "az", 0, 0, tiled=True).reshape(4 * R_AX, 128)
-
-    halos = (near_below, near_above, far_below, far_above, left, right)
     swept, first_tile = call(
         far_kernel,
-        (*fields, *halos),
-        [whole(a) for a in (*fields, *halos)],
-        (shape(ROWS, NR), shape(ROWS, 128)),
-        scratch=[pltpu.VMEM((TILES, 36 * 8, 128), F32)] * 4,
+        [*near_tiles, *tiles, near_below, near_above, far_below, far_above, left, right],
+        [HBM((ROWS, NR), F32), VMEM((ROWS, 128), F32)],
+        [VMEM((TILES, 36 * 8, 128), F32)] * 4 + [VMEM((ROWS, NR), F32), DMA],
         cost=4.0,
     )
 
-    tables = filter_tables()
-    back = call(filter_kernel, (got, *tables), [whole(a) for a in (got, *tables)], shape(2 * R_AX, 128))
+    (back,) = call(
+        filter_kernel, [got, *held_tables], [HBM((2 * R_AX, 128), F32)], [VMEM((2 * R_AX, 128), F32), DMA]
+    )
     returned = lax.all_to_all(back.reshape(R_AX, 2, 128), "az", 0, 0, tiled=True).reshape(2 * R_AX, 128)
-    delta = call(arrival_kernel, (got, volume), [whole(got), whole(volume)], shape(XR, ROWS))
-    out = call(
+    (delta,) = call(arrival_kernel, [got, volume], [VMEM((XR, ROWS), F32)])
+    (out,) = call(
         final_kernel,
-        (returned, delta, first_tile, swept),
-        [whole(returned), whole(delta), whole(first_tile), pl.BlockSpec(memory_space=pl.ANY)],
-        shape(ROWS, NR),
-        block(ROWS, 128),
-        input_output_aliases={3: 0},
+        [returned, delta, first_tile, (swept, HBM)],
+        [HBM((ROWS, NR), F32)],
+        [VMEM((ROWS, 128), F32), DMA],
+        aliases={3: 0},
     )
     return out.reshape(COLS, PLANES, NR)
 

time: 59 us -> 61.9 us (1.049)
  Pallas kernels: 10 us -> 12.1 us
  starting transfers between devices: 28.8 us -> 30.9 us
  local copies, waits for them, and re-layouts: 4.6 us -> 3.34 us
    ppermute x1, starting transfers between devices: 0.41 us -> 3.42 us  [local(): right = lax.ppermute(far_left, 'az', lower_az)]
    all_to_all x1, starting transfers between devices: 13.4 us -> 10.7 us  [local(): lax.all_to_all(send.reshape(R_AX, 4, 128), 'az', 0, 0, tiled=True)]
    pallas_call x9 -> x10, Pallas kernels: 10 us -> 12.1 us  [call(): pl.pallas_call(kernel, in_specs=specs, out_specs=out_specs, out_shape=lis...]
    ppermute x1, starting transfers between devices: 0.1 us -> 1.95 us  [local(): left = lax.ppermute(far_right, 'az', higher_az)]
    unnamed x40 -> x28, local copies, waits for them, and re-layouts: 4.6 us -> 3.34 us
  transfers between devices with their start and end apart: 9 -> 9, of which waited for: 4 -> 4; matrix products, arithmetic and copies ran while one was open for 0% -> 0% of each run, Pallas kernels for 12% -> 13%
where the time goes in v3:
time: 61.9 us; the launch traced here: 61.3 us
  starting transfers between devices  30.9 us (50%)
  waiting for transfers between devices  14.8 us (24%)
  Pallas kernels  12.1 us (20%)
  local copies, waits for them, and re-layouts  3.34 us (5%)
    pallas_call x10, Pallas kernels, call(): pl.pallas_call(kernel, in_specs=specs, out_specs=out_specs, out_shape=lis...  12.1 us
    all_to_all x1, starting transfers between devices, local(): lax.all_to_all(send.reshape(R_AX, 4, 128), 'az', 0, 0, tiled=True)  10.7 us
    all_to_all x1, waiting for transfers between devices, local(): lax.all_to_all(send.reshape(R_AX, 4, 128), 'az', 0, 0, tiled=True)  6.68 us
    all_to_all x1, waiting for transfers between devices, local(): lax.all_to_all(back.reshape(R_AX, 2, 128), 'az', 0, 0, tiled=True)  6.14 us
    all_to_all x1, starting transfers between devices, local(): lax.all_to_all(back.reshape(R_AX, 2, 128), 'az', 0, 0, tiled=True)  4.89 us
    ppermute x1, starting transfers between devices, local(): near_left = lax.ppermute(near_right, 'az', higher_az)  3.57 us
    ppermute x1, starting transfers between devices, local(): right = lax.ppermute(far_left, 'az', lower_az)  3.42 us
    unnamed x28, local copies, waits for them, and re-layouts  3.34 us
  transfers between devices with their start and end apart: 9, of which 4 were waited for; matrix products, arithmetic and copies ran while one was open for 0% of the time, Pallas kernels for 13%

profile of v3, /device:TPU:1, one launch (start us, length us, event | category | flops | bytes accessed | tf_op | source)
XLA Modules:
  0.0 61.3 jit_solution(13705934531655227379)
XLA Ops:
  0.0 1.1 %shard_map.145 = (f32[256,128]{1,0:T(8,128)S(1)}, f32[256,128]{1,0:T(8,128)S(1)}, f32[256,128]{1,0:T(8,128)S(1)}, f32[256,128]{1,0:T(8,128)S(1)}, f32[192,128]{1,0:T(8,128)S(1)}, /*index=5*/f32[160,128]{1,0:T(8,128)S(1)}) custom-call(f32[256,512]{1,0:T(8,128)} %bitcast.16, f32[256,512]{1,0:T(8,128)} %bitcast.19, f32[256,512]{1,0:T(8,128)} %bitcast.22, ...), custom_call_target="tpu_custom_call" | custom-call | flops 1000000 | bytes 3000000 | tf_op jit(solution)/shard_map/pallas_call | solution.py:442
  1.1 2.2 %collective-permute-start = (f32[192,128]{1,0:T(8,128)S(1)}, f32[192,128]{1,0:T(8,128)S(1)}, u32[]{:S(2)}, u32[]{:S(2)}) collective-permute-start(f32[192,128]{1,0:T(8,128)S(1)} %get-tuple-element.34), channel_id=1, source_target_pairs={{0,64},{64,128},{128,192},{192,0},{1,65},{65,129},{129,193},{193,1... | collective-permute-start | bytes 294920 | tf_op jit(solution)/shard_map/ppermute | solution.py:475
  3.4 1.5 %collective-permute-start.1 = (f32[160,128]{1,0:T(8,128)S(1)}, f32[160,128]{1,0:T(8,128)S(1)}, u32[]{:S(2)}, u32[]{:S(2)}) collective-permute-start(f32[160,128]{1,0:T(8,128)S(1)} %get-tuple-element.35), channel_id=1, source_target_pairs={{64,0},{128,64},{192,128},{0,192},{65,1},{129,65},{193,129},{1,193... | collective-permute-start | bytes 245768 | tf_op jit(solution)/shard_map/ppermute | solution.py:476
  4.9 1.8 %collective-permute-done.1.refs_5_.refs_9_ = f32[160,128]{1,0:T(8,128)S(1)} collective-permute-done((f32[160,128]{1,0:T(8,128)S(1)}, f32[160,128]{1,0:T(8,128)S(1)}, u32[]{:S(2)}, u32[]{:S(2)}) %collective-permute-start.1) | collective-permute-done | bytes 81952 | tf_op jit(solution)/shard_map/ppermute | solution.py:476
  6.8 3.6 %collective-permute-start.2 = (f32[168,128]{1,0:T(8,128)S(1)}, f32[168,128]{1,0:T(8,128)S(1)}, u32[]{:S(2)}, u32[]{:S(2)}) collective-permute-start(f32[168,128]{1,0:T(8,128)S(1)} %shard_map.146), channel_id=1, source_target_pairs={{0,1},{1,2},{2,3},{3,4},{4,5},{5,6},{6,7},{7,8},{8,9},{9,10},{10,1... | collective-permute-start | bytes 258056 | tf_op jit(solution)/shard_map/ppermute | solution.py:490
  10.4 2.0 %shard_map.147 = (f32[128,128]{1,0:T(8,128)S(1)}, f32[16,256]{1,0:T(8,128)S(1)}, f32[768,128]{1,0:T(8,128)S(1)}, f32[768,128]{1,0:T(8,128)S(1)}, f32[768,128]{1,...) custom-call(s32[32,128]{1,0:T(8,128)S(1)} %copy-done.4, ...), custom_call_target="tpu_custom_call" | custom-call | flops 1000000 | bytes 3000000 | tf_op jit(solution)/shard_map/pallas_call | solution.py:442
  12.4 1.1 %shard_map.148.refs_4_ = f32[256,128]{1,0:T(8,128)} custom-call(f32[256,128]{1,0:T(8,128)S(1)} %get-tuple-element.30.refs_0_, f32[256,128]{1,0:T(8,128)S(1)} %get-tuple-element.31.refs_1_, f32[256,128]{1,0:T(8,128)S(1)} %get-tuple-element.32.refs_2_, f32[256,128]{1,0:T(8,128)S(1)} %get-tuple-element.33.refs_3_, ...), custom_call_target="tpu_custom_call" | custom-call | flops 1000000 | bytes 3000000 | tf_op jit(solution)/shard_map/pallas_call | solution.py:442
  13.6 0.9 %shard_map.151 = (f32[56,512]{1,0:T(8,128)S(1)}, f32[48,512]{1,0:T(8,128)S(1)}) custom-call(f32[256,512]{1,0:T(8,128)} %bitcast.18, f32[256,512]{1,0:T(8,128)} %bitcast.21, f32[256,512]{1,0:T(8,128)} %bitcast.24, f32[256,512]{1,0:T(8,128)} %bitcast.27, f32[256,128]{1,0:T(8,128)} %shard_map.148.refs_4_), custom_call_target="tpu_custom_call" | custom-call | flops 1000000 | bytes 3000000 | tf_op jit(solution)/shard_map/pallas_call | solution.py:442
  14.5 1.9 %collective-permute-start.3 = (f32[56,512]{1,0:T(8,128)S(1)}, f32[56,512]{1,0:T(8,128)S(1)}, u32[]{:S(2)}, u32[]{:S(2)}) collective-permute-start(f32[56,512]{1,0:T(8,128)S(1)} %get-tuple-element.49), channel_id=1, source_target_pairs={{0,1},{1,2},{2,3},{3,4},{4,5},{5,6},{6,7},{7,8},{8,9},{9,10},{10,1... | collective-permute-start | bytes 344072 | tf_op jit(solution)/shard_map/ppermute | solution.py:505
  16.5 3.4 %collective-permute-start.4 = (f32[48,512]{1,0:T(8,128)S(1)}, f32[48,512]{1,0:T(8,128)S(1)}, u32[]{:S(2)}, u32[]{:S(2)}) collective-permute-start(f32[48,512]{1,0:T(8,128)S(1)} %get-tuple-element.50), channel_id=1, source_target_pairs={{1,0},{2,1},{3,2},{4,3},{5,4},{6,5},{7,6},{8,7},{9,8},{10,9},{11,1... | collective-permute-start | bytes 294920 | tf_op jit(solution)/shard_map/ppermute | solution.py:506
  19.9 10.7 %all-to-all-start = ((f32[64,4,128]{2,1,0:T(4,128)}), f32[64,4,128]{2,1,0:T(4,128)S(1)}, u32[]{:S(2)}, u32[]{:S(2)}) async-start(f32[64,4,128]{2,1,0:T(4,128)} %bitcast.6), calls=%async_computation | async-start | bytes 262144 | tf_op jit(solution)/shard_map/all_to_all | solution.py:497
  30.6 1.0 %shard_map.152 = (f32[664,128]{1,0:T(8,128)}, f32[552,128]{1,0:T(8,128)}) custom-call(f32[768,128]{1,0:T(8,128)S(1)} %get-tuple-element.45.refs_0_.refs_4_, f32[768,128]{1,0:T(8,128)S(1)} %get-tuple-element.46.refs_1_.refs_5_, f32[768,128]{1,0:T(8,128)S(1)} %get-tuple-element.47.refs_2_.refs_6_, f32[768,128]{1,0:T(8,128)S(1)} %get-tuple-element.48.refs_3_.refs_7_, ...), custom_call_target="tpu_custom_call" | custom-call | flops 1000000 | bytes 3000000 | tf_op jit(solution)/shard_map/pallas_call | solution.py:442
  31.6 1.3 %collective-permute-start.5 = (f32[664,128]{1,0:T(8,128)}, f32[664,128]{1,0:T(8,128)S(1)}, u32[]{:S(2)}, u32[]{:S(2)}) collective-permute-start(f32[664,128]{1,0:T(8,128)} %get-tuple-element.51), channel_id=1, source_target_pairs={{0,64},{64,128},{128,192},{192,0},{1,65},{65,129},{129,193},{193,1... | collective-permute-start | bytes 1019912 | tf_op jit(solution)/shard_map/ppermute | solution.py:512
  32.9 1.4 %collective-permute-start.6 = (f32[552,128]{1,0:T(8,128)}, f32[552,128]{1,0:T(8,128)S(1)}, u32[]{:S(2)}, u32[]{:S(2)}) collective-permute-start(f32[552,128]{1,0:T(8,128)} %get-tuple-element.52), channel_id=1, source_target_pairs={{64,0},{128,64},{192,128},{0,192},{65,1},{129,65},{193,129},{1,193... | collective-permute-start | bytes 847880 | tf_op jit(solution)/shard_map/ppermute | solution.py:513
  34.3 6.7 %all-to-all-done = f32[64,4,128]{2,1,0:T(4,128)S(1)} async-done(((f32[64,4,128]{2,1,0:T(4,128)}), f32[64,4,128]{2,1,0:T(4,128)S(1)}, u32[]{:S(2)}, u32[]{:S(2)}) %all-to-all-start) | async-done | bytes 131104 | tf_op jit(solution)/shard_map/all_to_all | solution.py:497
  41.0 0.9 %copy-done.1 = bf16[256,512]{1,0:T(8,128)(2,1)S(1)} copy-done((bf16[256,512]{1,0:T(8,128)(2,1)S(1)}, bf16[256,512]{1,0:T(8,128)(2,1)}, u32[]{:S(2)}) %copy-start.1) | copy-done | bytes 262168
  41.9 0.9 %copy-done.3 = f32[160,256]{1,0:T(8,128)S(1)} copy-done((f32[160,256]{1,0:T(8,128)S(1)}, f32[160,256]{1,0:T(8,128)}, u32[]{:S(2)}) %copy-start.3) | copy-done | bytes 163864
  42.8 0.7 %copy-done.9 = bf16[64,80]{1,0:T(8,128)(2,1)S(1)} copy-done((bf16[64,80]{1,0:T(8,128)(2,1)S(1)}, bf16[64,80]{1,0:T(8,128)(2,1)}, u32[]{:S(2)}) %copy-start.9) | copy-done | bytes 10264
  43.5 0.7 %copy-done.11 = bf16[64,80]{1,0:T(8,128)(2,1)S(1)} copy-done((bf16[64,80]{1,0:T(8,128)(2,1)S(1)}, bf16[64,80]{1,0:T(8,128)(2,1)}, u32[]{:S(2)}) %copy-start.11) | copy-done | bytes 10264
  44.3 1.6 %shard_map.149 = f32[128,128]{1,0:T(8,128)} custom-call(f32[256,128]{1,0:T(8,128)S(1)} %bitcast.11, bf16[80,64]{1,0:T(8,128)(2,1)S(1)} %get-tuple-element.37.first_h, bf16[80,64]{1,0:T(8,128)(2,1)S(1)} %get-tuple-element.38.first_l, bf16[256,512]{1,0:T(8,128)(2,1)S(1)} %get-tuple-element.39.block_h, bf16[256,512]{1,0:T(8,128)(2,1)S(1)} %copy-done.1, ...), custom_call_target="tpu_custom_call" | custom-call | flops 1000000 | bytes 3000000 | tf_op jit(solution)/shard_map/pallas_call | solution.py:442
  45.9 4.9 %all-to-all-start.1 = ((f32[64,2,128]{2,1,0:T(2,128)}), f32[64,2,128]{2,1,0:T(2,128)S(1)}, u32[]{:S(2)}, u32[]{:S(2)}) async-start(f32[64,2,128]{2,1,0:T(2,128)} %bitcast.28), calls=%async_computation.1 | async-start | bytes 131072 | tf_op jit(solution)/shard_map/all_to_all | solution.py:526
  51.2 3.3 %shard_map.153 = (f32[256,512]{1,0:T(8,128)}, f32[256,128]{1,0:T(8,128)S(1)}) custom-call(f32[256,128]{1,0:T(8,128)S(1)} %get-tuple-element.30.refs_0_, f32[256,128]{1,0:T(8,128)S(1)} %get-tuple-element.31.refs_1_, f32[256,128]{1,0:T(8,128)S(1)} %get-tuple-element.32.refs_2_, f32[256,128]{1,0:T(8,128)S(1)} %get-tuple-element.33.refs_3_, ...), custom_call_target="tpu_custom_call" | custom-call | flops 4000000 | bytes 12000000 | tf_op jit(solution)/shard_map/pallas_call | solution.py:442
  54.4 6.1 %all-to-all-done.1 = f32[64,2,128]{2,1,0:T(2,128)S(1)} async-done(((f32[64,2,128]{2,1,0:T(2,128)}), f32[64,2,128]{2,1,0:T(2,128)S(1)}, u32[]{:S(2)}, u32[]{:S(2)}) %all-to-all-start.1) | async-done | bytes 65568 | tf_op jit(solution)/shard_map/all_to_all | solution.py:526
  60.6 0.8 %shard_map.154 = f32[256,512]{1,0:T(8,128)} custom-call(f32[128,128]{1,0:T(8,128)S(1)} %bitcast.13, f32[16,256]{1,0:T(8,128)S(1)} %shard_map.150.delta, f32[256,128]{1,0:T(8,128)S(1)} %get-tuple-element.53.swept, f32[256,512]{1,0:T(8,128)} %get-tuple-element.54._), custom_call_target="tpu_custom_call", output_to_operand_aliasing={{}: (3, {})} | custom-call | flops 1000000 | bytes 3000000 | tf_op jit(solution)/shard_map/pallas_call | solution.py:442
  (32 shorter events, 0.6 us)
Async XLA Ops:
  1.1 5.6 %collective-permute-start = (f32[192,128]{1,0:T(8,128)S(1)}, f32[192,128]{1,0:T(8,128)S(1)}, u32[]{:S(2)}, u32[]{:S(2)}) collective-permute-start(f32[192,128]{1,0:T(8,128)S(1)} %get-tuple-element.34), channel_id=1, source_target_pairs={{0,64},{64,128},{128,192},{192,0},{1,65},{65,129},{129,193},{193,1... | collective-permute-start | bytes 294920 | tf_op jit(solution)/shard_map/ppermute | solution.py:475
  3.4 3.3 %collective-permute-start.1 = (f32[160,128]{1,0:T(8,128)S(1)}, f32[160,128]{1,0:T(8,128)S(1)}, u32[]{:S(2)}, u32[]{:S(2)}) collective-permute-start(f32[160,128]{1,0:T(8,128)S(1)} %get-tuple-element.35), channel_id=1, source_target_pairs={{64,0},{128,64},{192,128},{0,192},{65,1},{129,65},{193,129},{1,193... | collective-permute-start | bytes 245768 | tf_op jit(solution)/shard_map/ppermute | solution.py:476
  6.8 3.6 %copy-start.4 = (s32[32,128]{1,0:T(8,128)S(1)}, s32[32,128]{1,0:T(8,128)}, u32[]{:S(2)}) copy-start(s32[32,128]{1,0:T(8,128)} %refs_0_.1) | copy-start | bytes 49156
  6.8 3.6 %copy-start.5 = (f32[32,128]{1,0:T(8,128)S(1)}, f32[32,128]{1,0:T(8,128)}, u32[]{:S(2)}) copy-start(f32[32,128]{1,0:T(8,128)} %refs_1_.1) | copy-start | bytes 49156
  6.8 3.6 %copy-start.12 = (s32[32,8]{0,1:T(8,128)S(1)}, s32[32,8]{0,1:T(8,128)}, u32[]{:S(2)}) copy-start(s32[32,8]{0,1:T(8,128)} %param.21) | copy-start | bytes 3076
  6.8 3.6 %copy-start.13 = (s32[32,8]{0,1:T(8,128)S(1)}, s32[32,8]{0,1:T(8,128)}, u32[]{:S(2)}) copy-start(s32[32,8]{0,1:T(8,128)} %param.22) | copy-start | bytes 3076
  6.8 5.6 %collective-permute-start.2 = (f32[168,128]{1,0:T(8,128)S(1)}, f32[168,128]{1,0:T(8,128)S(1)}, u32[]{:S(2)}, u32[]{:S(2)}) collective-permute-start(f32[168,128]{1,0:T(8,128)S(1)} %shard_map.146), channel_id=1, source_target_pairs={{0,1},{1,2},{2,3},{3,4},{4,5},{5,6},{6,7},{7,8},{8,9},{9,10},{10,1... | collective-permute-start | bytes 258056 | tf_op jit(solution)/shard_map/ppermute | solution.py:490
  12.4 1.2 %copy-start = (bf16[256,512]{1,0:T(8,128)(2,1)}, bf16[256,512]{1,0:T(8,128)(2,1)S(1)}, u32[]{:S(2)}) copy-start(bf16[256,512]{1,0:T(8,128)(2,1)S(1)} %get-tuple-element.40.block_l) | copy-start | bytes 786436
  12.4 1.2 %copy-start.2 = (f32[160,256]{1,0:T(8,128)}, f32[160,256]{1,0:T(8,128)S(1)}, u32[]{:S(2)}) copy-start(f32[160,256]{1,0:T(8,128)S(1)} %get-tuple-element.41.twiddle) | copy-start | bytes 491524
  12.4 1.2 %copy-start.6 = (f32[16,256]{1,0:T(8,128)}, f32[16,256]{1,0:T(8,128)S(1)}, u32[]{:S(2)}) copy-start(f32[16,256]{1,0:T(8,128)S(1)} %get-tuple-element.44.volume) | copy-start | bytes 49156
  12.4 1.2 %copy-start.8 = (bf16[64,80]{1,0:T(8,128)(2,1)}, bf16[64,80]{1,0:T(8,128)(2,1)S(1)}, u32[]{:S(2)}) copy-start(bf16[64,80]{1,0:T(8,128)(2,1)S(1)} %get-tuple-element.42.last_h) | copy-start | bytes 30724
  12.4 1.2 %copy-start.10 = (bf16[64,80]{1,0:T(8,128)(2,1)}, bf16[64,80]{1,0:T(8,128)(2,1)S(1)}, u32[]{:S(2)}) copy-start(bf16[64,80]{1,0:T(8,128)(2,1)S(1)} %get-tuple-element.43.last_l) | copy-start | bytes 30724
  14.5 16.1 %collective-permute-start.3 = (f32[56,512]{1,0:T(8,128)S(1)}, f32[56,512]{1,0:T(8,128)S(1)}, u32[]{:S(2)}, u32[]{:S(2)}) collective-permute-start(f32[56,512]{1,0:T(8,128)S(1)} %get-tuple-element.49), channel_id=1, source_target_pairs={{0,1},{1,2},{2,3},{3,4},{4,5},{5,6},{6,7},{7,8},{8,9},{9,10},{10,1... | collective-permute-start | bytes 344072 | tf_op jit(solution)/shard_map/ppermute | solution.py:505
  16.5 14.1 %collective-permute-start.4 = (f32[48,512]{1,0:T(8,128)S(1)}, f32[48,512]{1,0:T(8,128)S(1)}, u32[]{:S(2)}, u32[]{:S(2)}) collective-permute-start(f32[48,512]{1,0:T(8,128)S(1)} %get-tuple-element.50), channel_id=1, source_target_pairs={{1,0},{2,1},{3,2},{4,3},{5,4},{6,5},{7,6},{8,7},{9,8},{10,9},{11,1... | collective-permute-start | bytes 294920 | tf_op jit(solution)/shard_map/ppermute | solution.py:506
  19.9 21.1 %all-to-all-start = ((f32[64,4,128]{2,1,0:T(4,128)}), f32[64,4,128]{2,1,0:T(4,128)S(1)}, u32[]{:S(2)}, u32[]{:S(2)}) async-start(f32[64,4,128]{2,1,0:T(4,128)} %bitcast.6), calls=%async_computation | async-start | bytes 262144 | tf_op jit(solution)/shard_map/all_to_all | solution.py:497
  31.6 19.6 %collective-permute-start.5 = (f32[664,128]{1,0:T(8,128)}, f32[664,128]{1,0:T(8,128)S(1)}, u32[]{:S(2)}, u32[]{:S(2)}) collective-permute-start(f32[664,128]{1,0:T(8,128)} %get-tuple-element.51), channel_id=1, source_target_pairs={{0,64},{64,128},{128,192},{192,0},{1,65},{65,129},{129,193},{193,1... | collective-permute-start | bytes 1019912 | tf_op jit(solution)/shard_map/ppermute | solution.py:512
  32.9 18.3 %collective-permute-start.6 = (f32[552,128]{1,0:T(8,128)}, f32[552,128]{1,0:T(8,128)S(1)}, u32[]{:S(2)}, u32[]{:S(2)}) collective-permute-start(f32[552,128]{1,0:T(8,128)} %get-tuple-element.52), channel_id=1, source_target_pairs={{64,0},{128,64},{192,128},{0,192},{65,1},{129,65},{193,129},{1,193... | collective-permute-start | bytes 847880 | tf_op jit(solution)/shard_map/ppermute | solution.py:513
  41.0 1.0 %copy-start.1 = (bf16[256,512]{1,0:T(8,128)(2,1)S(1)}, bf16[256,512]{1,0:T(8,128)(2,1)}, u32[]{:S(2)}) copy-start(bf16[256,512]{1,0:T(8,128)(2,1)} %copy-done) | copy-start | bytes 786436
  41.9 0.9 %copy-start.3 = (f32[160,256]{1,0:T(8,128)S(1)}, f32[160,256]{1,0:T(8,128)}, u32[]{:S(2)}) copy-start(f32[160,256]{1,0:T(8,128)} %copy-done.2) | copy-start | bytes 491524
  42.8 0.7 %copy-start.9 = (bf16[64,80]{1,0:T(8,128)(2,1)S(1)}, bf16[64,80]{1,0:T(8,128)(2,1)}, u32[]{:S(2)}) copy-start(bf16[64,80]{1,0:T(8,128)(2,1)} %copy-done.8) | copy-start | bytes 30724
  43.5 0.7 %copy-start.11 = (bf16[64,80]{1,0:T(8,128)(2,1)S(1)}, bf16[64,80]{1,0:T(8,128)(2,1)}, u32[]{:S(2)}) copy-start(bf16[64,80]{1,0:T(8,128)(2,1)} %copy-done.10) | copy-start | bytes 30724
  45.9 4.9 %copy-start.7 = (f32[16,256]{1,0:T(8,128)S(1)}, f32[16,256]{1,0:T(8,128)}, u32[]{:S(2)}) copy-start(f32[16,256]{1,0:T(8,128)} %copy-done.6) | copy-start | bytes 49156
  45.9 14.7 %all-to-all-start.1 = ((f32[64,2,128]{2,1,0:T(2,128)}), f32[64,2,128]{2,1,0:T(2,128)S(1)}, u32[]{:S(2)}, u32[]{:S(2)}) async-start(f32[64,2,128]{2,1,0:T(2,128)} %bitcast.28), calls=%async_computation.1 | async-start | bytes 131072 | tf_op jit(solution)/shard_map/all_to_all | solution.py:526

commit v4 on v3

--- a/solution.py
+++ b/solution.py
@@ -72,18 +72,27 @@
 
 
 def pack_first(*refs):
-    fields, tiles, (up, down, semaphores) = refs[:4], refs[4:8], refs[8:]
+    fields, tiles, (up, down, right, left, semaphores) = refs[:4], refs[4:8], refs[8:]
     copies = copy_all([(f.at[:, pl.ds(0, 128)], tile) for f, tile in zip(fields, tiles)], semaphores)
+    pairs = []
+    for columns, out, shift in ((LEFT, right, COLS), (RIGHT, left, -COLS)):
+        for field in range(4):
+            at = [k for k, (f, _) in enumerate(columns) if f == field]
+            source = fields[field].at[pl.ds((columns[at[0]][1] + shift) * 8, len(at) * 8), :]
+            pairs.append((source, out.at[pl.ds(at[0] * 8, len(at) * 8), :]))
+    far_copies = copy_all(pairs, semaphores, 4)
     for field, copy in enumerate(copies):
         copy.wait()
         for planes, out, shift in ((BELOW, up, PLANES), (ABOVE, down, -PLANES)):
             for k, (of, plane) in enumerate(planes):
                 if of == field:
                     out[k * COLS : (k + 1) * COLS, :] = tiles[field][pl.ds(plane + shift, COLS, stride=PLANES), :]
+    for copy in far_copies:
+        copy.wait()
 
 
 def pack_near_columns(*refs):
-    tiles, (below, above, right) = refs[:4], refs[4:]
+    tiles, (below, above, _, _, right) = refs[:4], refs[4:]
     for k, (field, column) in enumerate(NEAR_LEFT):
         right[k * 8 : k * 8 + 8, :] = tiles[field][(column + COLS) * 8 : (column + COLS + 1) * 8, :]
     right[len(NEAR_LEFT) * 8 :, :] = jnp.zeros((48, 128), F32)
@@ -94,20 +103,14 @@
         right[at : at + 1, :] = source[row : row + 1, :]
 
 
-def pack_far_columns(*refs):
-    fields, (_, right, left, semaphores) = refs[:4], refs[4:]
+def pack_far_planes(*refs):
+    fields, (left, right, up, down, *tiles, semaphores) = refs[:4], refs[4:]
     pairs = []
-    for columns, out, shift in ((LEFT, right, COLS), (RIGHT, left, -COLS)):
-        for field in range(4):
-            at = [k for k, (f, _) in enumerate(columns) if f == field]
-            source = fields[field].at[pl.ds((columns[at[0]][1] + shift) * 8, len(at) * 8), :]
-            pairs.append((source, out.at[pl.ds(at[0] * 8, len(at) * 8), :]))
+    for field, tile in zip(fields, tiles):
+        for k in range(1, TILES):
+            pairs.append((field.at[:, pl.ds(k * 128, 128)], tile.at[pl.ds((k - 1) * ROWS, ROWS), :]))
     for copy in copy_all(pairs, semaphores):
         copy.wait()
-
-
-def pack_far_planes(*refs):
-    tiles, (left, right, up, down) = refs[:4], refs[4:]
     for entries, out, shift in ((FAR_BELOW, up, PLANES), (FAR_ABOVE, down, -PLANES)):
         for tile, field, plane, column, count, row in entries:
             lanes = pl.ds(tile * 128, 128)
@@ -235,8 +238,9 @@
 
 
 def far_kernel(*refs):
-    near_tiles, tiles, (near_below, near_above, below, above, left, right) = refs[:4], refs[4:8], refs[8:14]
-    result, first_tile, *halos, out, semaphore = refs[14:]
+    sources, (near_below, near_above, below, above, left, right) = refs[:4], refs[4:10]
+    (result, first_tile), halos, fields, (out, semaphores) = refs[10:12], refs[12:16], refs[16:20], refs[20:]
+    copies = copy_all(zip(sources, fields), semaphores)
     lowest = -2
     for planes, near, entries, far in ((BELOW, near_below, FAR_BELOW, below), (ABOVE, near_above, FAR_ABOVE, above)):
         for k, (field, plane) in enumerate(planes):
@@ -251,10 +255,7 @@
             if isinstance(column, int) and (field, column) in columns:
                 at = columns.index((field, column)) * 8
                 return source[at : at + 8, :]
-        at = column * 8 if isinstance(column, int) else pl.multiple_of(column * 8, 8)
-        parts = [near_tiles[field][pl.ds(at, 8), :]]
-        parts += [tiles[field][pl.ds(tile * ROWS + at, 8), :] for tile in range(TILES - 1)]
-        return jnp.concatenate(parts, axis=1)
+        return fields[field][pl.ds(column * 8 if isinstance(column, int) else pl.multiple_of(column * 8, 8), 8), :]
 
     def load_halo(field, column):
         at = (column - lowest) * 8
@@ -266,8 +267,10 @@
         out[rows, :] = values
         first_tile[rows, :] = values[:, :128]
 
+    for copy in copies:
+        copy.wait()
     sweep(lowest, load_own, load_halo, store, NR, False)
-    copy_out(out, result, semaphore)
+    copy_out(out, result, semaphores.at[4])
 
 
 def pieces(values, count):
@@ -306,13 +309,8 @@
 
 
 def crossing_kernel(*refs):
-    (code, width, reader, landing), fields, tables = refs[:4], refs[4:8], refs[8:15]
-    (out, volume_out), tiles, held, semaphores = refs[15:17], refs[17:21], refs[21:28], refs[28]
-    pairs = list(zip(tables, held))
-    for field, tile in zip(fields, tiles):
-        for k in range(1, TILES):
-            pairs.append((field.at[:, pl.ds(k * 128, 128)], tile.at[pl.ds((k - 1) * ROWS, ROWS), :]))
-    copies = copy_all(pairs, semaphores)
+    (code, width, reader, landing), tables, (out, volume_out) = refs[:4], refs[4:11], refs[11:13]
+    copies = copy_all(zip(tables, refs[13:20]), refs[20])
     iota = functools.partial(lax.broadcasted_iota, jnp.int32)
     volume = plic_volume(code[...], width[...])
     both = jnp.concatenate([reader[...].astype(F32), landing[...].astype(F32)], axis=0).astype(BF16)
@@ -466,27 +464,32 @@
     lower_ax, lower_az = ([(j, i) for i, j in pairs] for pairs in (higher_ax, higher_az))
     fields = [(a.reshape(ROWS, NR), HBM) for a in (fraction, courant_axial, courant_azimuth, courant_radial)]
 
-    *near_tiles, near_up, near_down = call(
+    *near_tiles, near_up, near_down, far_right, far_left = call(
         pack_first,
         fields,
-        [VMEM((ROWS, 128), F32)] * 4 + [VMEM((len(BELOW) * COLS, 128), F32), VMEM((len(ABOVE) * COLS, 128), F32)],
-        [DMA((4,))],
+        [VMEM((ROWS, 128), F32)] * 4
+        + [VMEM((len(BELOW) * COLS, 128), F32), VMEM((len(ABOVE) * COLS, 128), F32)]
+        + [VMEM((len(LEFT) * 8, NR), F32), VMEM((len(RIGHT) * 8, NR), F32)],
+        [DMA((12,))],
     )
     near_below = lax.ppermute(near_up, "ax", higher_ax)
     near_above = lax.ppermute(near_down, "ax", lower_ax)
+    left = lax.ppermute(far_right, "az", higher_az)
+    right = lax.ppermute(far_left, "az", lower_az)
 
     tables = filter_tables()
-    results = call(
+    crossing, volume, *held_tables = call(
         crossing_kernel,
-        [plane_code, strip_width, tile_reader.T, landing_column.T, *fields, *((t, HBM) for t in map(jnp.asarray, tables))],
-        [VMEM((2 * R_AX, 128), F32), VMEM((XR, ROWS), F32)]
-        + [VMEM(((TILES - 1) * ROWS, 128), F32)] * 4
-        + [VMEM(t.shape, t.dtype) for t in tables],
-        [DMA((len(tables) + 4 * (TILES - 1),))],
-    )
-    (crossing, volume), tiles, held_tables = results[:2], results[2:6], results[6:]
-
-    (near_right,) = call(pack_near_columns, [*near_tiles, near_below, near_above], [VMEM((NEAR_ROWS, 128), F32)])
+        [plane_code, strip_width, tile_reader.T, landing_column.T, *((jnp.asarray(t), HBM) for t in tables)],
+        [VMEM((2 * R_AX, 128), F32), VMEM((XR, ROWS), F32)] + [VMEM(t.shape, t.dtype) for t in tables],
+        [DMA((len(tables),))],
+    )
+
+    (near_right,) = call(
+        pack_near_columns,
+        [*near_tiles, near_below, near_above, (left, pl.ANY), (right, pl.ANY)],
+        [VMEM((NEAR_ROWS, 128), F32)],
+    )
     near_left = lax.ppermute(near_right, "az", higher_az)
     (send,) = call(
         near_kernel,
@@ -496,27 +499,20 @@
     )
     got = lax.all_to_all(send.reshape(R_AX, 4, 128), "az", 0, 0, tiled=True).reshape(4 * R_AX, 128)
 
-    far_right, far_left = call(
-        pack_far_columns,
-        [*fields, (send, HBM)],
-        [VMEM((len(LEFT) * 8, NR), F32), VMEM((len(RIGHT) * 8, NR), F32)],
-        [DMA((8,))],
-    )
-    left = lax.ppermute(far_right, "az", higher_az)
-    right = lax.ppermute(far_left, "az", lower_az)
     far_up, far_down = call(
         pack_far_planes,
-        [*tiles, left, right],
+        [*fields, left, right],
         [VMEM((FAR_BELOW_ROWS, 128), F32), VMEM((FAR_ABOVE_ROWS, 128), F32)],
+        [VMEM(((TILES - 1) * ROWS, 128), F32)] * 4 + [DMA((4 * (TILES - 1),))],
     )
     far_below = lax.ppermute(far_up, "ax", higher_ax)
     far_above = lax.ppermute(far_down, "ax", lower_ax)
 
     swept, first_tile = call(
         far_kernel,
-        [*near_tiles, *tiles, near_below, near_above, far_below, far_above, left, right],
+        [*fields, near_below, near_above, far_below, far_above, left, right],
         [HBM((ROWS, NR), F32), VMEM((ROWS, 128), F32)],
-        [VMEM((TILES, 36 * 8, 128), F32)] * 4 + [VMEM((ROWS, NR), F32), DMA],
+        [VMEM((TILES, 36 * 8, 128), F32)] * 4 + [VMEM((ROWS, NR), F32)] * 5 + [DMA((5,))],
         cost=4.0,
     )
 

time: 61.9 us -> 57.4 us (0.927)
  local copies, waits for them, and re-layouts: 3.34 us -> 0.02 us
  starting transfers between devices: 30.9 us -> 27.6 us
  waiting for transfers between devices: 14.8 us -> 16.6 us
    ppermute x1, waiting for transfers between devices: 0.01 us -> 3.57 us  [local(): near_left = lax.ppermute(near_right, 'az', higher_az)]
    ppermute x1, starting transfers between devices: 3.42 us -> 0.01 us  [local(): right = lax.ppermute(far_left, 'az', lower_az)]
    unnamed x28 -> x8, local copies, waits for them, and re-layouts: 3.34 us -> 0.02 us
    ppermute x1, starting transfers between devices: 3.57 us -> 2.16 us  [local(): near_left = lax.ppermute(near_right, 'az', higher_az)]
    all_to_all x1, waiting for transfers between devices: 6.14 us -> 4.79 us  [local(): lax.all_to_all(back.reshape(R_AX, 2, 128), 'az', 0, 0, tiled=True)]
    ppermute x1, starting transfers between devices: 1.95 us -> 3.1 us  [local(): left = lax.ppermute(far_right, 'az', higher_az)]
    ppermute x1, starting transfers between devices: 2.2 us -> 1.3 us  [local(): near_below = lax.ppermute(near_up, 'ax', higher_ax)]
    all_to_all x1, waiting for transfers between devices: 6.68 us -> 5.81 us  [local(): lax.all_to_all(send.reshape(R_AX, 4, 128), 'az', 0, 0, tiled=True)]
  transfers between devices with their start and end apart: 9 -> 9, of which waited for: 4 -> 6; matrix products, arithmetic and copies ran while one was open for 0% -> 0% of each run, Pallas kernels for 13% -> 17%
where the time goes in v4:
time: 57.4 us; the launch traced here: 57 us
  starting transfers between devices  27.6 us (48%)
  waiting for transfers between devices  16.6 us (29%)
  Pallas kernels  12.7 us (22%)
    pallas_call x9, Pallas kernels, call(): pl.pallas_call(kernel, in_specs=specs, out_specs=out_specs, out_shape=lis...  12.7 us
    all_to_all x1, starting transfers between devices, local(): lax.all_to_all(send.reshape(R_AX, 4, 128), 'az', 0, 0, tiled=True)  11.2 us
    all_to_all x1, waiting for transfers between devices, local(): lax.all_to_all(send.reshape(R_AX, 4, 128), 'az', 0, 0, tiled=True)  5.81 us
    all_to_all x1, starting transfers between devices, local(): lax.all_to_all(back.reshape(R_AX, 2, 128), 'az', 0, 0, tiled=True)  5.02 us
    all_to_all x1, waiting for transfers between devices, local(): lax.all_to_all(back.reshape(R_AX, 2, 128), 'az', 0, 0, tiled=True)  4.79 us
    ppermute x1, waiting for transfers between devices, local(): near_left = lax.ppermute(near_right, 'az', higher_az)  3.57 us
    ppermute x1, starting transfers between devices, local(): left = lax.ppermute(far_right, 'az', higher_az)  3.1 us
    ppermute x1, starting transfers between devices, local(): near_left = lax.ppermute(near_right, 'az', higher_az)  2.16 us
  transfers between devices with their start and end apart: 9, of which 6 were waited for; matrix products, arithmetic and copies ran while one was open for 0% of the time, Pallas kernels for 17%

profile of v4, /device:TPU:1, one launch (start us, length us, event | category | flops | bytes accessed | tf_op | source)
XLA Modules:
  0.0 57.0 jit_solution(219793107028762403)
XLA Ops:
  0.0 1.2 %shard_map.145 = (f32[256,128]{1,0:T(8,128)S(1)}, f32[256,128]{1,0:T(8,128)S(1)}, f32[256,128]{1,0:T(8,128)S(1)}, f32[256,128]{1,0:T(8,128)S(1)}, f32[192,128]{1...) custom-call(f32[256,512]{1,0:T(8,128)} %bitcast.16, f32[256,512]{1,0:T(8,128)} %bitcast.19, ...), custom_call_target="tpu_custom_call" | custom-call | flops 1000000 | bytes 3000000 | tf_op jit(solution)/shard_map/pallas_call | solution.py:440
  1.2 3.1 %collective-permute-start.2 = (f32[56,512]{1,0:T(8,128)S(1)}, f32[56,512]{1,0:T(8,128)S(1)}, u32[]{:S(2)}, u32[]{:S(2)}) collective-permute-start(f32[56,512]{1,0:T(8,128)S(1)} %get-tuple-element.32), channel_id=1, source_target_pairs={{0,1},{1,2},{2,3},{3,4},{4,5},{5,6},{6,7},{7,8},{8,9},{9,10},{10,1... | collective-permute-start | bytes 344072 | tf_op jit(solution)/shard_map/ppermute | solution.py:477
  4.3 1.3 %collective-permute-start = (f32[192,128]{1,0:T(8,128)S(1)}, f32[192,128]{1,0:T(8,128)S(1)}, u32[]{:S(2)}, u32[]{:S(2)}) collective-permute-start(f32[192,128]{1,0:T(8,128)S(1)} %get-tuple-element.30), channel_id=1, source_target_pairs={{0,64},{64,128},{128,192},{192,0},{1,65},{65,129},{129,193},{193,1... | collective-permute-start | bytes 294920 | tf_op jit(solution)/shard_map/ppermute | solution.py:475
  5.6 0.0 collective-permute-start.3
  5.6 2.0 %collective-permute-start.1 = (f32[160,128]{1,0:T(8,128)S(1)}, f32[160,128]{1,0:T(8,128)S(1)}, u32[]{:S(2)}, u32[]{:S(2)}) collective-permute-start(f32[160,128]{1,0:T(8,128)S(1)} %get-tuple-element.31), channel_id=1, source_target_pairs={{64,0},{128,64},{192,128},{0,192},{65,1},{129,65},{193,129},{1,193... | collective-permute-start | bytes 245768 | tf_op jit(solution)/shard_map/ppermute | solution.py:476
  7.6 1.6 %collective-permute-done.1.refs_5_ = f32[160,128]{1,0:T(8,128)S(1)} collective-permute-done((f32[160,128]{1,0:T(8,128)S(1)}, f32[160,128]{1,0:T(8,128)S(1)}, u32[]{:S(2)}, u32[]{:S(2)}) %collective-permute-start.1) | collective-permute-done | bytes 81952 | tf_op jit(solution)/shard_map/ppermute | solution.py:476
  9.2 0.5 collective-permute-done.refs_4_
  9.8 0.2 collective-permute-done.3.refs_7_.refs_5_.refs_9_
  10.0 0.0 copy-start.3
  10.0 2.2 %collective-permute-start.4 = (f32[168,128]{1,0:T(8,128)S(1)}, f32[168,128]{1,0:T(8,128)S(1)}, u32[]{:S(2)}, u32[]{:S(2)}) collective-permute-start(f32[168,128]{1,0:T(8,128)S(1)} %shard_map.146), channel_id=1, source_target_pairs={{0,1},{1,2},{2,3},{3,4},{4,5},{5,6},{6,7},{7,8},{8,9},{9,10},{10,1... | collective-permute-start | bytes 258056 | tf_op jit(solution)/shard_map/ppermute | solution.py:493
  12.2 1.3 %shard_map.147 = (f32[128,128]{1,0:T(8,128)S(1)}, f32[16,256]{1,0:T(8,128)S(1)}, bf16[80,64]{1,0:T(8,128)(2,1)S(1)}, bf16[80,64]{1,0:T(8,128)(2,1)S(1)}, bf16[25...) custom-call(s32[32,128]{1,0:T(8,128)S(1)} %copy-done, ...), custom_call_target="tpu_custom_call" | custom-call | flops 1000000 | bytes 3000000 | tf_op jit(solution)/shard_map/pallas_call | solution.py:440
  13.5 3.6 %collective-permute-done.4.refs_6_ = f32[168,128]{1,0:T(8,128)S(1)} collective-permute-done((f32[168,128]{1,0:T(8,128)S(1)}, f32[168,128]{1,0:T(8,128)S(1)}, u32[]{:S(2)}, u32[]{:S(2)}) %collective-permute-start.4) | collective-permute-done | bytes 86048 | tf_op jit(solution)/shard_map/ppermute | solution.py:493
  17.1 1.1 %shard_map.148 = f32[256,128]{1,0:T(8,128)} custom-call(f32[256,128]{1,0:T(8,128)S(1)} %get-tuple-element.26.refs_0_, f32[256,128]{1,0:T(8,128)S(1)} %get-tuple-element.27.refs_1_, f32[256,128]{1,0:T(8,128)S(1)} %get-tuple-element.28.refs_2_, f32[256,128]{1,0:T(8,128)S(1)} %get-tuple-element.29.refs_3_, f32[192,128]{1,0:T(8,128)S(1)} %collective-permute-done.refs_4_, ...), custom_call_target="tpu_custom_call" | custom-call | flops 1000000 | bytes 3000000 | tf_op jit(solution)/shard_map/pallas_call | solution.py:440
  18.2 11.2 %all-to-all-start = ((f32[64,4,128]{2,1,0:T(4,128)}), f32[64,4,128]{2,1,0:T(4,128)S(1)}, u32[]{:S(2)}, u32[]{:S(2)}) async-start(f32[64,4,128]{2,1,0:T(4,128)} %bitcast.28), calls=%async_computation | async-start | bytes 262144 | tf_op jit(solution)/shard_map/all_to_all | solution.py:500
  29.4 1.7 %shard_map.151 = (f32[664,128]{1,0:T(8,128)S(1)}, f32[552,128]{1,0:T(8,128)S(1)}) custom-call(f32[256,512]{1,0:T(8,128)} %bitcast.17, f32[256,512]{1,0:T(8,128)} %bitcast.20, f32[256,512]{1,0:T(8,128)} %bitcast.23, f32[256,512]{1,0:T(8,128)} %bitcast.26, f32[56,512]{1,0:T(8,128)S(1)} %collective-permute-done.2.refs_6_.refs_4_.refs_8_, ...), custom_call_target="tpu_custom_call" | custom-call | flops 1000000 | bytes 3000000 | tf_op jit(solution)/shard_map/pallas_call | solution.py:440
  31.1 1.4 %collective-permute-start.5 = (f32[664,128]{1,0:T(8,128)S(1)}, f32[664,128]{1,0:T(8,128)S(1)}, u32[]{:S(2)}, u32[]{:S(2)}) collective-permute-start(f32[664,128]{1,0:T(8,128)S(1)} %get-tuple-element.43), channel_id=1, source_target_pairs={{0,64},{64,128},{128,192},{192,0},{1,65},{65,129},{129,193},{193,1... | collective-permute-start | bytes 1019912 | tf_op jit(solution)/shard_map/ppermute | solution.py:508
  32.5 1.4 %collective-permute-start.6 = (f32[552,128]{1,0:T(8,128)S(1)}, f32[552,128]{1,0:T(8,128)S(1)}, u32[]{:S(2)}, u32[]{:S(2)}) collective-permute-start(f32[552,128]{1,0:T(8,128)S(1)} %get-tuple-element.44), channel_id=1, source_target_pairs={{64,0},{128,64},{192,128},{0,192},{65,1},{129,65},{193,129},{1,193... | collective-permute-start | bytes 847880 | tf_op jit(solution)/shard_map/ppermute | solution.py:509
  33.9 5.8 %all-to-all-done = f32[64,4,128]{2,1,0:T(4,128)S(1)} async-done(((f32[64,4,128]{2,1,0:T(4,128)}), f32[64,4,128]{2,1,0:T(4,128)S(1)}, u32[]{:S(2)}, u32[]{:S(2)}) %all-to-all-start) | async-done | bytes 131104 | tf_op jit(solution)/shard_map/all_to_all | solution.py:500
  39.8 1.6 %shard_map.149 = f32[128,128]{1,0:T(8,128)} custom-call(f32[256,128]{1,0:T(8,128)S(1)} %bitcast.11, bf16[80,64]{1,0:T(8,128)(2,1)S(1)} %get-tuple-element.35.first_h, bf16[80,64]{1,0:T(8,128)(2,1)S(1)} %get-tuple-element.36.first_l, bf16[256,512]{1,0:T(8,128)(2,1)S(1)} %get-tuple-element.37.block_h, bf16[256,512]{1,0:T(8,128)(2,1)S(1)} %get-tuple-element.38.block_l, ...), custom_call_target="tpu_custom_call" | custom-call | flops 1000000 | bytes 3000000 | tf_op jit(solution)/shard_map/pallas_call | solution.py:440
  41.4 5.0 %all-to-all-start.1 = ((f32[64,2,128]{2,1,0:T(2,128)}), f32[64,2,128]{2,1,0:T(2,128)S(1)}, u32[]{:S(2)}, u32[]{:S(2)}) async-start(f32[64,2,128]{2,1,0:T(2,128)} %bitcast.29), calls=%async_computation.1 | async-start | bytes 131072 | tf_op jit(solution)/shard_map/all_to_all | solution.py:522
  46.5 4.6 %shard_map.152 = (f32[256,512]{1,0:T(8,128)}, f32[256,128]{1,0:T(8,128)S(1)}) custom-call(f32[256,512]{1,0:T(8,128)} %bitcast.18, f32[256,512]{1,0:T(8,128)} %bitcast.21, f32[256,512]{1,0:T(8,128)} %bitcast.24, f32[256,512]{1,0:T(8,128)} %bitcast.27, f32[192,128]{1,0:T(8,128)S(1)} %collective-permute-done.refs_4_, ...), custom_call_target="tpu_custom_call" | custom-call | flops 4000000 | bytes 12000000 | tf_op jit(solution)/shard_map/pallas_call | solution.py:440
  51.1 0.4 shard_map.150.delta
  51.4 4.8 %all-to-all-done.1 = f32[64,2,128]{2,1,0:T(2,128)S(1)} async-done(((f32[64,2,128]{2,1,0:T(2,128)}), f32[64,2,128]{2,1,0:T(2,128)S(1)}, u32[]{:S(2)}, u32[]{:S(2)}) %all-to-all-start.1) | async-done | bytes 65568 | tf_op jit(solution)/shard_map/all_to_all | solution.py:522
  56.2 0.8 %shard_map.153 = f32[256,512]{1,0:T(8,128)} custom-call(f32[128,128]{1,0:T(8,128)S(1)} %bitcast.13, f32[16,256]{1,0:T(8,128)S(1)} %shard_map.150.delta, f32[256,128]{1,0:T(8,128)S(1)} %get-tuple-element.45.swept, f32[256,512]{1,0:T(8,128)} %get-tuple-element.46._), custom_call_target="tpu_custom_call", output_to_operand_aliasing={{}: (3, {})} | custom-call | flops 1000000 | bytes 3000000 | tf_op jit(solution)/shard_map/pallas_call | solution.py:440
  (11 shorter events, 0.0 us)
Async XLA Ops:
  1.2 8.7 %collective-permute-start.2 = (f32[56,512]{1,0:T(8,128)S(1)}, f32[56,512]{1,0:T(8,128)S(1)}, u32[]{:S(2)}, u32[]{:S(2)}) collective-permute-start(f32[56,512]{1,0:T(8,128)S(1)} %get-tuple-element.32), channel_id=1, source_target_pairs={{0,1},{1,2},{2,3},{3,4},{4,5},{5,6},{6,7},{7,8},{8,9},{9,10},{10,1... | collective-permute-start | bytes 344072 | tf_op jit(solution)/shard_map/ppermute | solution.py:477
  4.3 5.4 %collective-permute-start = (f32[192,128]{1,0:T(8,128)S(1)}, f32[192,128]{1,0:T(8,128)S(1)}, u32[]{:S(2)}, u32[]{:S(2)}) collective-permute-start(f32[192,128]{1,0:T(8,128)S(1)} %get-tuple-element.30), channel_id=1, source_target_pairs={{0,64},{64,128},{128,192},{192,0},{1,65},{65,129},{129,193},{193,1... | collective-permute-start | bytes 294920 | tf_op jit(solution)/shard_map/ppermute | solution.py:475
  5.6 4.3 %collective-permute-start.3 = (f32[48,512]{1,0:T(8,128)S(1)}, f32[48,512]{1,0:T(8,128)S(1)}, u32[]{:S(2)}, u32[]{:S(2)}) collective-permute-start(f32[48,512]{1,0:T(8,128)S(1)} %get-tuple-element.33), channel_id=1, source_target_pairs={{1,0},{2,1},{3,2},{4,3},{5,4},{6,5},{7,6},{8,7},{9,8},{10,9},{11,1... | collective-permute-start | bytes 294920 | tf_op jit(solution)/shard_map/ppermute | solution.py:478
  5.6 3.6 %collective-permute-start.1 = (f32[160,128]{1,0:T(8,128)S(1)}, f32[160,128]{1,0:T(8,128)S(1)}, u32[]{:S(2)}, u32[]{:S(2)}) collective-permute-start(f32[160,128]{1,0:T(8,128)S(1)} %get-tuple-element.31), channel_id=1, source_target_pairs={{64,0},{128,64},{192,128},{0,192},{65,1},{129,65},{193,129},{1,193... | collective-permute-start | bytes 245768 | tf_op jit(solution)/shard_map/ppermute | solution.py:476
  10.0 2.2 %copy-start = (s32[32,128]{1,0:T(8,128)S(1)}, s32[32,128]{1,0:T(8,128)}, u32[]{:S(2)}) copy-start(s32[32,128]{1,0:T(8,128)} %refs_0_.1) | copy-start | bytes 49156
  10.0 2.2 %copy-start.1 = (f32[32,128]{1,0:T(8,128)S(1)}, f32[32,128]{1,0:T(8,128)}, u32[]{:S(2)}) copy-start(f32[32,128]{1,0:T(8,128)} %refs_1_.1) | copy-start | bytes 49156
  10.0 2.2 %copy-start.2 = (s32[32,8]{0,1:T(8,128)S(1)}, s32[32,8]{0,1:T(8,128)}, u32[]{:S(2)}) copy-start(s32[32,8]{0,1:T(8,128)} %param.21) | copy-start | bytes 3076
  10.0 2.2 %copy-start.3 = (s32[32,8]{0,1:T(8,128)S(1)}, s32[32,8]{0,1:T(8,128)}, u32[]{:S(2)}) copy-start(s32[32,8]{0,1:T(8,128)} %param.22) | copy-start | bytes 3076
  10.0 7.1 %collective-permute-start.4 = (f32[168,128]{1,0:T(8,128)S(1)}, f32[168,128]{1,0:T(8,128)S(1)}, u32[]{:S(2)}, u32[]{:S(2)}) collective-permute-start(f32[168,128]{1,0:T(8,128)S(1)} %shard_map.146), channel_id=1, source_target_pairs={{0,1},{1,2},{2,3},{3,4},{4,5},{5,6},{6,7},{7,8},{8,9},{9,10},{10,1... | collective-permute-start | bytes 258056 | tf_op jit(solution)/shard_map/ppermute | solution.py:493
  18.2 21.6 %all-to-all-start = ((f32[64,4,128]{2,1,0:T(4,128)}), f32[64,4,128]{2,1,0:T(4,128)S(1)}, u32[]{:S(2)}, u32[]{:S(2)}) async-start(f32[64,4,128]{2,1,0:T(4,128)} %bitcast.28), calls=%async_computation | async-start | bytes 262144 | tf_op jit(solution)/shard_map/all_to_all | solution.py:500
  31.1 15.3 %collective-permute-start.5 = (f32[664,128]{1,0:T(8,128)S(1)}, f32[664,128]{1,0:T(8,128)S(1)}, u32[]{:S(2)}, u32[]{:S(2)}) collective-permute-start(f32[664,128]{1,0:T(8,128)S(1)} %get-tuple-element.43), channel_id=1, source_target_pairs={{0,64},{64,128},{128,192},{192,0},{1,65},{65,129},{129,193},{193,1... | collective-permute-start | bytes 1019912 | tf_op jit(solution)/shard_map/ppermute | solution.py:508
  32.5 13.9 %collective-permute-start.6 = (f32[552,128]{1,0:T(8,128)S(1)}, f32[552,128]{1,0:T(8,128)S(1)}, u32[]{:S(2)}, u32[]{:S(2)}) collective-permute-start(f32[552,128]{1,0:T(8,128)S(1)} %get-tuple-element.44), channel_id=1, source_target_pairs={{64,0},{128,64},{192,128},{0,192},{65,1},{129,65},{193,129},{1,193... | collective-permute-start | bytes 847880 | tf_op jit(solution)/shard_map/ppermute | solution.py:509
  41.4 14.8 %all-to-all-start.1 = ((f32[64,2,128]{2,1,0:T(2,128)}), f32[64,2,128]{2,1,0:T(2,128)S(1)}, u32[]{:S(2)}, u32[]{:S(2)}) async-start(f32[64,2,128]{2,1,0:T(2,128)} %bitcast.29), calls=%async_computation.1 | async-start | bytes 131072 | tf_op jit(solution)/shard_map/all_to_all | solution.py:522

commit v5 on v4

--- a/solution.py
+++ b/solution.py
@@ -26,36 +26,36 @@
 ABOVE = ((0, 8), (0, 9), (1, 8), (2, 8), (3, 8))
 HALO_PLANES = ((-2, -1, 8, 9), (-2, -1, 8), (-1, 8), (-1, 8))
 
-NEAR_LEFT = tuple((f, c) for f in range(3) for c in range(-4, 0)) + tuple((3, c) for c in range(-3, 0))
-NEAR_CORNERS = tuple((f, c, p) for f, c in NEAR_LEFT for p in HALO_PLANES[f])
-NEAR_ROWS = 8 * len(NEAR_LEFT) + 48
-LEFT = ((0, -2), (0, -1), (1, -2), (1, -1), (2, -2), (2, -1), (3, -1))
-RIGHT = ((0, 32), (0, 33), (1, 32), (1, 33), (2, 32), (3, 32))
+LOWEST = -4
+LEFT = tuple((f, c) for f in range(3) for c in range(-4, 0)) + tuple((3, c) for c in range(-3, 0))
+LEFT_COUNT = (4, 4, 4, 3)
 TILES = NR // 128
-
-
-def far_layout(planes):
+KEPT = ROWS - 16
+
+
+def halo_layout(planes, tiles):
     entries, row = [], 0
-    for tile in range(TILES):
+    for tile in tiles:
         for field, plane in planes:
-            left = sum(f == field for f, _ in LEFT)
-            right = sum(f == field for f, _ in RIGHT)
-            if tile:
-                runs = ((-left, left + COLS + right),)
-            else:
-                runs = ((-left, left), (COLS, right))
-            for column, count in runs:
-                entries.append((tile, field, plane, column, count, row))
-                row += count
+            entries.append((tile, field, plane, LEFT_COUNT[field], row))
+            row += LEFT_COUNT[field] + COLS
     return entries, -(-row // 8) * 8
 
 
-FAR_BELOW, FAR_BELOW_ROWS = far_layout(BELOW)
-FAR_ABOVE, FAR_ABOVE_ROWS = far_layout(ABOVE)
+NEAR_BELOW, NEAR_BELOW_ROWS = halo_layout(BELOW, (0,))
+NEAR_ABOVE, NEAR_ABOVE_ROWS = halo_layout(ABOVE, (0,))
+FAR_BELOW, FAR_BELOW_ROWS = halo_layout(BELOW, range(1, TILES))
+FAR_ABOVE, FAR_ABOVE_ROWS = halo_layout(ABOVE, range(1, TILES))
 
 
 def plane_slot(plane):
     return plane % 16 - 8
+
+
+def copy_out(source, target, semaphore):
+    copy = pltpu.make_async_copy(source, target, semaphore)
+    copy.start()
+    copy.wait()
 
 
 def copy_all(pairs, semaphores, first=0):
@@ -65,73 +65,58 @@
     return copies
 
 
-def copy_out(source, target, semaphore):
-    copy = pltpu.make_async_copy(source, target, semaphore)
-    copy.start()
-    copy.wait()
-
-
-def pack_first(*refs):
-    fields, tiles, (up, down, right, left, semaphores) = refs[:4], refs[4:8], refs[8:]
-    copies = copy_all([(f.at[:, pl.ds(0, 128)], tile) for f, tile in zip(fields, tiles)], semaphores)
-    pairs = []
-    for columns, out, shift in ((LEFT, right, COLS), (RIGHT, left, -COLS)):
-        for field in range(4):
-            at = [k for k, (f, _) in enumerate(columns) if f == field]
-            source = fields[field].at[pl.ds((columns[at[0]][1] + shift) * 8, len(at) * 8), :]
-            pairs.append((source, out.at[pl.ds(at[0] * 8, len(at) * 8), :]))
-    far_copies = copy_all(pairs, semaphores, 4)
-    for field, copy in enumerate(copies):
+def pack_columns(*refs):
+    fields, (right, semaphores) = refs[:4], refs[4:]
+    pairs, row = [], 0
+    for field, count in zip(fields, LEFT_COUNT):
+        pairs.append((field.at[pl.ds(ROWS - count * 8, count * 8), :], right.at[pl.ds(row, count * 8), :]))
+        row += count * 8
+    for copy in copy_all(pairs, semaphores):
         copy.wait()
-        for planes, out, shift in ((BELOW, up, PLANES), (ABOVE, down, -PLANES)):
-            for k, (of, plane) in enumerate(planes):
-                if of == field:
-                    out[k * COLS : (k + 1) * COLS, :] = tiles[field][pl.ds(plane + shift, COLS, stride=PLANES), :]
-    for copy in far_copies:
-        copy.wait()
-
-
-def pack_near_columns(*refs):
-    tiles, (below, above, _, _, right) = refs[:4], refs[4:]
-    for k, (field, column) in enumerate(NEAR_LEFT):
-        right[k * 8 : k * 8 + 8, :] = tiles[field][(column + COLS) * 8 : (column + COLS + 1) * 8, :]
-    right[len(NEAR_LEFT) * 8 :, :] = jnp.zeros((48, 128), F32)
-    for k, (field, column, plane) in enumerate(NEAR_CORNERS):
-        planes, source = (BELOW, below) if plane < 0 else (ABOVE, above)
-        row = planes.index((field, plane)) * COLS + column + COLS
-        at = len(NEAR_LEFT) * 8 + k
-        right[at : at + 1, :] = source[row : row + 1, :]
+
+
+def pack_planes(entries, out, shift, load, left):
+    for tile, field, plane, count, row in entries:
+        for at in range(count):
+            origin = LEFT.index((field, at - count)) * 8 + plane + shift
+            out[row + at : row + at + 1, :] = left[origin : origin + 1, pl.ds(tile * 128, 128)]
+        out[row + count : row + count + COLS, :] = load(tile, field, plane + shift)
+    used = entries[-1][4] + entries[-1][3] + COLS
+    if used < out.shape[0]:
+        out[used:, :] = jnp.zeros((out.shape[0] - used, 128), F32)
+
+
+def pack_near_planes(*refs):
+    tiles, (left, up, down) = refs[:4], refs[4:]
+
+    def load(_, field, plane):
+        return tiles[field][pl.ds(plane, COLS, stride=PLANES), :]
+
+    pack_planes(NEAR_BELOW, up, PLANES, load, left)
+    pack_planes(NEAR_ABOVE, down, -PLANES, load, left)
 
 
 def pack_far_planes(*refs):
-    fields, (left, right, up, down, *tiles, semaphores) = refs[:4], refs[4:]
+    fields, (left, up, down, *tiles, semaphores) = refs[:4], refs[4:]
     pairs = []
     for field, tile in zip(fields, tiles):
         for k in range(1, TILES):
             pairs.append((field.at[:, pl.ds(k * 128, 128)], tile.at[pl.ds((k - 1) * ROWS, ROWS), :]))
     for copy in copy_all(pairs, semaphores):
         copy.wait()
-    for entries, out, shift in ((FAR_BELOW, up, PLANES), (FAR_ABOVE, down, -PLANES)):
-        for tile, field, plane, column, count, row in entries:
-            lanes = pl.ds(tile * 128, 128)
-            for at in range(count):
-                for columns, source in ((LEFT, left), (RIGHT, right)):
-                    if (field, column + at) in columns:
-                        origin = columns.index((field, column + at)) * 8 + plane + shift
-                        out[row + at : row + at + 1, :] = source[origin : origin + 1, lanes]
-            if tile:
-                rows = pl.ds((tile - 1) * ROWS + plane + shift, COLS, stride=PLANES)
-                out[row - column : row - column + COLS, :] = tiles[field][rows, :]
-        used = sum(e[4] for e in entries)
-        if used < out.shape[0]:
-            out[used:, :] = jnp.zeros((out.shape[0] - used, 128), F32)
+
+    def load(tile, field, plane):
+        return tiles[field][pl.ds((tile - 1) * ROWS + plane, COLS, stride=PLANES), :]
+
+    pack_planes(FAR_BELOW, up, PLANES, load, left)
+    pack_planes(FAR_ABOVE, down, -PLANES, load, left)
 
 
 def upwind(courant, below_cell, above_cell):
     return courant * jnp.where(courant > 0.0, below_cell, above_cell)
 
 
-def sweep(lowest, load_own, load_halo, store, lanes, unrolled):
+def sweep(count, load_own, load_halo, store, lanes, unrolled):
     plane = lax.broadcasted_iota(jnp.int32, (8, lanes), 0)
     cycle = lax.broadcasted_iota(jnp.int32, (8, lanes), 1)
     first, last = plane == 0, plane == 7
@@ -193,42 +178,48 @@
 
     state = (None, None, None, None)
     for stage in range(6):
-        state = step(lowest + stage, state, stage)
-    if unrolled:
-        for stage in range(6, 34):
-            state = step(lowest + stage, state, stage)
-    else:
-        state = lax.fori_loop(lowest + 6, lowest + 34, lambda column, s: step(column, s, 6), state, unroll=4)
-    for stage in (34, 35):
-        state = step(lowest + stage, state, stage)
+        state = step(LOWEST + stage, state, stage)
+    stage = 6
+    if not unrolled:
+        state = lax.fori_loop(LOWEST + 6, LOWEST + 34, lambda column, s: step(column, s, 6), state, unroll=4)
+        stage = 34
+    for stage in range(stage, count):
+        state = step(LOWEST + stage, state, stage)
+
+
+def fill_halos(halos, entries, source):
+    for tile, field, plane, count, row in entries:
+        rows = pl.ds((-count - LOWEST) * 8 + plane_slot(plane), count + COLS, stride=8)
+        halos[field].at[tile][rows, :] = source[row : row + count + COLS, :]
+
+
+def row_slice(column):
+    return pl.ds(column * 8 if isinstance(column, int) else pl.multiple_of(column * 8, 8), 8)
+
+
+def loaders(fields, left, halos, tiles):
+    def load_own(field, column):
+        if isinstance(column, int) and column < 0:
+            return left[row_slice(LEFT.index((field, column))), pl.ds(0, tiles * 128)]
+        return fields[field][row_slice(column), :]
+
+    def load_halo(field, column):
+        parts = [halos[field].at[tile][row_slice(column - LOWEST), :] for tile in range(tiles)]
+        return jnp.concatenate(parts, axis=1) if tiles > 1 else parts[0]
+
+    return load_own, load_halo
 
 
 def near_kernel(*refs):
     fields, (below, above, left, crossing, send) = refs[:4], refs[4:9]
     halos, (swept, out, semaphore) = refs[9:13], refs[13:]
-    lowest = -4
-    for planes, source in ((BELOW, below), (ABOVE, above)):
-        for k, (field, plane) in enumerate(planes):
-            rows = pl.ds(-lowest * 8 + plane_slot(plane), COLS, stride=8)
-            halos[field][rows, :] = source[k * COLS : (k + 1) * COLS, :]
-    for k, (field, column, plane) in enumerate(NEAR_CORNERS):
-        at = (column - lowest) * 8 + plane_slot(plane)
-        row = len(NEAR_LEFT) * 8 + k
-        halos[field][at : at + 1, :] = left[row : row + 1, :]
-
-    def load_own(field, column):
-        if column < 0:
-            at = NEAR_LEFT.index((field, column)) * 8
-            return left[at : at + 8, :]
-        return fields[field][column * 8 : column * 8 + 8, :]
-
-    def load_halo(field, column):
-        return halos[field][(column - lowest) * 8 : (column - lowest + 1) * 8, :]
+    fill_halos(halos, NEAR_BELOW, below)
+    fill_halos(halos, NEAR_ABOVE, above)
 
     def store(column, values):
-        swept[(column + 2) * 8 : (column + 3) * 8, :] = values
-
-    sweep(lowest, load_own, load_halo, store, 128, True)
+        swept[row_slice(column + 2), :] = values
+
+    sweep(COLS + 4, *loaders(fields, left, halos, 1), store, 128, True)
     turned = swept[...].T
     out[pl.ds(0, R_AX, stride=4), :] = turned[:R_AX, :128]
     out[pl.ds(1, R_AX, stride=4), :] = turned[:R_AX, 128:]
@@ -237,40 +228,40 @@
     copy_out(out, send, semaphore)
 
 
-def far_kernel(*refs):
-    sources, (near_below, near_above, below, above, left, right) = refs[:4], refs[4:10]
-    (result, first_tile), halos, fields, (out, semaphores) = refs[10:12], refs[12:16], refs[16:20], refs[20:]
-    copies = copy_all(zip(sources, fields), semaphores)
-    lowest = -2
-    for planes, near, entries, far in ((BELOW, near_below, FAR_BELOW, below), (ABOVE, near_above, FAR_ABOVE, above)):
-        for k, (field, plane) in enumerate(planes):
-            rows = pl.ds(-lowest * 8 + plane_slot(plane), COLS, stride=8)
-            halos[field].at[0][rows, :] = near[k * COLS : (k + 1) * COLS, :]
-        for tile, field, plane, column, count, row in entries:
-            rows = pl.ds((column - lowest) * 8 + plane_slot(plane), count, stride=8)
-            halos[field].at[tile][rows, :] = far[row : row + count, :]
-
-    def load_own(field, column):
-        for columns, source in ((LEFT, left), (RIGHT, right)):
-            if isinstance(column, int) and (field, column) in columns:
-                at = columns.index((field, column)) * 8
-                return source[at : at + 8, :]
-        return fields[field][pl.ds(column * 8 if isinstance(column, int) else pl.multiple_of(column * 8, 8), 8), :]
-
-    def load_halo(field, column):
-        at = (column - lowest) * 8
-        rows = pl.ds(at if isinstance(at, int) else pl.multiple_of(at, 8), 8)
-        return jnp.concatenate([halos[field].at[tile][rows, :] for tile in range(TILES)], axis=1)
-
-    def store(column, values):
-        rows = pl.ds(column * 8 if isinstance(column, int) else pl.multiple_of(column * 8, 8), 8)
-        out[rows, :] = values
-        first_tile[rows, :] = values[:, :128]
-
+def fill_far_halos(halos, near_below, near_above, below, above):
+    for entries, source in ((NEAR_BELOW, near_below), (NEAR_ABOVE, near_above), (FAR_BELOW, below), (FAR_ABOVE, above)):
+        fill_halos(halos, entries, source)
+
+
+def far_first_kernel(*refs):
+    sources, planes, (left, out), halos = refs[:4], refs[4:8], refs[8:10], refs[10:14]
+    fields, semaphores = refs[14:18], refs[18]
+    copies = copy_all([(f.at[pl.ds(0, 16), :], held) for f, held in zip(sources, fields)], semaphores)
+    fill_far_halos(halos, *planes)
     for copy in copies:
         copy.wait()
-    sweep(lowest, load_own, load_halo, store, NR, False)
-    copy_out(out, result, semaphores.at[4])
+
+    def store(column, values):
+        out[row_slice(column + 2), :] = values
+
+    sweep(6, *loaders(fields, left, halos, TILES), store, NR, True)
+
+
+def far_kernel(*refs):
+    sources, planes, (left, result, first_tile), halos = refs[:4], refs[4:8], refs[8:11], refs[11:15]
+    fields, (out, semaphores) = refs[15:19], refs[19:]
+    copies = copy_all(zip(sources, fields), semaphores)
+    fill_far_halos(halos, *planes)
+    for copy in copies:
+        copy.wait()
+
+    def store(column, values):
+        if not isinstance(column, int) or column >= 0:
+            out[row_slice(column), :] = values
+            first_tile[row_slice(column), :] = values[:, :128]
+
+    sweep(COLS + 4, *loaders(fields, left, halos, TILES), store, NR, False)
+    copy_out(out, result.at[pl.ds(0, KEPT), :], semaphores.at[4])
 
 
 def pieces(values, count):
@@ -309,8 +300,9 @@
 
 
 def crossing_kernel(*refs):
-    (code, width, reader, landing), tables, (out, volume_out) = refs[:4], refs[4:11], refs[11:13]
-    copies = copy_all(zip(tables, refs[13:20]), refs[20])
+    (code, width, reader, landing), fields, tables, (out, volume_out) = refs[:4], refs[4:8], refs[8:15], refs[15:17]
+    sources = [f.at[:, pl.ds(0, 128)] for f in fields] + list(tables)
+    copies = copy_all(zip(sources, refs[17:28]), refs[28])
     iota = functools.partial(lax.broadcasted_iota, jnp.int32)
     volume = plic_volume(code[...], width[...])
     both = jnp.concatenate([reader[...].astype(F32), landing[...].astype(F32)], axis=0).astype(BF16)
@@ -416,14 +408,19 @@
     copy_out(out, send, semaphore)
 
 
-def final_kernel(received, delta, swept, _, result, out, semaphore):
+def final_kernel(received, delta, swept, last, _, result, out, semaphores):
+    rest = (pl.ds(KEPT, ROWS - KEPT), pl.ds(128, NR - 128))
+    copy = pltpu.make_async_copy(last.at[:, pl.ds(128, NR - 128)], result.at[rest], semaphores.at[1])
+    copy.start()
     near = jnp.concatenate(
         [received[pl.ds(0, R_AX, stride=2), :], received[pl.ds(1, R_AX, stride=2), :]], axis=1
     )
     near = jnp.concatenate([near[:XR] + delta[...], near[XR:], jnp.zeros((R_AX, ROWS), F32)], axis=0)
     cycle = lax.broadcasted_iota(jnp.int32, (ROWS, 128), 1)
-    out[...] = jnp.where(cycle < R_AX, near.T, swept[...])
-    copy_out(out, result.at[:, pl.ds(0, 128)], semaphore)
+    first_tile = jnp.concatenate([swept[...], last[:, :128]], axis=0)
+    out[...] = jnp.where(cycle < R_AX, near.T, first_tile)
+    copy_out(out, result.at[:, pl.ds(0, 128)], semaphores.at[0])
+    copy.wait()
 
 
 VMEM, HBM = pltpu.VMEM, pltpu.HBM
@@ -464,55 +461,54 @@
     lower_ax, lower_az = ([(j, i) for i, j in pairs] for pairs in (higher_ax, higher_az))
     fields = [(a.reshape(ROWS, NR), HBM) for a in (fraction, courant_axial, courant_azimuth, courant_radial)]
 
-    *near_tiles, near_up, near_down, far_right, far_left = call(
-        pack_first,
-        fields,
-        [VMEM((ROWS, 128), F32)] * 4
-        + [VMEM((len(BELOW) * COLS, 128), F32), VMEM((len(ABOVE) * COLS, 128), F32)]
-        + [VMEM((len(LEFT) * 8, NR), F32), VMEM((len(RIGHT) * 8, NR), F32)],
-        [DMA((12,))],
+    (right,) = call(pack_columns, fields, [VMEM((len(LEFT) * 8, NR), F32)], [DMA((4,))])
+    left = lax.ppermute(right, "az", higher_az)
+
+    tables = filter_tables()
+    crossing, volume, *held = call(
+        crossing_kernel,
+        [plane_code, strip_width, tile_reader.T, landing_column.T, *fields, *((jnp.asarray(t), HBM) for t in tables)],
+        [VMEM((2 * R_AX, 128), F32), VMEM((XR, ROWS), F32)]
+        + [VMEM((ROWS, 128), F32)] * 4
+        + [VMEM(t.shape, t.dtype) for t in tables],
+        [DMA((4 + len(tables),))],
+    )
+    near_tiles, held_tables = held[:4], held[4:]
+
+    near_up, near_down = call(
+        pack_near_planes,
+        [*near_tiles, left],
+        [VMEM((NEAR_BELOW_ROWS, 128), F32), VMEM((NEAR_ABOVE_ROWS, 128), F32)],
     )
     near_below = lax.ppermute(near_up, "ax", higher_ax)
     near_above = lax.ppermute(near_down, "ax", lower_ax)
-    left = lax.ppermute(far_right, "az", higher_az)
-    right = lax.ppermute(far_left, "az", lower_az)
-
-    tables = filter_tables()
-    crossing, volume, *held_tables = call(
-        crossing_kernel,
-        [plane_code, strip_width, tile_reader.T, landing_column.T, *((jnp.asarray(t), HBM) for t in tables)],
-        [VMEM((2 * R_AX, 128), F32), VMEM((XR, ROWS), F32)] + [VMEM(t.shape, t.dtype) for t in tables],
-        [DMA((len(tables),))],
-    )
-
-    (near_right,) = call(
-        pack_near_columns,
-        [*near_tiles, near_below, near_above, (left, pl.ANY), (right, pl.ANY)],
-        [VMEM((NEAR_ROWS, 128), F32)],
-    )
-    near_left = lax.ppermute(near_right, "az", higher_az)
     (send,) = call(
         near_kernel,
-        [*near_tiles, near_below, near_above, near_left, crossing],
+        [*near_tiles, near_below, near_above, left, crossing],
         [HBM((4 * R_AX, 128), F32)],
-        [VMEM((36 * 8, 128), F32)] * 4 + [VMEM((ROWS, 128), F32), VMEM((4 * R_AX, 128), F32), DMA],
+        [VMEM((1, 36 * 8, 128), F32)] * 4 + [VMEM((ROWS, 128), F32), VMEM((4 * R_AX, 128), F32), DMA],
     )
     got = lax.all_to_all(send.reshape(R_AX, 4, 128), "az", 0, 0, tiled=True).reshape(4 * R_AX, 128)
 
     far_up, far_down = call(
         pack_far_planes,
-        [*fields, left, right],
+        [*fields, left],
         [VMEM((FAR_BELOW_ROWS, 128), F32), VMEM((FAR_ABOVE_ROWS, 128), F32)],
         [VMEM(((TILES - 1) * ROWS, 128), F32)] * 4 + [DMA((4 * (TILES - 1),))],
     )
     far_below = lax.ppermute(far_up, "ax", higher_ax)
     far_above = lax.ppermute(far_down, "ax", lower_ax)
-
+    far_inputs = [*fields, near_below, near_above, far_below, far_above, left]
+    far_halos = [VMEM((TILES, 36 * 8, 128), F32)] * 4
+    (first_columns,) = call(
+        far_first_kernel, far_inputs, [VMEM((16, NR), F32)], far_halos + [VMEM((16, NR), F32)] * 4 + [DMA((4,))]
+    )
+    last_columns = lax.ppermute(first_columns, "az", lower_az)
     swept, first_tile = call(
         far_kernel,
-        [*fields, near_below, near_above, far_below, far_above, left, right],
-        [HBM((ROWS, NR), F32), VMEM((ROWS, 128), F32)],
-        [VMEM((TILES, 36 * 8, 128), F32)] * 4 + [VMEM((ROWS, NR), F32)] * 5 + [DMA((5,))],
+        far_inputs,
+        [HBM((ROWS, NR), F32), VMEM((KEPT, 128), F32)],
+        far_halos + [VMEM((ROWS, NR), F32)] * 4 + [VMEM((KEPT, NR), F32), DMA((5,))],
         cost=4.0,
     )
 
@@ -523,10 +519,10 @@
     (delta,) = call(arrival_kernel, [got, volume], [VMEM((XR, ROWS), F32)])
     (out,) = call(
         final_kernel,
-        [returned, delta, first_tile, (swept, HBM)],
+        [returned, delta, first_tile, last_columns, (swept, HBM)],
         [HBM((ROWS, NR), F32)],
-        [VMEM((ROWS, 128), F32), DMA],
-        aliases={3: 0},
+        [VMEM((ROWS, 128), F32), DMA((2,))],
+        aliases={4: 0},
     )
     return out.reshape(COLS, PLANES, NR)
 

time: 57.4 us -> 56.5 us (0.984)
  waiting for transfers between devices: 16.6 us -> 12.8 us
  starting transfers between devices: 27.6 us -> 29 us
  Pallas kernels: 12.7 us -> 14 us
    all_to_all x1, starting transfers between devices: 11.2 us -> 14.6 us  [local(): lax.all_to_all(send.reshape(R_AX, 4, 128), 'az', 0, 0, tiled=True)]
    ppermute x3 -> x2, waiting for transfers between devices: 3.79 us -> 1.42 us  [the longest x1 1.42 us: local(): left = lax.ppermute(right, 'az', higher_az)]
    ppermute x3 -> x2, starting transfers between devices: 5.27 us -> 3.64 us  [the longest x1 3.1 us: local(): left = lax.ppermute(right, 'az', higher_az)]
    all_to_all x1, waiting for transfers between devices: 4.79 us -> 3.16 us  [local(): lax.all_to_all(back.reshape(R_AX, 2, 128), 'az', 0, 0, tiled=True)]
    pallas_call x9 -> x10, Pallas kernels: 12.7 us -> 14 us  [call(): pl.pallas_call(kernel, in_specs=specs, out_specs=out_specs, out_shape=lis...]
  transfers between devices with their start and end apart: 9 -> 8, of which waited for: 6 -> 5; matrix products, arithmetic and copies ran while one was open for 0% -> 0% of each run, Pallas kernels for 17% -> 20%
where the time goes in v5:
time: 56.5 us; the launch traced here: 55.9 us
  starting transfers between devices  29 us (51%)
  Pallas kernels  14 us (25%)
  waiting for transfers between devices  12.8 us (23%)
    all_to_all x1, starting transfers between devices, local(): lax.all_to_all(send.reshape(R_AX, 4, 128), 'az', 0, 0, tiled=True)  14.6 us
    pallas_call x10, Pallas kernels, call(): pl.pallas_call(kernel, in_specs=specs, out_specs=out_specs, out_shape=lis...  14 us
    all_to_all x1, waiting for transfers between devices, local(): lax.all_to_all(send.reshape(R_AX, 4, 128), 'az', 0, 0, tiled=True)  5.88 us
    all_to_all x1, starting transfers between devices, local(): lax.all_to_all(back.reshape(R_AX, 2, 128), 'az', 0, 0, tiled=True)  5.02 us
    all_to_all x1, waiting for transfers between devices, local(): lax.all_to_all(back.reshape(R_AX, 2, 128), 'az', 0, 0, tiled=True)  3.16 us
    ppermute x1, starting transfers between devices, local(): left = lax.ppermute(right, 'az', higher_az)  3.1 us
    ppermute x1, waiting for transfers between devices, local(): near_above = lax.ppermute(near_down, 'ax', lower_ax)  2.19 us
    ppermute x1, starting transfers between devices, local(): near_above = lax.ppermute(near_down, 'ax', lower_ax)  1.53 us
  transfers between devices with their start and end apart: 8, of which 5 were waited for; matrix products, arithmetic and copies ran while one was open for 0% of the time, Pallas kernels for 20%

profile of v5, /device:TPU:1, one launch (start us, length us, event | category | flops | bytes accessed | tf_op | source)
XLA Modules:
  0.0 55.9 jit_solution(12523999402276507165)
XLA Ops:
  0.0 1.0 %shard_map.146 = f32[120,512]{1,0:T(8,128)S(1)} custom-call(f32[256,512]{1,0:T(8,128)} %bitcast.16, f32[256,512]{1,0:T(8,128)} %bitcast.21, f32[256,512]{1,0:T(8,128)} %bitcast.26, f32[256,512]{1,0:T(8,128)} %bitcast.31), custom_call_target="tpu_custom_call" | custom-call | flops 1000000 | bytes 3000000 | tf_op jit(solution)/shard_map/pallas_call | solution.py:437
  1.0 3.1 %collective-permute-start = (f32[120,512]{1,0:T(8,128)S(1)}, f32[120,512]{1,0:T(8,128)S(1)}, u32[]{:S(2)}, u32[]{:S(2)}) collective-permute-start(f32[120,512]{1,0:T(8,128)S(1)} %shard_map.146), channel_id=1, source_target_pairs={{0,1},{1,2},{2,3},{3,4},{4,5},{5,6},{6,7},{7,8},{8,9},{9,10},{10,1... | collective-permute-start | bytes 737288 | tf_op jit(solution)/shard_map/ppermute | solution.py:465
  4.1 1.7 %shard_map.145 = (f32[128,128]{1,0:T(8,128)S(1)}, f32[16,256]{1,0:T(8,128)S(1)}, f32[256,128]{1,0:T(8,128)S(1)}, f32[256,128]{1,0:T(8,128)S(1)}, f32[256,128]{1,...) custom-call(s32[32,128]{1,0:T(8,128)S(1)} %copy-done, ...), custom_call_target="tpu_custom_call" | custom-call | flops 1000000 | bytes 3000000 | tf_op jit(solution)/shard_map/pallas_call | solution.py:437
  5.8 1.4 %collective-permute-done.refs_4_.refs_6_.refs_8_ = f32[120,512]{1,0:T(8,128)S(1)} collective-permute-done((f32[120,512]{1,0:T(8,128)S(1)}, f32[120,512]{1,0:T(8,128)S(1)}, u32[]{:S(2)}, u32[]{:S(2)}) %collective-permute-start) | collective-permute-done | bytes 245792 | tf_op jit(solution)/shard_map/ppermute | solution.py:465
  7.3 0.1 shard_map.147
  7.3 1.4 %collective-permute-start.1 = (f32[216,128]{1,0:T(8,128)S(1)}, f32[216,128]{1,0:T(8,128)S(1)}, u32[]{:S(2)}, u32[]{:S(2)}) collective-permute-start(f32[216,128]{1,0:T(8,128)S(1)} %get-tuple-element.28), channel_id=1, source_target_pairs={{0,64},{64,128},{128,192},{192,0},{1,65},{65,129},{129,193},{193,1... | collective-permute-start | bytes 331784 | tf_op jit(solution)/shard_map/ppermute | solution.py:483
  8.7 1.5 %collective-permute-start.2 = (f32[184,128]{1,0:T(8,128)S(1)}, f32[184,128]{1,0:T(8,128)S(1)}, u32[]{:S(2)}, u32[]{:S(2)}) collective-permute-start(f32[184,128]{1,0:T(8,128)S(1)} %get-tuple-element.29), channel_id=1, source_target_pairs={{64,0},{128,64},{192,128},{0,192},{65,1},{129,65},{193,129},{1,193... | collective-permute-start | bytes 282632 | tf_op jit(solution)/shard_map/ppermute | solution.py:484
  10.2 2.2 %collective-permute-done.2.refs_5_ = f32[184,128]{1,0:T(8,128)S(1)} collective-permute-done((f32[184,128]{1,0:T(8,128)S(1)}, f32[184,128]{1,0:T(8,128)S(1)}, u32[]{:S(2)}, u32[]{:S(2)}) %collective-permute-start.2) | collective-permute-done | bytes 94240 | tf_op jit(solution)/shard_map/ppermute | solution.py:484
  12.4 0.2 collective-permute-done.1.refs_4_
  12.6 1.1 %shard_map.148 = f32[256,128]{1,0:T(8,128)} custom-call(f32[256,128]{1,0:T(8,128)S(1)} %get-tuple-element.24.refs_0_, f32[256,128]{1,0:T(8,128)S(1)} %get-tuple-element.25.refs_1_, f32[256,128]{1,0:T(8,128)S(1)} %get-tuple-element.26.refs_2_, f32[256,128]{1,0:T(8,128)S(1)} %get-tuple-element.27.refs_3_, f32[216,128]{1,0:T(8,128)S(1)} %collective-permute-done.1.refs_4_, ...), custom_call_target="tpu_custom_call" | custom-call | flops 1000000 | bytes 3000000 | tf_op jit(solution)/shard_map/pallas_call | solution.py:437
  13.6 14.6 %all-to-all-start = ((f32[64,4,128]{2,1,0:T(4,128)}), f32[64,4,128]{2,1,0:T(4,128)S(1)}, u32[]{:S(2)}, u32[]{:S(2)}) async-start(f32[64,4,128]{2,1,0:T(4,128)} %bitcast.36), calls=%async_computation | async-start | bytes 262144 | tf_op jit(solution)/shard_map/all_to_all | solution.py:491
  28.3 1.7 %shard_map.151 = (f32[648,128]{1,0:T(8,128)S(1)}, f32[544,128]{1,0:T(8,128)S(1)}) custom-call(f32[256,512]{1,0:T(8,128)} %bitcast.18, f32[256,512]{1,0:T(8,128)} %bitcast.23, f32[256,512]{1,0:T(8,128)} %bitcast.28, f32[256,512]{1,0:T(8,128)} %bitcast.33, f32[120,512]{1,0:T(8,128)S(1)} %collective-permute-done.refs_4_.refs_6_.refs_8_), custom_call_target="tpu_custom_call" | custom-call | flops 1000000 | bytes 3000000 | tf_op jit(solution)/shard_map/pallas_call | solution.py:437
  30.0 1.4 %collective-permute-start.3 = (f32[648,128]{1,0:T(8,128)S(1)}, f32[648,128]{1,0:T(8,128)S(1)}, u32[]{:S(2)}, u32[]{:S(2)}) collective-permute-start(f32[648,128]{1,0:T(8,128)S(1)} %get-tuple-element.39), channel_id=1, source_target_pairs={{0,64},{64,128},{128,192},{192,0},{1,65},{65,129},{129,193},{193,1... | collective-permute-start | bytes 995336 | tf_op jit(solution)/shard_map/ppermute | solution.py:499
  31.4 1.4 %collective-permute-start.4 = (f32[544,128]{1,0:T(8,128)S(1)}, f32[544,128]{1,0:T(8,128)S(1)}, u32[]{:S(2)}, u32[]{:S(2)}) collective-permute-start(f32[544,128]{1,0:T(8,128)S(1)} %get-tuple-element.40), channel_id=1, source_target_pairs={{64,0},{128,64},{192,128},{0,192},{65,1},{129,65},{193,129},{1,193... | collective-permute-start | bytes 835592 | tf_op jit(solution)/shard_map/ppermute | solution.py:500
  32.8 5.9 %all-to-all-done = f32[64,4,128]{2,1,0:T(4,128)S(1)} async-done(((f32[64,4,128]{2,1,0:T(4,128)}), f32[64,4,128]{2,1,0:T(4,128)S(1)}, u32[]{:S(2)}, u32[]{:S(2)}) %all-to-all-start) | async-done | bytes 131104 | tf_op jit(solution)/shard_map/all_to_all | solution.py:491
  38.7 1.6 %shard_map.149 = f32[128,128]{1,0:T(8,128)} custom-call(f32[256,128]{1,0:T(8,128)S(1)} %bitcast.11, bf16[80,64]{1,0:T(8,128)(2,1)S(1)} %get-tuple-element.31.first_h, bf16[80,64]{1,0:T(8,128)(2,1)S(1)} %get-tuple-element.32.first_l, bf16[256,512]{1,0:T(8,128)(2,1)S(1)} %get-tuple-element.33.block_h, bf16[256,512]{1,0:T(8,128)(2,1)S(1)} %get-tuple-element.34.block_l, ...), custom_call_target="tpu_custom_call" | custom-call | flops 1000000 | bytes 3000000 | tf_op jit(solution)/shard_map/pallas_call | solution.py:437
  40.3 5.0 %all-to-all-start.1 = ((f32[64,2,128]{2,1,0:T(2,128)}), f32[64,2,128]{2,1,0:T(2,128)S(1)}, u32[]{:S(2)}, u32[]{:S(2)}) async-start(f32[64,2,128]{2,1,0:T(2,128)} %bitcast.37), calls=%async_computation.1 | async-start | bytes 131072 | tf_op jit(solution)/shard_map/all_to_all | solution.py:518
  45.3 0.0 collective-permute-done.3.refs_6_
  45.3 1.1 %shard_map.153 = f32[16,512]{1,0:T(8,128)S(1)} custom-call(f32[256,512]{1,0:T(8,128)} %bitcast.19, f32[256,512]{1,0:T(8,128)} %bitcast.24, f32[256,512]{1,0:T(8,128)} %bitcast.29, f32[256,512]{1,0:T(8,128)} %bitcast.34, f32[216,128]{1,0:T(8,128)S(1)} %collective-permute-done.1.refs_4_, f32[184,128]{1,0:T(8,128)S(1)} %collective-permute-done.2.refs_5_, ...), custom_call_target="tpu_custom_call" | custom-call | flops 1000000 | bytes 3000000 | tf_op jit(solution)/shard_map/pallas_call | solution.py:437
  46.5 0.5 collective-permute-start.5
  47.0 4.6 %shard_map.152 = (f32[256,512]{1,0:T(8,128)}, f32[240,128]{1,0:T(8,128)S(1)}) custom-call(f32[256,512]{1,0:T(8,128)} %bitcast.20, f32[256,512]{1,0:T(8,128)} %bitcast.25, f32[256,512]{1,0:T(8,128)} %bitcast.30, f32[256,512]{1,0:T(8,128)} %bitcast.35, f32[216,128]{1,0:T(8,128)S(1)} %collective-permute-done.1.refs_4_, ...), custom_call_target="tpu_custom_call" | custom-call | flops 4000000 | bytes 12000000 | tf_op jit(solution)/shard_map/pallas_call | solution.py:437
  51.6 0.4 shard_map.150.delta
  52.0 3.2 %all-to-all-done.1 = f32[64,2,128]{2,1,0:T(2,128)S(1)} async-done(((f32[64,2,128]{2,1,0:T(2,128)}), f32[64,2,128]{2,1,0:T(2,128)S(1)}, u32[]{:S(2)}, u32[]{:S(2)}) %all-to-all-start.1) | async-done | bytes 65568 | tf_op jit(solution)/shard_map/all_to_all | solution.py:518
  55.1 0.8 %shard_map.154 = f32[256,512]{1,0:T(8,128)} custom-call(f32[128,128]{1,0:T(8,128)S(1)} %bitcast.13, f32[16,256]{1,0:T(8,128)S(1)} %shard_map.150.delta, f32[240,128]{1,0:T(8,128)S(1)} %get-tuple-element.41.swept, f32[16,512]{1,0:T(8,128)S(1)} %collective-permute-done.5.last, f32[256,512]{1,0:T(8,128)} %get-tuple-element.42._), custom_call_target="tpu_custom_call", output_to_operand_aliasing={{}: (4, {})} | custom-call | flops 1000000 | bytes 3000000 | tf_op jit(solution)/shard_map/pallas_call | solution.py:437
  (10 shorter events, 0.0 us)
Async XLA Ops:
  0.0 4.1 %copy-start = (s32[32,128]{1,0:T(8,128)S(1)}, s32[32,128]{1,0:T(8,128)}, u32[]{:S(2)}) copy-start(s32[32,128]{1,0:T(8,128)} %refs_0_.1) | copy-start | bytes 49156
  0.0 4.1 %copy-start.1 = (f32[32,128]{1,0:T(8,128)S(1)}, f32[32,128]{1,0:T(8,128)}, u32[]{:S(2)}) copy-start(f32[32,128]{1,0:T(8,128)} %refs_1_.1) | copy-start | bytes 49156
  0.0 4.1 %copy-start.2 = (s32[32,8]{0,1:T(8,128)S(1)}, s32[32,8]{0,1:T(8,128)}, u32[]{:S(2)}) copy-start(s32[32,8]{0,1:T(8,128)} %param.21) | copy-start | bytes 3076
  0.0 4.1 %copy-start.3 = (s32[32,8]{0,1:T(8,128)S(1)}, s32[32,8]{0,1:T(8,128)}, u32[]{:S(2)}) copy-start(s32[32,8]{0,1:T(8,128)} %param.22) | copy-start | bytes 3076
  1.0 6.2 %collective-permute-start = (f32[120,512]{1,0:T(8,128)S(1)}, f32[120,512]{1,0:T(8,128)S(1)}, u32[]{:S(2)}, u32[]{:S(2)}) collective-permute-start(f32[120,512]{1,0:T(8,128)S(1)} %shard_map.146), channel_id=1, source_target_pairs={{0,1},{1,2},{2,3},{3,4},{4,5},{5,6},{6,7},{7,8},{8,9},{9,10},{10,1... | collective-permute-start | bytes 737288 | tf_op jit(solution)/shard_map/ppermute | solution.py:465
  7.3 5.2 %collective-permute-start.1 = (f32[216,128]{1,0:T(8,128)S(1)}, f32[216,128]{1,0:T(8,128)S(1)}, u32[]{:S(2)}, u32[]{:S(2)}) collective-permute-start(f32[216,128]{1,0:T(8,128)S(1)} %get-tuple-element.28), channel_id=1, source_target_pairs={{0,64},{64,128},{128,192},{192,0},{1,65},{65,129},{129,193},{193,1... | collective-permute-start | bytes 331784 | tf_op jit(solution)/shard_map/ppermute | solution.py:483
  8.7 3.7 %collective-permute-start.2 = (f32[184,128]{1,0:T(8,128)S(1)}, f32[184,128]{1,0:T(8,128)S(1)}, u32[]{:S(2)}, u32[]{:S(2)}) collective-permute-start(f32[184,128]{1,0:T(8,128)S(1)} %get-tuple-element.29), channel_id=1, source_target_pairs={{64,0},{128,64},{192,128},{0,192},{65,1},{129,65},{193,129},{1,193... | collective-permute-start | bytes 282632 | tf_op jit(solution)/shard_map/ppermute | solution.py:484
  13.6 25.0 %all-to-all-start = ((f32[64,4,128]{2,1,0:T(4,128)}), f32[64,4,128]{2,1,0:T(4,128)S(1)}, u32[]{:S(2)}, u32[]{:S(2)}) async-start(f32[64,4,128]{2,1,0:T(4,128)} %bitcast.36), calls=%async_computation | async-start | bytes 262144 | tf_op jit(solution)/shard_map/all_to_all | solution.py:491
  30.0 15.3 %collective-permute-start.3 = (f32[648,128]{1,0:T(8,128)S(1)}, f32[648,128]{1,0:T(8,128)S(1)}, u32[]{:S(2)}, u32[]{:S(2)}) collective-permute-start(f32[648,128]{1,0:T(8,128)S(1)} %get-tuple-element.39), channel_id=1, source_target_pairs={{0,64},{64,128},{128,192},{192,0},{1,65},{65,129},{129,193},{193,1... | collective-permute-start | bytes 995336 | tf_op jit(solution)/shard_map/ppermute | solution.py:499
  31.4 13.9 %collective-permute-start.4 = (f32[544,128]{1,0:T(8,128)S(1)}, f32[544,128]{1,0:T(8,128)S(1)}, u32[]{:S(2)}, u32[]{:S(2)}) collective-permute-start(f32[544,128]{1,0:T(8,128)S(1)} %get-tuple-element.40), channel_id=1, source_target_pairs={{64,0},{128,64},{192,128},{0,192},{65,1},{129,65},{193,129},{1,193... | collective-permute-start | bytes 835592 | tf_op jit(solution)/shard_map/ppermute | solution.py:500
  40.3 14.8 %all-to-all-start.1 = ((f32[64,2,128]{2,1,0:T(2,128)}), f32[64,2,128]{2,1,0:T(2,128)S(1)}, u32[]{:S(2)}, u32[]{:S(2)}) async-start(f32[64,2,128]{2,1,0:T(2,128)} %bitcast.37), calls=%async_computation.1 | async-start | bytes 131072 | tf_op jit(solution)/shard_map/all_to_all | solution.py:518
  46.5 5.5 %collective-permute-start.5 = (f32[16,512]{1,0:T(8,128)S(1)}, f32[16,512]{1,0:T(8,128)S(1)}, u32[]{:S(2)}, u32[]{:S(2)}) collective-permute-start(f32[16,512]{1,0:T(8,128)S(1)} %shard_map.153), channel_id=1, source_target_pairs={{1,0},{2,1},{3,2},{4,3},{5,4},{6,5},{7,6},{8,7},{9,8},{10,9},{11,1... | collective-permute-start | bytes 98312 | tf_op jit(solution)/shard_map/ppermute | solution.py:506

commit v6 on v5

--- a/solution.py
+++ b/solution.py
@@ -116,7 +116,7 @@
     return courant * jnp.where(courant > 0.0, below_cell, above_cell)
 
 
-def sweep(count, load_own, load_halo, store, lanes, unrolled):
+def sweep(count, load_own, load_halo, store, lanes, segments=None):
     plane = lax.broadcasted_iota(jnp.int32, (8, lanes), 0)
     cycle = lax.broadcasted_iota(jnp.int32, (8, lanes), 1)
     first, last = plane == 0, plane == 7
@@ -180,9 +180,10 @@
     for stage in range(6):
         state = step(LOWEST + stage, state, stage)
     stage = 6
-    if not unrolled:
-        state = lax.fori_loop(LOWEST + 6, LOWEST + 34, lambda column, s: step(column, s, 6), state, unroll=4)
-        stage = 34
+    for start, stop, before in segments or ():
+        before()
+        state = lax.fori_loop(start, stop, lambda column, s: step(column, s, 6), state, unroll=4)
+        stage = stop - LOWEST
     for stage in range(stage, count):
         state = step(LOWEST + stage, state, stage)
 
@@ -211,21 +212,19 @@
 
 
 def near_kernel(*refs):
-    fields, (below, above, left, crossing, send) = refs[:4], refs[4:9]
-    halos, (swept, out, semaphore) = refs[9:13], refs[13:]
+    fields, (below, above, left, crossing, _, _, out), halos, swept = refs[:4], refs[4:11], refs[11:15], refs[15]
     fill_halos(halos, NEAR_BELOW, below)
     fill_halos(halos, NEAR_ABOVE, above)
 
     def store(column, values):
         swept[row_slice(column + 2), :] = values
 
-    sweep(COLS + 4, *loaders(fields, left, halos, 1), store, 128, True)
+    sweep(COLS + 4, *loaders(fields, left, halos, 1), store, 128)
     turned = swept[...].T
     out[pl.ds(0, R_AX, stride=4), :] = turned[:R_AX, :128]
     out[pl.ds(1, R_AX, stride=4), :] = turned[:R_AX, 128:]
     out[pl.ds(2, R_AX, stride=4), :] = crossing[:R_AX, :]
     out[pl.ds(3, R_AX, stride=4), :] = crossing[R_AX:, :]
-    copy_out(out, send, semaphore)
 
 
 def fill_far_halos(halos, near_below, near_above, below, above):
@@ -244,24 +243,44 @@
     def store(column, values):
         out[row_slice(column + 2), :] = values
 
-    sweep(6, *loaders(fields, left, halos, TILES), store, NR, True)
+    sweep(6, *loaders(fields, left, halos, TILES), store, NR)
 
 
 def far_kernel(*refs):
     sources, planes, (left, result, first_tile), halos = refs[:4], refs[4:8], refs[8:11], refs[11:15]
     fields, (out, semaphores) = refs[15:19], refs[19:]
-    copies = copy_all(zip(sources, fields), semaphores)
+    arrive = [(0, 80), (80, 144), (144, 208), (208, 256)]
+    leave = [(0, 64), (64, 128), (128, 192), (192, KEPT)]
+    incoming = [
+        copy_all([(f.at[pl.ds(a, b - a), :], held.at[pl.ds(a, b - a), :]) for f, held in zip(sources, fields)], semaphores, 4 * k)
+        for k, (a, b) in enumerate(arrive)
+    ]
+    outgoing = []
     fill_far_halos(halos, *planes)
-    for copy in copies:
-        copy.wait()
 
     def store(column, values):
         if not isinstance(column, int) or column >= 0:
             out[row_slice(column), :] = values
             first_tile[row_slice(column), :] = values[:, :128]
 
-    sweep(COLS + 4, *loaders(fields, left, halos, TILES), store, NR, False)
-    copy_out(out, result.at[pl.ds(0, KEPT), :], semaphores.at[4])
+    def send(piece):
+        a, b = leave[piece]
+        pairs = [(out.at[pl.ds(a, b - a), :], result.at[pl.ds(a, b - a), :])]
+        outgoing.extend(copy_all(pairs, semaphores, 16 + piece))
+
+    def pause(piece):
+        for copy in incoming[piece]:
+            copy.wait()
+        if piece:
+            send(piece - 1)
+
+    for copy in incoming[0]:
+        copy.wait()
+    segments = [(2, 10, lambda: None)] + [(8 * k + 2, min(8 * k + 10, 30), functools.partial(pause, k)) for k in (1, 2, 3)]
+    sweep(COLS + 4, *loaders(fields, left, halos, TILES), store, NR, segments)
+    send(3)
+    for copy in outgoing:
+        copy.wait()
 
 
 def pieces(values, count):
@@ -378,7 +397,7 @@
     return mm(ah, bh) + (mm(al, bh) + mm(ah, bl))
 
 
-def filter_kernel(received, first_h, first_l, block_h, block_l, twiddle, last_h, last_l, send, out, semaphore):
+def filter_kernel(received, first_h, first_l, block_h, block_l, twiddle, last_h, last_l, out):
     sectors = jnp.concatenate(
         [received[pl.ds(0, R_AX, stride=4), :], received[pl.ds(1, R_AX, stride=4), :]], axis=1
     )
@@ -405,7 +424,6 @@
     result = dot3((last_h[...], last_l[...]), pieces(turned, 2))
     out[pl.ds(0, R_AX, stride=2), :] = result[:, :128]
     out[pl.ds(1, R_AX, stride=2), :] = result[:, 128:]
-    copy_out(out, send, semaphore)
 
 
 def final_kernel(received, delta, swept, last, _, result, out, semaphores):
@@ -433,7 +451,7 @@
         array, space = given if isinstance(given, tuple) else (given, VMEM)
         arrays.append(pltpu.with_memory_space_constraint(array, HBM) if space is HBM else array)
         specs.append(pl.BlockSpec(memory_space=space))
-    out_specs = [pl.BlockSpec(memory_space=o.memory_space) for o in outputs]
+    out_specs = [pl.BlockSpec(memory_space=getattr(o, "memory_space", VMEM)) for o in outputs]
     return pl.pallas_call(
         kernel,
         in_specs=specs,
@@ -444,6 +462,10 @@
         cost_estimate=pl.CostEstimate(flops=int(cost * 1e6), bytes_accessed=int(cost * 3e6), transcendentals=0),
         compiler_params=pltpu.CompilerParams(vmem_limit_bytes=16 * 1024 * 1024),
     )(*arrays)
+
+
+def free(*dims):
+    return jax.ShapeDtypeStruct(dims, F32)
 
 
 def local(
@@ -482,20 +504,20 @@
     )
     near_below = lax.ppermute(near_up, "ax", higher_ax)
     near_above = lax.ppermute(near_down, "ax", lower_ax)
-    (send,) = call(
-        near_kernel,
-        [*near_tiles, near_below, near_above, left, crossing],
-        [HBM((4 * R_AX, 128), F32)],
-        [VMEM((1, 36 * 8, 128), F32)] * 4 + [VMEM((ROWS, 128), F32), VMEM((4 * R_AX, 128), F32), DMA],
-    )
-    got = lax.all_to_all(send.reshape(R_AX, 4, 128), "az", 0, 0, tiled=True).reshape(4 * R_AX, 128)
-
     far_up, far_down = call(
         pack_far_planes,
         [*fields, left],
         [VMEM((FAR_BELOW_ROWS, 128), F32), VMEM((FAR_ABOVE_ROWS, 128), F32)],
         [VMEM(((TILES - 1) * ROWS, 128), F32)] * 4 + [DMA((4 * (TILES - 1),))],
     )
+    (send,) = call(
+        near_kernel,
+        [*near_tiles, near_below, near_above, left, crossing, (far_up, pl.ANY), (far_down, pl.ANY)],
+        [free(4 * R_AX, 128)],
+        [VMEM((1, 36 * 8, 128), F32)] * 4 + [VMEM((ROWS, 128), F32)],
+    )
+    got = lax.all_to_all(send.reshape(R_AX, 4, 128), "az", 0, 0, tiled=True).reshape(4 * R_AX, 128)
+
     far_below = lax.ppermute(far_up, "ax", higher_ax)
     far_above = lax.ppermute(far_down, "ax", lower_ax)
     far_inputs = [*fields, near_below, near_above, far_below, far_above, left]
@@ -508,13 +530,11 @@
         far_kernel,
         far_inputs,
         [HBM((ROWS, NR), F32), VMEM((KEPT, 128), F32)],
-        far_halos + [VMEM((ROWS, NR), F32)] * 4 + [VMEM((KEPT, NR), F32), DMA((5,))],
+        far_halos + [VMEM((ROWS, NR), F32)] * 4 + [VMEM((KEPT, NR), F32), DMA((20,))],
         cost=4.0,
     )
 
-    (back,) = call(
-        filter_kernel, [got, *held_tables], [HBM((2 * R_AX, 128), F32)], [VMEM((2 * R_AX, 128), F32), DMA]
-    )
+    (back,) = call(filter_kernel, [got, *held_tables], [free(2 * R_AX, 128)])
     returned = lax.all_to_all(back.reshape(R_AX, 2, 128), "az", 0, 0, tiled=True).reshape(2 * R_AX, 128)
     (delta,) = call(arrival_kernel, [got, volume], [VMEM((XR, ROWS), F32)])
     (out,) = call(

time: 56.5 us -> 56.1 us (level)
    all_to_all x1, waiting for transfers between devices: 5.88 us -> 7.6 us  [local(): lax.all_to_all(send.reshape(R_AX, 4, 128), 'az', 0, 0, tiled=True)]
    ppermute x1, waiting for transfers between devices: 2.19 us -> 0.47 us  [local(): near_above = lax.ppermute(near_down, 'ax', lower_ax)]
  transfers between devices with their start and end apart: 8 -> 8, of which waited for: 5 -> 5; matrix products, arithmetic and copies ran while one was open for 0% -> 0% of each run, Pallas kernels for 20% -> 19%
where the time goes in v6:
time: 56.1 us; the launch traced here: 55.7 us
  starting transfers between devices  28.8 us (51%)
  Pallas kernels  13.5 us (24%)
  waiting for transfers between devices  13.3 us (24%)
    all_to_all x1, starting transfers between devices, local(): lax.all_to_all(send.reshape(R_AX, 4, 128), 'az', 0, 0, tiled=True)  14.6 us
    pallas_call x10, Pallas kernels, call(): pl.pallas_call(kernel, in_specs=specs, out_specs=out_specs, out_shape=lis...  13.5 us
    all_to_all x1, waiting for transfers between devices, local(): lax.all_to_all(send.reshape(R_AX, 4, 128), 'az', 0, 0, tiled=True)  7.6 us
    all_to_all x1, starting transfers between devices, local(): lax.all_to_all(back.reshape(R_AX, 2, 128), 'az', 0, 0, tiled=True)  4.88 us
    all_to_all x1, waiting for transfers between devices, local(): lax.all_to_all(back.reshape(R_AX, 2, 128), 'az', 0, 0, tiled=True)  3.64 us
    ppermute x1, starting transfers between devices, local(): left = lax.ppermute(right, 'az', higher_az)  3.1 us
    ppermute x1, starting transfers between devices, local(): near_above = lax.ppermute(near_down, 'ax', lower_ax)  1.53 us
    ppermute x1, waiting for transfers between devices, local(): left = lax.ppermute(right, 'az', higher_az)  1.42 us
  transfers between devices with their start and end apart: 8, of which 5 were waited for; matrix products, arithmetic and copies ran while one was open for 0% of the time, Pallas kernels for 19%

profile of v6, /device:TPU:1, one launch (start us, length us, event | category | flops | bytes accessed | tf_op | source)
XLA Modules:
  0.0 55.7 jit_solution(15716595715049266739)
XLA Ops:
  0.0 1.0 %shard_map.146 = f32[120,512]{1,0:T(8,128)S(1)} custom-call(f32[256,512]{1,0:T(8,128)} %bitcast.16, f32[256,512]{1,0:T(8,128)} %bitcast.21, f32[256,512]{1,0:T(8,128)} %bitcast.26, f32[256,512]{1,0:T(8,128)} %bitcast.31), custom_call_target="tpu_custom_call" | custom-call | flops 1000000 | bytes 3000000 | tf_op jit(solution)/shard_map/pallas_call | solution.py:455
  1.0 3.1 %collective-permute-start = (f32[120,512]{1,0:T(8,128)S(1)}, f32[120,512]{1,0:T(8,128)S(1)}, u32[]{:S(2)}, u32[]{:S(2)}) collective-permute-start(f32[120,512]{1,0:T(8,128)S(1)} %shard_map.146), channel_id=1, source_target_pairs={{0,1},{1,2},{2,3},{3,4},{4,5},{5,6},{6,7},{7,8},{8,9},{9,10},{10,1... | collective-permute-start | bytes 737288 | tf_op jit(solution)/shard_map/ppermute | solution.py:487
  4.1 1.7 %shard_map.145 = (f32[128,128]{1,0:T(8,128)S(1)}, f32[16,256]{1,0:T(8,128)S(1)}, f32[256,128]{1,0:T(8,128)S(1)}, f32[256,128]{1,0:T(8,128)S(1)}, f32[256,128]{1,...) custom-call(s32[32,128]{1,0:T(8,128)S(1)} %copy-done, ...), custom_call_target="tpu_custom_call" | custom-call | flops 1000000 | bytes 3000000 | tf_op jit(solution)/shard_map/pallas_call | solution.py:455
  5.8 1.4 %collective-permute-done.refs_4_.refs_6_.refs_8_ = f32[120,512]{1,0:T(8,128)S(1)} collective-permute-done((f32[120,512]{1,0:T(8,128)S(1)}, f32[120,512]{1,0:T(8,128)S(1)}, u32[]{:S(2)}, u32[]{:S(2)}) %collective-permute-start) | collective-permute-done | bytes 245792 | tf_op jit(solution)/shard_map/ppermute | solution.py:487
  7.3 0.1 shard_map.147
  7.3 1.4 %collective-permute-start.1 = (f32[216,128]{1,0:T(8,128)S(1)}, f32[216,128]{1,0:T(8,128)S(1)}, u32[]{:S(2)}, u32[]{:S(2)}) collective-permute-start(f32[216,128]{1,0:T(8,128)S(1)} %get-tuple-element.28), channel_id=1, source_target_pairs={{0,64},{64,128},{128,192},{192,0},{1,65},{65,129},{129,193},{193,1... | collective-permute-start | bytes 331784 | tf_op jit(solution)/shard_map/ppermute | solution.py:505
  8.7 1.5 %collective-permute-start.2 = (f32[184,128]{1,0:T(8,128)S(1)}, f32[184,128]{1,0:T(8,128)S(1)}, u32[]{:S(2)}, u32[]{:S(2)}) collective-permute-start(f32[184,128]{1,0:T(8,128)S(1)} %get-tuple-element.29), channel_id=1, source_target_pairs={{64,0},{128,64},{192,128},{0,192},{65,1},{129,65},{193,129},{1,193... | collective-permute-start | bytes 282632 | tf_op jit(solution)/shard_map/ppermute | solution.py:506
  10.2 1.7 %shard_map.148 = (f32[648,128]{1,0:T(8,128)S(1)}, f32[544,128]{1,0:T(8,128)S(1)}) custom-call(f32[256,512]{1,0:T(8,128)} %bitcast.18, f32[256,512]{1,0:T(8,128)} %bitcast.23, f32[256,512]{1,0:T(8,128)} %bitcast.28, f32[256,512]{1,0:T(8,128)} %bitcast.33, f32[120,512]{1,0:T(8,128)S(1)} %collective-permute-done.refs_4_.refs_6_.refs_8_), custom_call_target="tpu_custom_call" | custom-call | flops 1000000 | bytes 3000000 | tf_op jit(solution)/shard_map/pallas_call | solution.py:455
  11.9 0.5 collective-permute-done.2.refs_5_
  12.4 0.2 collective-permute-done.1.refs_4_
  12.6 1.1 %shard_map.149 = f32[256,128]{1,0:T(8,128)} custom-call(f32[256,128]{1,0:T(8,128)S(1)} %get-tuple-element.24.refs_0_, f32[256,128]{1,0:T(8,128)S(1)} %get-tuple-element.25.refs_1_, f32[256,128]{1,0:T(8,128)S(1)} %get-tuple-element.26.refs_2_, f32[256,128]{1,0:T(8,128)S(1)} %get-tuple-element.27.refs_3_, f32[216,128]{1,0:T(8,128)S(1)} %collective-permute-done.1.refs_4_, ...), custom_call_target="tpu_custom_call" | custom-call | flops 1000000 | bytes 3000000 | tf_op jit(solution)/shard_map/pallas_call | solution.py:455
  13.6 14.6 %all-to-all-start = ((f32[64,4,128]{2,1,0:T(4,128)}), f32[64,4,128]{2,1,0:T(4,128)S(1)}, u32[]{:S(2)}, u32[]{:S(2)}) async-start(f32[64,4,128]{2,1,0:T(4,128)} %bitcast.6), calls=%async_computation | async-start | bytes 262144 | tf_op jit(solution)/shard_map/all_to_all | solution.py:519
  28.3 1.4 %collective-permute-start.3 = (f32[648,128]{1,0:T(8,128)S(1)}, f32[648,128]{1,0:T(8,128)S(1)}, u32[]{:S(2)}, u32[]{:S(2)}) collective-permute-start(f32[648,128]{1,0:T(8,128)S(1)} %get-tuple-element.31.refs_8_), channel_id=1, source_target_pairs={{0,64},{64,128},{128,192},{192,0},{1,65},{65,129},{129,193},{193,1... | collective-permute-start | bytes 995336 | tf_op jit(solution)/shard_map/ppermute | solution.py:521
  29.7 1.4 %collective-permute-start.4 = (f32[544,128]{1,0:T(8,128)S(1)}, f32[544,128]{1,0:T(8,128)S(1)}, u32[]{:S(2)}, u32[]{:S(2)}) collective-permute-start(f32[544,128]{1,0:T(8,128)S(1)} %get-tuple-element.32.refs_9_), channel_id=1, source_target_pairs={{64,0},{128,64},{192,128},{0,192},{65,1},{129,65},{193,129},{1,193... | collective-permute-start | bytes 835592 | tf_op jit(solution)/shard_map/ppermute | solution.py:522
  31.0 7.6 %all-to-all-done = f32[64,4,128]{2,1,0:T(4,128)S(1)} async-done(((f32[64,4,128]{2,1,0:T(4,128)}), f32[64,4,128]{2,1,0:T(4,128)S(1)}, u32[]{:S(2)}, u32[]{:S(2)}) %all-to-all-start) | async-done | bytes 131104 | tf_op jit(solution)/shard_map/all_to_all | solution.py:519
  38.6 1.6 %shard_map.150 = f32[128,128]{1,0:T(8,128)} custom-call(f32[256,128]{1,0:T(8,128)S(1)} %bitcast.11, bf16[80,64]{1,0:T(8,128)(2,1)S(1)} %get-tuple-element.33.first_h, bf16[80,64]{1,0:T(8,128)(2,1)S(1)} %get-tuple-element.34.first_l, bf16[256,512]{1,0:T(8,128)(2,1)S(1)} %get-tuple-element.35.block_h, bf16[256,512]{1,0:T(8,128)(2,1)S(1)} %get-tuple-element.36.block_l, ...), custom_call_target="tpu_custom_call" | custom-call | flops 1000000 | bytes 3000000 | tf_op jit(solution)/shard_map/pallas_call | solution.py:455
  40.3 4.9 %all-to-all-start.1 = ((f32[64,2,128]{2,1,0:T(2,128)}), f32[64,2,128]{2,1,0:T(2,128)S(1)}, u32[]{:S(2)}, u32[]{:S(2)}) async-start(f32[64,2,128]{2,1,0:T(2,128)} %bitcast.8), calls=%async_computation.1 | async-start | bytes 131072 | tf_op jit(solution)/shard_map/all_to_all | solution.py:538
  45.2 1.1 %shard_map.153 = f32[16,512]{1,0:T(8,128)S(1)} custom-call(f32[256,512]{1,0:T(8,128)} %bitcast.19, f32[256,512]{1,0:T(8,128)} %bitcast.24, f32[256,512]{1,0:T(8,128)} %bitcast.29, f32[256,512]{1,0:T(8,128)} %bitcast.34, f32[216,128]{1,0:T(8,128)S(1)} %collective-permute-done.1.refs_4_, f32[184,128]{1,0:T(8,128)S(1)} %collective-permute-done.2.refs_5_, ...), custom_call_target="tpu_custom_call" | custom-call | flops 1000000 | bytes 3000000 | tf_op jit(solution)/shard_map/pallas_call | solution.py:455
  46.3 0.5 collective-permute-start.5
  46.8 4.1 %shard_map.152 = (f32[256,512]{1,0:T(8,128)}, f32[240,128]{1,0:T(8,128)S(1)}) custom-call(f32[256,512]{1,0:T(8,128)} %bitcast.20, f32[256,512]{1,0:T(8,128)} %bitcast.25, f32[256,512]{1,0:T(8,128)} %bitcast.30, f32[256,512]{1,0:T(8,128)} %bitcast.35, f32[216,128]{1,0:T(8,128)S(1)} %collective-permute-done.1.refs_4_, ...), custom_call_target="tpu_custom_call" | custom-call | flops 4000000 | bytes 12000000 | tf_op jit(solution)/shard_map/pallas_call | solution.py:455
  50.9 0.4 shard_map.151.delta
  51.3 0.0 collective-permute-done.5.last
  51.3 3.6 %all-to-all-done.1 = f32[64,2,128]{2,1,0:T(2,128)S(1)} async-done(((f32[64,2,128]{2,1,0:T(2,128)}), f32[64,2,128]{2,1,0:T(2,128)S(1)}, u32[]{:S(2)}, u32[]{:S(2)}) %all-to-all-start.1) | async-done | bytes 65568 | tf_op jit(solution)/shard_map/all_to_all | solution.py:538
  54.9 0.8 %shard_map.154 = f32[256,512]{1,0:T(8,128)} custom-call(f32[128,128]{1,0:T(8,128)S(1)} %bitcast.13, f32[16,256]{1,0:T(8,128)S(1)} %shard_map.151.delta, f32[240,128]{1,0:T(8,128)S(1)} %get-tuple-element.41.swept, f32[16,512]{1,0:T(8,128)S(1)} %collective-permute-done.5.last, f32[256,512]{1,0:T(8,128)} %get-tuple-element.42._), custom_call_target="tpu_custom_call", output_to_operand_aliasing={{}: (4, {})} | custom-call | flops 1000000 | bytes 3000000 | tf_op jit(solution)/shard_map/pallas_call | solution.py:455
  (10 shorter events, 0.0 us)
Async XLA Ops:
  0.0 4.1 %copy-start = (s32[32,128]{1,0:T(8,128)S(1)}, s32[32,128]{1,0:T(8,128)}, u32[]{:S(2)}) copy-start(s32[32,128]{1,0:T(8,128)} %refs_0_.1) | copy-start | bytes 49156
  0.0 4.1 %copy-start.1 = (f32[32,128]{1,0:T(8,128)S(1)}, f32[32,128]{1,0:T(8,128)}, u32[]{:S(2)}) copy-start(f32[32,128]{1,0:T(8,128)} %refs_1_.1) | copy-start | bytes 49156
  0.0 4.1 %copy-start.2 = (s32[32,8]{0,1:T(8,128)S(1)}, s32[32,8]{0,1:T(8,128)}, u32[]{:S(2)}) copy-start(s32[32,8]{0,1:T(8,128)} %param.21) | copy-start | bytes 3076
  0.0 4.1 %copy-start.3 = (s32[32,8]{0,1:T(8,128)S(1)}, s32[32,8]{0,1:T(8,128)}, u32[]{:S(2)}) copy-start(s32[32,8]{0,1:T(8,128)} %param.22) | copy-start | bytes 3076
  1.0 6.2 %collective-permute-start = (f32[120,512]{1,0:T(8,128)S(1)}, f32[120,512]{1,0:T(8,128)S(1)}, u32[]{:S(2)}, u32[]{:S(2)}) collective-permute-start(f32[120,512]{1,0:T(8,128)S(1)} %shard_map.146), channel_id=1, source_target_pairs={{0,1},{1,2},{2,3},{3,4},{4,5},{5,6},{6,7},{7,8},{8,9},{9,10},{10,1... | collective-permute-start | bytes 737288 | tf_op jit(solution)/shard_map/ppermute | solution.py:487
  7.3 5.2 %collective-permute-start.1 = (f32[216,128]{1,0:T(8,128)S(1)}, f32[216,128]{1,0:T(8,128)S(1)}, u32[]{:S(2)}, u32[]{:S(2)}) collective-permute-start(f32[216,128]{1,0:T(8,128)S(1)} %get-tuple-element.28), channel_id=1, source_target_pairs={{0,64},{64,128},{128,192},{192,0},{1,65},{65,129},{129,193},{193,1... | collective-permute-start | bytes 331784 | tf_op jit(solution)/shard_map/ppermute | solution.py:505
  8.7 3.7 %collective-permute-start.2 = (f32[184,128]{1,0:T(8,128)S(1)}, f32[184,128]{1,0:T(8,128)S(1)}, u32[]{:S(2)}, u32[]{:S(2)}) collective-permute-start(f32[184,128]{1,0:T(8,128)S(1)} %get-tuple-element.29), channel_id=1, source_target_pairs={{64,0},{128,64},{192,128},{0,192},{65,1},{129,65},{193,129},{1,193... | collective-permute-start | bytes 282632 | tf_op jit(solution)/shard_map/ppermute | solution.py:506
  13.6 25.0 %all-to-all-start = ((f32[64,4,128]{2,1,0:T(4,128)}), f32[64,4,128]{2,1,0:T(4,128)S(1)}, u32[]{:S(2)}, u32[]{:S(2)}) async-start(f32[64,4,128]{2,1,0:T(4,128)} %bitcast.6), calls=%async_computation | async-start | bytes 262144 | tf_op jit(solution)/shard_map/all_to_all | solution.py:519
  28.3 16.9 %collective-permute-start.3 = (f32[648,128]{1,0:T(8,128)S(1)}, f32[648,128]{1,0:T(8,128)S(1)}, u32[]{:S(2)}, u32[]{:S(2)}) collective-permute-start(f32[648,128]{1,0:T(8,128)S(1)} %get-tuple-element.31.refs_8_), channel_id=1, source_target_pairs={{0,64},{64,128},{128,192},{192,0},{1,65},{65,129},{129,193},{193,1... | collective-permute-start | bytes 995336 | tf_op jit(solution)/shard_map/ppermute | solution.py:521
  29.7 15.5 %collective-permute-start.4 = (f32[544,128]{1,0:T(8,128)S(1)}, f32[544,128]{1,0:T(8,128)S(1)}, u32[]{:S(2)}, u32[]{:S(2)}) collective-permute-start(f32[544,128]{1,0:T(8,128)S(1)} %get-tuple-element.32.refs_9_), channel_id=1, source_target_pairs={{64,0},{128,64},{192,128},{0,192},{65,1},{129,65},{193,129},{1,193... | collective-permute-start | bytes 835592 | tf_op jit(solution)/shard_map/ppermute | solution.py:522
  40.3 14.7 %all-to-all-start.1 = ((f32[64,2,128]{2,1,0:T(2,128)}), f32[64,2,128]{2,1,0:T(2,128)S(1)}, u32[]{:S(2)}, u32[]{:S(2)}) async-start(f32[64,2,128]{2,1,0:T(2,128)} %bitcast.8), calls=%async_computation.1 | async-start | bytes 131072 | tf_op jit(solution)/shard_map/all_to_all | solution.py:538
  46.3 5.0 %collective-permute-start.5 = (f32[16,512]{1,0:T(8,128)S(1)}, f32[16,512]{1,0:T(8,128)S(1)}, u32[]{:S(2)}, u32[]{:S(2)}) collective-permute-start(f32[16,512]{1,0:T(8,128)S(1)} %shard_map.153), channel_id=1, source_target_pairs={{1,0},{2,1},{3,2},{4,3},{5,4},{6,5},{7,6},{8,7},{9,8},{10,9},{11,1... | collective-permute-start | bytes 98312 | tf_op jit(solution)/shard_map/ppermute | solution.py:528

commit v7 on v6

--- a/solution.py
+++ b/solution.py
@@ -66,10 +66,12 @@
 
 
 def pack_columns(*refs):
-    fields, (right, semaphores) = refs[:4], refs[4:]
+    fields, (right, semaphores) = refs[:4], refs[-2:]
+    lanes = right.shape[1]
     pairs, row = [], 0
     for field, count in zip(fields, LEFT_COUNT):
-        pairs.append((field.at[pl.ds(ROWS - count * 8, count * 8), :], right.at[pl.ds(row, count * 8), :]))
+        source = field.at[pl.ds(ROWS - count * 8, count * 8), pl.ds(0 if lanes == 128 else NR - lanes, lanes)]
+        pairs.append((source, right.at[pl.ds(row, count * 8), :]))
         row += count * 8
     for copy in copy_all(pairs, semaphores):
         copy.wait()
@@ -79,7 +81,7 @@
     for tile, field, plane, count, row in entries:
         for at in range(count):
             origin = LEFT.index((field, at - count)) * 8 + plane + shift
-            out[row + at : row + at + 1, :] = left[origin : origin + 1, pl.ds(tile * 128, 128)]
+            out[row + at : row + at + 1, :] = left[origin : origin + 1, pl.ds(max(tile - 1, 0) * 128, 128)]
         out[row + count : row + count + COLS, :] = load(tile, field, plane + shift)
     used = entries[-1][4] + entries[-1][3] + COLS
     if used < out.shape[0]:
@@ -201,7 +203,8 @@
 def loaders(fields, left, halos, tiles):
     def load_own(field, column):
         if isinstance(column, int) and column < 0:
-            return left[row_slice(LEFT.index((field, column))), pl.ds(0, tiles * 128)]
+            parts = [part[row_slice(LEFT.index((field, column))), :] for part in left]
+            return jnp.concatenate(parts, axis=1) if tiles > 1 else parts[0]
         return fields[field][row_slice(column), :]
 
     def load_halo(field, column):
@@ -212,14 +215,14 @@
 
 
 def near_kernel(*refs):
-    fields, (below, above, left, crossing, _, _, out), halos, swept = refs[:4], refs[4:11], refs[11:15], refs[15]
+    fields, (below, above, left, crossing, out), halos, swept = refs[:4], refs[4:9], refs[9:13], refs[13]
     fill_halos(halos, NEAR_BELOW, below)
     fill_halos(halos, NEAR_ABOVE, above)
 
     def store(column, values):
         swept[row_slice(column + 2), :] = values
 
-    sweep(COLS + 4, *loaders(fields, left, halos, 1), store, 128)
+    sweep(COLS + 4, *loaders(fields, [left], halos, 1), store, 128)
     turned = swept[...].T
     out[pl.ds(0, R_AX, stride=4), :] = turned[:R_AX, :128]
     out[pl.ds(1, R_AX, stride=4), :] = turned[:R_AX, 128:]
@@ -233,8 +236,8 @@
 
 
 def far_first_kernel(*refs):
-    sources, planes, (left, out), halos = refs[:4], refs[4:8], refs[8:10], refs[10:14]
-    fields, semaphores = refs[14:18], refs[18]
+    sources, planes, left, out, halos = refs[:4], refs[4:8], refs[8:10], refs[10], refs[11:15]
+    fields, semaphores = refs[15:19], refs[19]
     copies = copy_all([(f.at[pl.ds(0, 16), :], held) for f, held in zip(sources, fields)], semaphores)
     fill_far_halos(halos, *planes)
     for copy in copies:
@@ -247,8 +250,8 @@
 
 
 def far_kernel(*refs):
-    sources, planes, (left, result, first_tile), halos = refs[:4], refs[4:8], refs[8:11], refs[11:15]
-    fields, (out, semaphores) = refs[15:19], refs[19:]
+    sources, planes, left, (result, first_tile), halos = refs[:4], refs[4:8], refs[8:10], refs[10:12], refs[12:16]
+    fields, (out, semaphores) = refs[16:20], refs[20:]
     arrive = [(0, 80), (80, 144), (144, 208), (208, 256)]
     leave = [(0, 64), (64, 128), (128, 192), (192, KEPT)]
     incoming = [
@@ -394,7 +397,9 @@
 
 def dot3(a, b):
     (ah, al), (bh, bl) = a, b
-    return mm(ah, bh) + (mm(al, bh) + mm(ah, bl))
+    rows = ah.shape[0]
+    both = mm(jnp.concatenate([ah, al], axis=0), bh)
+    return both[:rows] + (both[rows:] + mm(ah, bl))
 
 
 def filter_kernel(received, first_h, first_l, block_h, block_l, twiddle, last_h, last_l, out):
@@ -483,8 +488,8 @@
     lower_ax, lower_az = ([(j, i) for i, j in pairs] for pairs in (higher_ax, higher_az))
     fields = [(a.reshape(ROWS, NR), HBM) for a in (fraction, courant_axial, courant_azimuth, courant_radial)]
 
-    (right,) = call(pack_columns, fields, [VMEM((len(LEFT) * 8, NR), F32)], [DMA((4,))])
-    left = lax.ppermute(right, "az", higher_az)
+    (near_right,) = call(pack_columns, fields, [VMEM((len(LEFT) * 8, 128), F32)], [DMA((4,))])
+    near_left = lax.ppermute(near_right, "az", higher_az)
 
     tables = filter_tables()
     crossing, volume, *held = call(
@@ -499,20 +504,24 @@
 
     near_up, near_down = call(
         pack_near_planes,
-        [*near_tiles, left],
+        [*near_tiles, near_left],
         [VMEM((NEAR_BELOW_ROWS, 128), F32), VMEM((NEAR_ABOVE_ROWS, 128), F32)],
     )
     near_below = lax.ppermute(near_up, "ax", higher_ax)
     near_above = lax.ppermute(near_down, "ax", lower_ax)
+    (far_right,) = call(
+        pack_columns, [*fields, (near_up, pl.ANY)], [VMEM((len(LEFT) * 8, NR - 128), F32)], [DMA((4,))]
+    )
+    far_left = lax.ppermute(far_right, "az", higher_az)
     far_up, far_down = call(
         pack_far_planes,
-        [*fields, left],
+        [*fields, far_left],
         [VMEM((FAR_BELOW_ROWS, 128), F32), VMEM((FAR_ABOVE_ROWS, 128), F32)],
         [VMEM(((TILES - 1) * ROWS, 128), F32)] * 4 + [DMA((4 * (TILES - 1),))],
     )
     (send,) = call(
         near_kernel,
-        [*near_tiles, near_below, near_above, left, crossing, (far_up, pl.ANY), (far_down, pl.ANY)],
+        [*near_tiles, near_below, near_above, near_left, crossing],
         [free(4 * R_AX, 128)],
         [VMEM((1, 36 * 8, 128), F32)] * 4 + [VMEM((ROWS, 128), F32)],
     )
@@ -520,7 +529,7 @@
 
     far_below = lax.ppermute(far_up, "ax", higher_ax)
     far_above = lax.ppermute(far_down, "ax", lower_ax)
-    far_inputs = [*fields, near_below, near_above, far_below, far_above, left]
+    far_inputs = [*fields, near_below, near_above, far_below, far_above, near_left, far_left]
     far_halos = [VMEM((TILES, 36 * 8, 128), F32)] * 4
     (first_columns,) = call(
         far_first_kernel, far_inputs, [VMEM((16, NR), F32)], far_halos + [VMEM((16, NR), F32)] * 4 + [DMA((4,))]

time: 56.1 us -> 55.1 us (0.982)
  waiting for transfers between devices: 13.3 us -> 11.6 us
  Pallas kernels: 13.5 us -> 14.2 us
    all_to_all x1, starting transfers between devices: 14.6 us -> 12.5 us  [local(): lax.all_to_all(send.reshape(R_AX, 4, 128), 'az', 0, 0, tiled=True)]
    ppermute x1 -> x2, starting transfers between devices: 3.1 us -> 5.09 us  [the longest x1 3.1 us: local(): near_left = lax.ppermute(near_right, 'az', higher_az)]
    all_to_all x1, waiting for transfers between devices: 7.6 us -> 5.87 us  [local(): lax.all_to_all(send.reshape(R_AX, 4, 128), 'az', 0, 0, tiled=True)]
    ppermute x1, waiting for transfers between devices: 0.47 us -> 1.98 us  [local(): near_above = lax.ppermute(near_down, 'ax', lower_ax)]
    ppermute x1 -> x2, waiting for transfers between devices: 1.42 us -> 0.01 us  [the longest x1 0.01 us: local(): near_left = lax.ppermute(near_right, 'az', higher_az)]
    pallas_call x10 -> x11, Pallas kernels: 13.5 us -> 14.2 us  [call(): pl.pallas_call(kernel, in_specs=specs, out_specs=out_specs, out_shape=lis...]
  transfers between devices with their start and end apart: 8 -> 9, of which waited for: 5 -> 4; matrix products, arithmetic and copies ran while one was open for 0% -> 0% of each run, Pallas kernels for 19% -> 21%
where the time goes in v7:
time: 55.1 us; the launch traced here: 54.6 us
  starting transfers between devices  28.7 us (52%)
  Pallas kernels  14.2 us (26%)
  waiting for transfers between devices  11.6 us (21%)
    pallas_call x11, Pallas kernels, call(): pl.pallas_call(kernel, in_specs=specs, out_specs=out_specs, out_shape=lis...  14.2 us
    all_to_all x1, starting transfers between devices, local(): lax.all_to_all(send.reshape(R_AX, 4, 128), 'az', 0, 0, tiled=True)  12.5 us
    all_to_all x1, waiting for transfers between devices, local(): lax.all_to_all(send.reshape(R_AX, 4, 128), 'az', 0, 0, tiled=True)  5.87 us
    all_to_all x1, starting transfers between devices, local(): lax.all_to_all(back.reshape(R_AX, 2, 128), 'az', 0, 0, tiled=True)  5.01 us
    all_to_all x1, waiting for transfers between devices, local(): lax.all_to_all(back.reshape(R_AX, 2, 128), 'az', 0, 0, tiled=True)  3.62 us
    ppermute x1, starting transfers between devices, local(): near_left = lax.ppermute(near_right, 'az', higher_az)  3.1 us
    ppermute x1, starting transfers between devices, local(): far_left = lax.ppermute(far_right, 'az', higher_az)  1.99 us
    ppermute x1, waiting for transfers between devices, local(): near_above = lax.ppermute(near_down, 'ax', lower_ax)  1.98 us
  transfers between devices with their start and end apart: 9, of which 4 were waited for; matrix products, arithmetic and copies ran while one was open for 0% of the time, Pallas kernels for 21%

profile of v7, /device:TPU:1, one launch (start us, length us, event | category | flops | bytes accessed | tf_op | source)
XLA Modules:
  0.0 54.6 jit_solution(3667385492932262011)
XLA Ops:
  0.0 0.8 %shard_map.146 = f32[120,128]{1,0:T(8,128)S(1)} custom-call(f32[256,512]{1,0:T(8,128)} %bitcast.16, f32[256,512]{1,0:T(8,128)} %bitcast.22, f32[256,512]{1,0:T(8,128)} %bitcast.28, f32[256,512]{1,0:T(8,128)} %bitcast.34), custom_call_target="tpu_custom_call" | custom-call | flops 1000000 | bytes 3000000 | tf_op jit(solution)/shard_map/pallas_call | solution.py:460
  0.9 3.1 %collective-permute-start = (f32[120,128]{1,0:T(8,128)S(1)}, f32[120,128]{1,0:T(8,128)S(1)}, u32[]{:S(2)}, u32[]{:S(2)}) collective-permute-start(f32[120,128]{1,0:T(8,128)S(1)} %shard_map.146), channel_id=1, source_target_pairs={{0,1},{1,2},{2,3},{3,4},{4,5},{5,6},{6,7},{7,8},{8,9},{9,10},{10,1... | collective-permute-start | bytes 184328 | tf_op jit(solution)/shard_map/ppermute | solution.py:492
  4.0 1.7 %shard_map.145 = (f32[128,128]{1,0:T(8,128)S(1)}, f32[16,256]{1,0:T(8,128)S(1)}, f32[256,128]{1,0:T(8,128)S(1)}, f32[256,128]{1,0:T(8,128)S(1)}, f32[256,128]{1,...) custom-call(s32[32,128]{1,0:T(8,128)S(1)} %copy-done, ...), custom_call_target="tpu_custom_call" | custom-call | flops 1000000 | bytes 3000000 | tf_op jit(solution)/shard_map/pallas_call | solution.py:460
  5.7 0.1 shard_map.147
  5.8 0.9 %shard_map.151 = f32[120,384]{1,0:T(8,128)S(1)} custom-call(f32[256,512]{1,0:T(8,128)} %bitcast.18, f32[256,512]{1,0:T(8,128)} %bitcast.24, f32[256,512]{1,0:T(8,128)} %bitcast.30, f32[256,512]{1,0:T(8,128)} %bitcast.36, f32[216,128]{1,0:T(8,128)S(1)} %get-tuple-element.28.refs_4_), custom_call_target="tpu_custom_call" | custom-call | flops 1000000 | bytes 3000000 | tf_op jit(solution)/shard_map/pallas_call | solution.py:460
  6.7 2.0 %collective-permute-start.3 = (f32[120,384]{1,0:T(8,128)S(1)}, f32[120,384]{1,0:T(8,128)S(1)}, u32[]{:S(2)}, u32[]{:S(2)}) collective-permute-start(f32[120,384]{1,0:T(8,128)S(1)} %shard_map.151), channel_id=1, source_target_pairs={{0,1},{1,2},{2,3},{3,4},{4,5},{5,6},{6,7},{7,8},{8,9},{9,10},{10,1... | collective-permute-start | bytes 552968 | tf_op jit(solution)/shard_map/ppermute | solution.py:515
  8.6 1.3 %collective-permute-start.1 = (f32[216,128]{1,0:T(8,128)S(1)}, f32[216,128]{1,0:T(8,128)S(1)}, u32[]{:S(2)}, u32[]{:S(2)}) collective-permute-start(f32[216,128]{1,0:T(8,128)S(1)} %get-tuple-element.28.refs_4_), channel_id=1, source_target_pairs={{0,64},{64,128},{128,192},{192,0},{1,65},{65,129},{129,193},{193,1... | collective-permute-start | bytes 331784 | tf_op jit(solution)/shard_map/ppermute | solution.py:510
  9.9 1.4 %collective-permute-start.2 = (f32[184,128]{1,0:T(8,128)S(1)}, f32[184,128]{1,0:T(8,128)S(1)}, u32[]{:S(2)}, u32[]{:S(2)}) collective-permute-start(f32[184,128]{1,0:T(8,128)S(1)} %get-tuple-element.29), channel_id=1, source_target_pairs={{64,0},{128,64},{192,128},{0,192},{65,1},{129,65},{193,129},{1,193... | collective-permute-start | bytes 282632 | tf_op jit(solution)/shard_map/ppermute | solution.py:511
  11.4 2.0 %collective-permute-done.2.refs_5_ = f32[184,128]{1,0:T(8,128)S(1)} collective-permute-done((f32[184,128]{1,0:T(8,128)S(1)}, f32[184,128]{1,0:T(8,128)S(1)}, u32[]{:S(2)}, u32[]{:S(2)}) %collective-permute-start.2) | collective-permute-done | bytes 94240 | tf_op jit(solution)/shard_map/ppermute | solution.py:511
  13.4 0.1 collective-permute-done.1.refs_4_
  13.5 1.1 %shard_map.148 = f32[256,128]{1,0:T(8,128)} custom-call(f32[256,128]{1,0:T(8,128)S(1)} %get-tuple-element.24.refs_0_, f32[256,128]{1,0:T(8,128)S(1)} %get-tuple-element.25.refs_1_, f32[256,128]{1,0:T(8,128)S(1)} %get-tuple-element.26.refs_2_, f32[256,128]{1,0:T(8,128)S(1)} %get-tuple-element.27.refs_3_, f32[216,128]{1,0:T(8,128)S(1)} %collective-permute-done.1.refs_4_, ...), custom_call_target="tpu_custom_call" | custom-call | flops 1000000 | bytes 3000000 | tf_op jit(solution)/shard_map/pallas_call | solution.py:460
  14.6 12.5 %all-to-all-start = ((f32[64,4,128]{2,1,0:T(4,128)}), f32[64,4,128]{2,1,0:T(4,128)S(1)}, u32[]{:S(2)}, u32[]{:S(2)}) async-start(f32[64,4,128]{2,1,0:T(4,128)} %bitcast.6), calls=%async_computation | async-start | bytes 262144 | tf_op jit(solution)/shard_map/all_to_all | solution.py:528
  27.2 1.7 %shard_map.152 = (f32[648,128]{1,0:T(8,128)S(1)}, f32[544,128]{1,0:T(8,128)S(1)}) custom-call(f32[256,512]{1,0:T(8,128)} %bitcast.19, f32[256,512]{1,0:T(8,128)} %bitcast.25, f32[256,512]{1,0:T(8,128)} %bitcast.31, f32[256,512]{1,0:T(8,128)} %bitcast.37, f32[120,384]{1,0:T(8,128)S(1)} %collective-permute-done.3.refs_4_.refs_9_), custom_call_target="tpu_custom_call" | custom-call | flops 1000000 | bytes 3000000 | tf_op jit(solution)/shard_map/pallas_call | solution.py:460
  28.9 1.4 %collective-permute-start.4 = (f32[648,128]{1,0:T(8,128)S(1)}, f32[648,128]{1,0:T(8,128)S(1)}, u32[]{:S(2)}, u32[]{:S(2)}) collective-permute-start(f32[648,128]{1,0:T(8,128)S(1)} %get-tuple-element.39), channel_id=1, source_target_pairs={{0,64},{64,128},{128,192},{192,0},{1,65},{65,129},{129,193},{193,1... | collective-permute-start | bytes 995336 | tf_op jit(solution)/shard_map/ppermute | solution.py:530
  30.3 1.4 %collective-permute-start.5 = (f32[544,128]{1,0:T(8,128)S(1)}, f32[544,128]{1,0:T(8,128)S(1)}, u32[]{:S(2)}, u32[]{:S(2)}) collective-permute-start(f32[544,128]{1,0:T(8,128)S(1)} %get-tuple-element.40), channel_id=1, source_target_pairs={{64,0},{128,64},{192,128},{0,192},{65,1},{129,65},{193,129},{1,193... | collective-permute-start | bytes 835592 | tf_op jit(solution)/shard_map/ppermute | solution.py:531
  31.6 5.9 %all-to-all-done = f32[64,4,128]{2,1,0:T(4,128)S(1)} async-done(((f32[64,4,128]{2,1,0:T(4,128)}), f32[64,4,128]{2,1,0:T(4,128)S(1)}, u32[]{:S(2)}, u32[]{:S(2)}) %all-to-all-start) | async-done | bytes 131104 | tf_op jit(solution)/shard_map/all_to_all | solution.py:528
  37.5 1.5 %shard_map.149 = f32[128,128]{1,0:T(8,128)} custom-call(f32[256,128]{1,0:T(8,128)S(1)} %bitcast.11, bf16[80,64]{1,0:T(8,128)(2,1)S(1)} %get-tuple-element.31.first_h, bf16[80,64]{1,0:T(8,128)(2,1)S(1)} %get-tuple-element.32.first_l, bf16[256,512]{1,0:T(8,128)(2,1)S(1)} %get-tuple-element.33.block_h, bf16[256,512]{1,0:T(8,128)(2,1)S(1)} %get-tuple-element.34.block_l, ...), custom_call_target="tpu_custom_call" | custom-call | flops 1000000 | bytes 3000000 | tf_op jit(solution)/shard_map/pallas_call | solution.py:460
  39.0 5.0 %all-to-all-start.1 = ((f32[64,2,128]{2,1,0:T(2,128)}), f32[64,2,128]{2,1,0:T(2,128)S(1)}, u32[]{:S(2)}, u32[]{:S(2)}) async-start(f32[64,2,128]{2,1,0:T(2,128)} %bitcast.8), calls=%async_computation.1 | async-start | bytes 131072 | tf_op jit(solution)/shard_map/all_to_all | solution.py:547
  44.1 1.1 %shard_map.154 = f32[16,512]{1,0:T(8,128)S(1)} custom-call(f32[256,512]{1,0:T(8,128)} %bitcast.20, f32[256,512]{1,0:T(8,128)} %bitcast.26, f32[256,512]{1,0:T(8,128)} %bitcast.32, f32[256,512]{1,0:T(8,128)} %bitcast.38, f32[216,128]{1,0:T(8,128)S(1)} %collective-permute-done.1.refs_4_, f32[184,128]{1,0:T(8,128)S(1)} %collective-permute-done.2.refs_5_, ...), custom_call_target="tpu_custom_call" | custom-call | flops 1000000 | bytes 3000000 | tf_op jit(solution)/shard_map/pallas_call | solution.py:460
  45.2 0.5 collective-permute-start.6
  45.7 0.4 shard_map.150.delta
  46.1 4.1 %shard_map.153 = (f32[256,512]{1,0:T(8,128)}, f32[240,128]{1,0:T(8,128)S(1)}) custom-call(f32[256,512]{1,0:T(8,128)} %bitcast.21, f32[256,512]{1,0:T(8,128)} %bitcast.27, f32[256,512]{1,0:T(8,128)} %bitcast.33, f32[256,512]{1,0:T(8,128)} %bitcast.39, f32[216,128]{1,0:T(8,128)S(1)} %collective-permute-done.1.refs_4_, ...), custom_call_target="tpu_custom_call" | custom-call | flops 4000000 | bytes 12000000 | tf_op jit(solution)/shard_map/pallas_call | solution.py:460
  50.2 3.6 %all-to-all-done.1 = f32[64,2,128]{2,1,0:T(2,128)S(1)} async-done(((f32[64,2,128]{2,1,0:T(2,128)}), f32[64,2,128]{2,1,0:T(2,128)S(1)}, u32[]{:S(2)}, u32[]{:S(2)}) %all-to-all-start.1) | async-done | bytes 65568 | tf_op jit(solution)/shard_map/all_to_all | solution.py:547
  53.8 0.8 %shard_map.155 = f32[256,512]{1,0:T(8,128)} custom-call(f32[128,128]{1,0:T(8,128)S(1)} %bitcast.13, f32[16,256]{1,0:T(8,128)S(1)} %shard_map.150.delta, f32[240,128]{1,0:T(8,128)S(1)} %get-tuple-element.41.swept, f32[16,512]{1,0:T(8,128)S(1)} %collective-permute-done.6.last, f32[256,512]{1,0:T(8,128)} %get-tuple-element.42._), custom_call_target="tpu_custom_call", output_to_operand_aliasing={{}: (4, {})} | custom-call | flops 1000000 | bytes 3000000 | tf_op jit(solution)/shard_map/pallas_call | solution.py:460
  (13 shorter events, 0.0 us)
Async XLA Ops:
  0.0 4.0 %copy-start = (s32[32,128]{1,0:T(8,128)S(1)}, s32[32,128]{1,0:T(8,128)}, u32[]{:S(2)}) copy-start(s32[32,128]{1,0:T(8,128)} %refs_0_.1) | copy-start | bytes 49156
  0.0 4.0 %copy-start.1 = (f32[32,128]{1,0:T(8,128)S(1)}, f32[32,128]{1,0:T(8,128)}, u32[]{:S(2)}) copy-start(f32[32,128]{1,0:T(8,128)} %refs_1_.1) | copy-start | bytes 49156
  0.0 4.0 %copy-start.2 = (s32[32,8]{0,1:T(8,128)S(1)}, s32[32,8]{0,1:T(8,128)}, u32[]{:S(2)}) copy-start(s32[32,8]{0,1:T(8,128)} %param.21) | copy-start | bytes 3076
  0.0 4.0 %copy-start.3 = (s32[32,8]{0,1:T(8,128)S(1)}, s32[32,8]{0,1:T(8,128)}, u32[]{:S(2)}) copy-start(s32[32,8]{0,1:T(8,128)} %param.22) | copy-start | bytes 3076
  0.9 4.8 %collective-permute-start = (f32[120,128]{1,0:T(8,128)S(1)}, f32[120,128]{1,0:T(8,128)S(1)}, u32[]{:S(2)}, u32[]{:S(2)}) collective-permute-start(f32[120,128]{1,0:T(8,128)S(1)} %shard_map.146), channel_id=1, source_target_pairs={{0,1},{1,2},{2,3},{3,4},{4,5},{5,6},{6,7},{7,8},{8,9},{9,10},{10,1... | collective-permute-start | bytes 184328 | tf_op jit(solution)/shard_map/ppermute | solution.py:492
  6.7 20.5 %collective-permute-start.3 = (f32[120,384]{1,0:T(8,128)S(1)}, f32[120,384]{1,0:T(8,128)S(1)}, u32[]{:S(2)}, u32[]{:S(2)}) collective-permute-start(f32[120,384]{1,0:T(8,128)S(1)} %shard_map.151), channel_id=1, source_target_pairs={{0,1},{1,2},{2,3},{3,4},{4,5},{5,6},{6,7},{7,8},{8,9},{9,10},{10,1... | collective-permute-start | bytes 552968 | tf_op jit(solution)/shard_map/ppermute | solution.py:515
  8.6 4.9 %collective-permute-start.1 = (f32[216,128]{1,0:T(8,128)S(1)}, f32[216,128]{1,0:T(8,128)S(1)}, u32[]{:S(2)}, u32[]{:S(2)}) collective-permute-start(f32[216,128]{1,0:T(8,128)S(1)} %get-tuple-element.28.refs_4_), channel_id=1, source_target_pairs={{0,64},{64,128},{128,192},{192,0},{1,65},{65,129},{129,193},{193,1... | collective-permute-start | bytes 331784 | tf_op jit(solution)/shard_map/ppermute | solution.py:510
  9.9 3.4 %collective-permute-start.2 = (f32[184,128]{1,0:T(8,128)S(1)}, f32[184,128]{1,0:T(8,128)S(1)}, u32[]{:S(2)}, u32[]{:S(2)}) collective-permute-start(f32[184,128]{1,0:T(8,128)S(1)} %get-tuple-element.29), channel_id=1, source_target_pairs={{64,0},{128,64},{192,128},{0,192},{65,1},{129,65},{193,129},{1,193... | collective-permute-start | bytes 282632 | tf_op jit(solution)/shard_map/ppermute | solution.py:511
  14.6 22.9 %all-to-all-start = ((f32[64,4,128]{2,1,0:T(4,128)}), f32[64,4,128]{2,1,0:T(4,128)S(1)}, u32[]{:S(2)}, u32[]{:S(2)}) async-start(f32[64,4,128]{2,1,0:T(4,128)} %bitcast.6), calls=%async_computation | async-start | bytes 262144 | tf_op jit(solution)/shard_map/all_to_all | solution.py:528
  28.9 15.2 %collective-permute-start.4 = (f32[648,128]{1,0:T(8,128)S(1)}, f32[648,128]{1,0:T(8,128)S(1)}, u32[]{:S(2)}, u32[]{:S(2)}) collective-permute-start(f32[648,128]{1,0:T(8,128)S(1)} %get-tuple-element.39), channel_id=1, source_target_pairs={{0,64},{64,128},{128,192},{192,0},{1,65},{65,129},{129,193},{193,1... | collective-permute-start | bytes 995336 | tf_op jit(solution)/shard_map/ppermute | solution.py:530
  30.3 13.8 %collective-permute-start.5 = (f32[544,128]{1,0:T(8,128)S(1)}, f32[544,128]{1,0:T(8,128)S(1)}, u32[]{:S(2)}, u32[]{:S(2)}) collective-permute-start(f32[544,128]{1,0:T(8,128)S(1)} %get-tuple-element.40), channel_id=1, source_target_pairs={{64,0},{128,64},{192,128},{0,192},{65,1},{129,65},{193,129},{1,193... | collective-permute-start | bytes 835592 | tf_op jit(solution)/shard_map/ppermute | solution.py:531
  39.0 14.8 %all-to-all-start.1 = ((f32[64,2,128]{2,1,0:T(2,128)}), f32[64,2,128]{2,1,0:T(2,128)S(1)}, u32[]{:S(2)}, u32[]{:S(2)}) async-start(f32[64,2,128]{2,1,0:T(2,128)} %bitcast.8), calls=%async_computation.1 | async-start | bytes 131072 | tf_op jit(solution)/shard_map/all_to_all | solution.py:547
  45.2 8.6 %collective-permute-start.6 = (f32[16,512]{1,0:T(8,128)S(1)}, f32[16,512]{1,0:T(8,128)S(1)}, u32[]{:S(2)}, u32[]{:S(2)}) collective-permute-start(f32[16,512]{1,0:T(8,128)S(1)} %shard_map.154), channel_id=1, source_target_pairs={{1,0},{2,1},{3,2},{4,3},{5,4},{6,5},{7,6},{8,7},{9,8},{10,9},{11,1... | collective-permute-start | bytes 98312 | tf_op jit(solution)/shard_map/ppermute | solution.py:537

commit v8 on v7

--- a/solution.py
+++ b/solution.py
@@ -65,8 +65,16 @@
     return copies
 
 
+def bring_tiles(*refs):
+    fields, tiles, (right, semaphores) = refs[:4], refs[4:8], refs[8:]
+    copies = copy_all([(f.at[:, pl.ds(0, 128)], tile) for f, tile in zip(fields, tiles)], semaphores, 4)
+    pack_columns(*fields, right, semaphores)
+    for copy in copies:
+        copy.wait()
+
+
 def pack_columns(*refs):
-    fields, (right, semaphores) = refs[:4], refs[-2:]
+    fields, (right, semaphores) = refs[:4], refs[4:]
     lanes = right.shape[1]
     pairs, row = [], 0
     for field, count in zip(fields, LEFT_COUNT):
@@ -322,9 +330,8 @@
 
 
 def crossing_kernel(*refs):
-    (code, width, reader, landing), fields, tables, (out, volume_out) = refs[:4], refs[4:8], refs[8:15], refs[15:17]
-    sources = [f.at[:, pl.ds(0, 128)] for f in fields] + list(tables)
-    copies = copy_all(zip(sources, refs[17:28]), refs[28])
+    (code, width, reader, landing), tables, (out, volume_out) = refs[:4], refs[4:11], refs[12:14]
+    copies = copy_all(zip(tables, refs[14:21]), refs[21])
     iota = functools.partial(lax.broadcasted_iota, jnp.int32)
     volume = plic_volume(code[...], width[...])
     both = jnp.concatenate([reader[...].astype(F32), landing[...].astype(F32)], axis=0).astype(BF16)
@@ -491,28 +498,29 @@
     (near_right,) = call(pack_columns, fields, [VMEM((len(LEFT) * 8, 128), F32)], [DMA((4,))])
     near_left = lax.ppermute(near_right, "az", higher_az)
 
-    tables = filter_tables()
-    crossing, volume, *held = call(
-        crossing_kernel,
-        [plane_code, strip_width, tile_reader.T, landing_column.T, *fields, *((jnp.asarray(t), HBM) for t in tables)],
-        [VMEM((2 * R_AX, 128), F32), VMEM((XR, ROWS), F32)]
-        + [VMEM((ROWS, 128), F32)] * 4
-        + [VMEM(t.shape, t.dtype) for t in tables],
-        [DMA((4 + len(tables),))],
-    )
-    near_tiles, held_tables = held[:4], held[4:]
-
+    *near_tiles, far_right = call(
+        bring_tiles,
+        fields,
+        [VMEM((ROWS, 128), F32)] * 4 + [VMEM((len(LEFT) * 8, NR - 128), F32)],
+        [DMA((8,))],
+    )
+    far_left = lax.ppermute(far_right, "az", higher_az)
     near_up, near_down = call(
         pack_near_planes,
         [*near_tiles, near_left],
         [VMEM((NEAR_BELOW_ROWS, 128), F32), VMEM((NEAR_ABOVE_ROWS, 128), F32)],
     )
+    tables = filter_tables()
+    crossing, volume, *held_tables = call(
+        crossing_kernel,
+        [plane_code, strip_width, tile_reader.T, landing_column.T]
+        + [(jnp.asarray(t), HBM) for t in tables]
+        + [(near_up, pl.ANY)],
+        [VMEM((2 * R_AX, 128), F32), VMEM((XR, ROWS), F32)] + [VMEM(t.shape, t.dtype) for t in tables],
+        [DMA((len(tables),))],
+    )
     near_below = lax.ppermute(near_up, "ax", higher_ax)
     near_above = lax.ppermute(near_down, "ax", lower_ax)
-    (far_right,) = call(
-        pack_columns, [*fields, (near_up, pl.ANY)], [VMEM((len(LEFT) * 8, NR - 128), F32)], [DMA((4,))]
-    )
-    far_left = lax.ppermute(far_right, "az", higher_az)
     far_up, far_down = call(
         pack_far_planes,
         [*fields, far_left],

time: 55.1 us -> 54 us (0.980)
  waiting for transfers between devices: 11.6 us -> 10.5 us
    all_to_all x1, starting transfers between devices: 12.5 us -> 14.5 us  [local(): lax.all_to_all(send.reshape(R_AX, 4, 128), 'az', 0, 0, tiled=True)]
    ppermute x1, starting transfers between devices: 1.99 us -> 0.1 us  [local(): far_left = lax.ppermute(far_right, 'az', higher_az)]
    ppermute x1, waiting for transfers between devices: 1.98 us -> 0.87 us  [local(): near_above = lax.ppermute(near_down, 'ax', lower_ax)]
  transfers between devices with their start and end apart: 9 -> 9, of which waited for: 4 -> 4; matrix products, arithmetic and copies ran while one was open for 0% -> 0% of each run, Pallas kernels for 21% -> 23%
where the time goes in v8:
time: 54 us; the launch traced here: 53.6 us
  starting transfers between devices  28.9 us (54%)
  Pallas kernels  14 us (26%)
  waiting for transfers between devices  10.5 us (19%)
    all_to_all x1, starting transfers between devices, local(): lax.all_to_all(send.reshape(R_AX, 4, 128), 'az', 0, 0, tiled=True)  14.5 us
    pallas_call x11, Pallas kernels, call(): pl.pallas_call(kernel, in_specs=specs, out_specs=out_specs, out_shape=lis...  14 us
    all_to_all x1, waiting for transfers between devices, local(): lax.all_to_all(send.reshape(R_AX, 4, 128), 'az', 0, 0, tiled=True)  5.87 us
    all_to_all x1, starting transfers between devices, local(): lax.all_to_all(back.reshape(R_AX, 2, 128), 'az', 0, 0, tiled=True)  5.01 us
    all_to_all x1, waiting for transfers between devices, local(): lax.all_to_all(back.reshape(R_AX, 2, 128), 'az', 0, 0, tiled=True)  3.61 us
    ppermute x1, starting transfers between devices, local(): near_left = lax.ppermute(near_right, 'az', higher_az)  3.1 us
    ppermute x1, starting transfers between devices, local(): near_above = lax.ppermute(near_down, 'ax', lower_ax)  1.53 us
    ppermute x1, starting transfers between devices, local(): far_above = lax.ppermute(far_down, 'ax', lower_ax)  1.39 us
  transfers between devices with their start and end apart: 9, of which 4 were waited for; matrix products, arithmetic and copies ran while one was open for 0% of the time, Pallas kernels for 23%

profile of v8, /device:TPU:1, one launch (start us, length us, event | category | flops | bytes accessed | tf_op | source)
XLA Modules:
  0.0 53.6 jit_solution(18273840368576380006)
XLA Ops:
  0.0 0.8 %shard_map.146 = f32[120,128]{1,0:T(8,128)S(1)} custom-call(f32[256,512]{1,0:T(8,128)} %bitcast.16, f32[256,512]{1,0:T(8,128)} %bitcast.21, f32[256,512]{1,0:T(8,128)} %bitcast.26, f32[256,512]{1,0:T(8,128)} %bitcast.31), custom_call_target="tpu_custom_call" | custom-call | flops 1000000 | bytes 3000000 | tf_op jit(solution)/shard_map/pallas_call | solution.py:467
  0.8 3.1 %collective-permute-start = (f32[120,128]{1,0:T(8,128)S(1)}, f32[120,128]{1,0:T(8,128)S(1)}, u32[]{:S(2)}, u32[]{:S(2)}) collective-permute-start(f32[120,128]{1,0:T(8,128)S(1)} %shard_map.146), channel_id=1, source_target_pairs={{0,1},{1,2},{2,3},{3,4},{4,5},{5,6},{6,7},{7,8},{8,9},{9,10},{10,1... | collective-permute-start | bytes 184328 | tf_op jit(solution)/shard_map/ppermute | solution.py:499
  3.9 1.2 %shard_map.145 = (f32[256,128]{1,0:T(8,128)S(1)}, f32[256,128]{1,0:T(8,128)S(1)}, f32[256,128]{1,0:T(8,128)S(1)}, f32[256,128]{1,0:T(8,128)S(1)}, f32[120,384]{1,0:T(8,128)S(1)}) custom-call(f32[256,512]{1,0:T(8,128)} %bitcast.17, f32[256,512]{1,0:T(8,128)} %bitcast.22, f32[256,512]{1,0:T(8,128)} %bitcast.27, f32[256,512]{1,0:T(8,128)} %bitcast.32), custom_call_target="tpu_custom_call" | custom-call | flops 1000000 | bytes 3000000 | tf_op jit(solution)/shard_map/pallas_call | solution.py:467
  5.1 0.1 collective-permute-start.3
  5.2 0.1 shard_map.147
  5.3 1.4 %collective-permute-start.1 = (f32[216,128]{1,0:T(8,128)S(1)}, f32[216,128]{1,0:T(8,128)S(1)}, u32[]{:S(2)}, u32[]{:S(2)}) collective-permute-start(f32[216,128]{1,0:T(8,128)S(1)} %get-tuple-element.29.refs_11_), channel_id=1, source_target_pairs={{0,64},{64,128},{128,192},{192,0},{1,65},{65,129},{129,193},{193,1... | collective-permute-start | bytes 331784 | tf_op jit(solution)/shard_map/ppermute | solution.py:522
  6.7 1.5 %collective-permute-start.2 = (f32[184,128]{1,0:T(8,128)S(1)}, f32[184,128]{1,0:T(8,128)S(1)}, u32[]{:S(2)}, u32[]{:S(2)}) collective-permute-start(f32[184,128]{1,0:T(8,128)S(1)} %get-tuple-element.30), channel_id=1, source_target_pairs={{64,0},{128,64},{192,128},{0,192},{65,1},{129,65},{193,129},{1,193... | collective-permute-start | bytes 282632 | tf_op jit(solution)/shard_map/ppermute | solution.py:523
  8.2 1.3 %shard_map.148 = (f32[128,128]{1,0:T(8,128)S(1)}, f32[16,256]{1,0:T(8,128)S(1)}, bf16[80,64]{1,0:T(8,128)(2,1)S(1)}, bf16[80,64]{1,0:T(8,128)(2,1)S(1)}, bf16[25...) custom-call(s32[32,128]{1,0:T(8,128)S(1)} %copy-done, ...), custom_call_target="tpu_custom_call" | custom-call | flops 1000000 | bytes 3000000 | tf_op jit(solution)/shard_map/pallas_call | solution.py:467
  9.5 0.9 %collective-permute-done.2.refs_5_ = f32[184,128]{1,0:T(8,128)S(1)} collective-permute-done((f32[184,128]{1,0:T(8,128)S(1)}, f32[184,128]{1,0:T(8,128)S(1)}, u32[]{:S(2)}, u32[]{:S(2)}) %collective-permute-start.2) | collective-permute-done | bytes 94240 | tf_op jit(solution)/shard_map/ppermute | solution.py:523
  10.4 0.2 collective-permute-done.1.refs_4_
  10.5 1.1 %shard_map.149 = f32[256,128]{1,0:T(8,128)} custom-call(f32[256,128]{1,0:T(8,128)S(1)} %get-tuple-element.25.refs_0_, f32[256,128]{1,0:T(8,128)S(1)} %get-tuple-element.26.refs_1_, f32[256,128]{1,0:T(8,128)S(1)} %get-tuple-element.27.refs_2_, f32[256,128]{1,0:T(8,128)S(1)} %get-tuple-element.28.refs_3_, f32[216,128]{1,0:T(8,128)S(1)} %collective-permute-done.1.refs_4_, ...), custom_call_target="tpu_custom_call" | custom-call | flops 1000000 | bytes 3000000 | tf_op jit(solution)/shard_map/pallas_call | solution.py:467
  11.6 14.5 %all-to-all-start = ((f32[64,4,128]{2,1,0:T(4,128)}), f32[64,4,128]{2,1,0:T(4,128)S(1)}, u32[]{:S(2)}, u32[]{:S(2)}) async-start(f32[64,4,128]{2,1,0:T(4,128)} %bitcast.6), calls=%async_computation | async-start | bytes 262144 | tf_op jit(solution)/shard_map/all_to_all | solution.py:536
  26.1 1.7 %shard_map.152 = (f32[648,128]{1,0:T(8,128)S(1)}, f32[544,128]{1,0:T(8,128)S(1)}) custom-call(f32[256,512]{1,0:T(8,128)} %bitcast.18, f32[256,512]{1,0:T(8,128)} %bitcast.23, f32[256,512]{1,0:T(8,128)} %bitcast.28, f32[256,512]{1,0:T(8,128)} %bitcast.33, f32[120,384]{1,0:T(8,128)S(1)} %collective-permute-done.3.refs_4_.refs_9_), custom_call_target="tpu_custom_call" | custom-call | flops 1000000 | bytes 3000000 | tf_op jit(solution)/shard_map/pallas_call | solution.py:467
  27.9 1.4 %collective-permute-start.4 = (f32[648,128]{1,0:T(8,128)S(1)}, f32[648,128]{1,0:T(8,128)S(1)}, u32[]{:S(2)}, u32[]{:S(2)}) collective-permute-start(f32[648,128]{1,0:T(8,128)S(1)} %get-tuple-element.41), channel_id=1, source_target_pairs={{0,64},{64,128},{128,192},{192,0},{1,65},{65,129},{129,193},{193,1... | collective-permute-start | bytes 995336 | tf_op jit(solution)/shard_map/ppermute | solution.py:538
  29.2 1.4 %collective-permute-start.5 = (f32[544,128]{1,0:T(8,128)S(1)}, f32[544,128]{1,0:T(8,128)S(1)}, u32[]{:S(2)}, u32[]{:S(2)}) collective-permute-start(f32[544,128]{1,0:T(8,128)S(1)} %get-tuple-element.42), channel_id=1, source_target_pairs={{64,0},{128,64},{192,128},{0,192},{65,1},{129,65},{193,129},{1,193... | collective-permute-start | bytes 835592 | tf_op jit(solution)/shard_map/ppermute | solution.py:539
  30.6 5.9 %all-to-all-done = f32[64,4,128]{2,1,0:T(4,128)S(1)} async-done(((f32[64,4,128]{2,1,0:T(4,128)}), f32[64,4,128]{2,1,0:T(4,128)S(1)}, u32[]{:S(2)}, u32[]{:S(2)}) %all-to-all-start) | async-done | bytes 131104 | tf_op jit(solution)/shard_map/all_to_all | solution.py:536
  36.5 1.5 %shard_map.150 = f32[128,128]{1,0:T(8,128)} custom-call(f32[256,128]{1,0:T(8,128)S(1)} %bitcast.11, bf16[80,64]{1,0:T(8,128)(2,1)S(1)} %get-tuple-element.32.first_h, bf16[80,64]{1,0:T(8,128)(2,1)S(1)} %get-tuple-element.33.first_l, bf16[256,512]{1,0:T(8,128)(2,1)S(1)} %get-tuple-element.34.block_h, bf16[256,512]{1,0:T(8,128)(2,1)S(1)} %get-tuple-element.35.block_l, ...), custom_call_target="tpu_custom_call" | custom-call | flops 1000000 | bytes 3000000 | tf_op jit(solution)/shard_map/pallas_call | solution.py:467
  38.0 5.0 %all-to-all-start.1 = ((f32[64,2,128]{2,1,0:T(2,128)}), f32[64,2,128]{2,1,0:T(2,128)S(1)}, u32[]{:S(2)}, u32[]{:S(2)}) async-start(f32[64,2,128]{2,1,0:T(2,128)} %bitcast.8), calls=%async_computation.1 | async-start | bytes 131072 | tf_op jit(solution)/shard_map/all_to_all | solution.py:555
  43.0 1.1 %shard_map.154 = f32[16,512]{1,0:T(8,128)S(1)} custom-call(f32[256,512]{1,0:T(8,128)} %bitcast.19, f32[256,512]{1,0:T(8,128)} %bitcast.24, f32[256,512]{1,0:T(8,128)} %bitcast.29, f32[256,512]{1,0:T(8,128)} %bitcast.34, f32[216,128]{1,0:T(8,128)S(1)} %collective-permute-done.1.refs_4_, f32[184,128]{1,0:T(8,128)S(1)} %collective-permute-done.2.refs_5_, ...), custom_call_target="tpu_custom_call" | custom-call | flops 1000000 | bytes 3000000 | tf_op jit(solution)/shard_map/pallas_call | solution.py:467
  44.2 0.5 collective-permute-start.6
  44.7 0.4 shard_map.151.delta
  45.0 4.1 %shard_map.153 = (f32[256,512]{1,0:T(8,128)}, f32[240,128]{1,0:T(8,128)S(1)}) custom-call(f32[256,512]{1,0:T(8,128)} %bitcast.20, f32[256,512]{1,0:T(8,128)} %bitcast.25, f32[256,512]{1,0:T(8,128)} %bitcast.30, f32[256,512]{1,0:T(8,128)} %bitcast.35, f32[216,128]{1,0:T(8,128)S(1)} %collective-permute-done.1.refs_4_, ...), custom_call_target="tpu_custom_call" | custom-call | flops 4000000 | bytes 12000000 | tf_op jit(solution)/shard_map/pallas_call | solution.py:467
  49.2 3.6 %all-to-all-done.1 = f32[64,2,128]{2,1,0:T(2,128)S(1)} async-done(((f32[64,2,128]{2,1,0:T(2,128)}), f32[64,2,128]{2,1,0:T(2,128)S(1)}, u32[]{:S(2)}, u32[]{:S(2)}) %all-to-all-start.1) | async-done | bytes 65568 | tf_op jit(solution)/shard_map/all_to_all | solution.py:555
  52.8 0.8 %shard_map.155 = f32[256,512]{1,0:T(8,128)} custom-call(f32[128,128]{1,0:T(8,128)S(1)} %bitcast.13, f32[16,256]{1,0:T(8,128)S(1)} %shard_map.151.delta, f32[240,128]{1,0:T(8,128)S(1)} %get-tuple-element.43.swept, f32[16,512]{1,0:T(8,128)S(1)} %collective-permute-done.6.last, f32[256,512]{1,0:T(8,128)} %get-tuple-element.44._), custom_call_target="tpu_custom_call", output_to_operand_aliasing={{}: (4, {})} | custom-call | flops 1000000 | bytes 3000000 | tf_op jit(solution)/shard_map/pallas_call | solution.py:467
  (13 shorter events, 0.1 us)
Async XLA Ops:
  0.8 4.4 %collective-permute-start = (f32[120,128]{1,0:T(8,128)S(1)}, f32[120,128]{1,0:T(8,128)S(1)}, u32[]{:S(2)}, u32[]{:S(2)}) collective-permute-start(f32[120,128]{1,0:T(8,128)S(1)} %shard_map.146), channel_id=1, source_target_pairs={{0,1},{1,2},{2,3},{3,4},{4,5},{5,6},{6,7},{7,8},{8,9},{9,10},{10,1... | collective-permute-start | bytes 184328 | tf_op jit(solution)/shard_map/ppermute | solution.py:499
  5.1 21.0 %collective-permute-start.3 = (f32[120,384]{1,0:T(8,128)S(1)}, f32[120,384]{1,0:T(8,128)S(1)}, u32[]{:S(2)}, u32[]{:S(2)}) collective-permute-start(f32[120,384]{1,0:T(8,128)S(1)} %get-tuple-element.40), channel_id=1, source_target_pairs={{0,1},{1,2},{2,3},{3,4},{4,5},{5,6},{6,7},{7,8},{8,9},{9,10},{10,1... | collective-permute-start | bytes 552968 | tf_op jit(solution)/shard_map/ppermute | solution.py:507
  5.2 3.0 %copy-start = (s32[32,128]{1,0:T(8,128)S(1)}, s32[32,128]{1,0:T(8,128)}, u32[]{:S(2)}) copy-start(s32[32,128]{1,0:T(8,128)} %refs_0_.1) | copy-start | bytes 49156
  5.2 3.0 %copy-start.1 = (f32[32,128]{1,0:T(8,128)S(1)}, f32[32,128]{1,0:T(8,128)}, u32[]{:S(2)}) copy-start(f32[32,128]{1,0:T(8,128)} %refs_1_.1) | copy-start | bytes 49156
  5.2 3.0 %copy-start.3 = (s32[32,8]{0,1:T(8,128)S(1)}, s32[32,8]{0,1:T(8,128)}, u32[]{:S(2)}) copy-start(s32[32,8]{0,1:T(8,128)} %param.22) | copy-start | bytes 3076
  5.3 2.9 %copy-start.2 = (s32[32,8]{0,1:T(8,128)S(1)}, s32[32,8]{0,1:T(8,128)}, u32[]{:S(2)}) copy-start(s32[32,8]{0,1:T(8,128)} %param.21) | copy-start | bytes 3076
  5.3 5.2 %collective-permute-start.1 = (f32[216,128]{1,0:T(8,128)S(1)}, f32[216,128]{1,0:T(8,128)S(1)}, u32[]{:S(2)}, u32[]{:S(2)}) collective-permute-start(f32[216,128]{1,0:T(8,128)S(1)} %get-tuple-element.29.refs_11_), channel_id=1, source_target_pairs={{0,64},{64,128},{128,192},{192,0},{1,65},{65,129},{129,193},{193,1... | collective-permute-start | bytes 331784 | tf_op jit(solution)/shard_map/ppermute | solution.py:522
  6.7 3.7 %collective-permute-start.2 = (f32[184,128]{1,0:T(8,128)S(1)}, f32[184,128]{1,0:T(8,128)S(1)}, u32[]{:S(2)}, u32[]{:S(2)}) collective-permute-start(f32[184,128]{1,0:T(8,128)S(1)} %get-tuple-element.30), channel_id=1, source_target_pairs={{64,0},{128,64},{192,128},{0,192},{65,1},{129,65},{193,129},{1,193... | collective-permute-start | bytes 282632 | tf_op jit(solution)/shard_map/ppermute | solution.py:523
  11.6 24.9 %all-to-all-start = ((f32[64,4,128]{2,1,0:T(4,128)}), f32[64,4,128]{2,1,0:T(4,128)S(1)}, u32[]{:S(2)}, u32[]{:S(2)}) async-start(f32[64,4,128]{2,1,0:T(4,128)} %bitcast.6), calls=%async_computation | async-start | bytes 262144 | tf_op jit(solution)/shard_map/all_to_all | solution.py:536
  27.9 15.2 %collective-permute-start.4 = (f32[648,128]{1,0:T(8,128)S(1)}, f32[648,128]{1,0:T(8,128)S(1)}, u32[]{:S(2)}, u32[]{:S(2)}) collective-permute-start(f32[648,128]{1,0:T(8,128)S(1)} %get-tuple-element.41), channel_id=1, source_target_pairs={{0,64},{64,128},{128,192},{192,0},{1,65},{65,129},{129,193},{193,1... | collective-permute-start | bytes 995336 | tf_op jit(solution)/shard_map/ppermute | solution.py:538
  29.2 13.8 %collective-permute-start.5 = (f32[544,128]{1,0:T(8,128)S(1)}, f32[544,128]{1,0:T(8,128)S(1)}, u32[]{:S(2)}, u32[]{:S(2)}) collective-permute-start(f32[544,128]{1,0:T(8,128)S(1)} %get-tuple-element.42), channel_id=1, source_target_pairs={{64,0},{128,64},{192,128},{0,192},{65,1},{129,65},{193,129},{1,193... | collective-permute-start | bytes 835592 | tf_op jit(solution)/shard_map/ppermute | solution.py:539
  38.0 14.8 %all-to-all-start.1 = ((f32[64,2,128]{2,1,0:T(2,128)}), f32[64,2,128]{2,1,0:T(2,128)S(1)}, u32[]{:S(2)}, u32[]{:S(2)}) async-start(f32[64,2,128]{2,1,0:T(2,128)} %bitcast.8), calls=%async_computation.1 | async-start | bytes 131072 | tf_op jit(solution)/shard_map/all_to_all | solution.py:555
  44.2 5.0 %collective-permute-start.6 = (f32[16,512]{1,0:T(8,128)S(1)}, f32[16,512]{1,0:T(8,128)S(1)}, u32[]{:S(2)}, u32[]{:S(2)}) collective-permute-start(f32[16,512]{1,0:T(8,128)S(1)} %shard_map.154), channel_id=1, source_target_pairs={{1,0},{2,1},{3,2},{4,3},{5,4},{6,5},{7,6},{8,7},{9,8},{10,9},{11,1... | collective-permute-start | bytes 98312 | tf_op jit(solution)/shard_map/ppermute | solution.py:545

commit v9 on v8

--- a/solution.py
+++ b/solution.py
@@ -44,8 +44,8 @@
 
 NEAR_BELOW, NEAR_BELOW_ROWS = halo_layout(BELOW, (0,))
 NEAR_ABOVE, NEAR_ABOVE_ROWS = halo_layout(ABOVE, (0,))
-FAR_BELOW, FAR_BELOW_ROWS = halo_layout(BELOW, range(1, TILES))
-FAR_ABOVE, FAR_ABOVE_ROWS = halo_layout(ABOVE, range(1, TILES))
+FAR_BELOW, FAR_BELOW_ROWS = halo_layout(BELOW, range(TILES))
+FAR_ABOVE, FAR_ABOVE_ROWS = halo_layout(ABOVE, range(TILES))
 
 
 def plane_slot(plane):
@@ -89,34 +89,67 @@
     for tile, field, plane, count, row in entries:
         for at in range(count):
             origin = LEFT.index((field, at - count)) * 8 + plane + shift
-            out[row + at : row + at + 1, :] = left[origin : origin + 1, pl.ds(max(tile - 1, 0) * 128, 128)]
+            part, lane = (left[0], 0) if tile == 0 else (left[1], tile * 128 - 128)
+            out[row + at : row + at + 1, :] = part[origin : origin + 1, pl.ds(lane, 128)]
         out[row + count : row + count + COLS, :] = load(tile, field, plane + shift)
     used = entries[-1][4] + entries[-1][3] + COLS
     if used < out.shape[0]:
         out[used:, :] = jnp.zeros((out.shape[0] - used, 128), F32)
 
 
+BLOCK = COLS + 4
+UP_ROWS, DOWN_ROWS = 4 * BLOCK, 112
+
+
+def squeeze(entries, flat, out):
+    lane = lax.broadcasted_iota(jnp.int32, (BLOCK, 128), 1)
+    planes = [flat[row + count - 4 : row + count + COLS, :] for _, _, _, count, row in entries]
+    last = planes[-1] if len(planes) % 2 else jnp.zeros((BLOCK, 128), F32)
+    for k, plane in enumerate(planes[:-1]):
+        last = jnp.where(lane == 64 + k, pltpu.roll(plane, k, 1) if k else plane, last)
+    blocks = [jnp.where(lane < 64, a, pltpu.roll(b, 64, 1)) for a, b in zip(planes[0::2], planes[1::2])] + [last]
+    for k, values in enumerate(blocks):
+        out[k * BLOCK : (k + 1) * BLOCK, :] = values
+    if len(blocks) * BLOCK < out.shape[0]:
+        out[len(blocks) * BLOCK :, :] = jnp.zeros((out.shape[0] - len(blocks) * BLOCK, 128), F32)
+
+
+def unfold(entries, packed, flat):
+    lane = lax.broadcasted_iota(jnp.int32, (BLOCK, 128), 1)
+    at = len(entries) // 2 * BLOCK
+    last = packed[at : at + BLOCK, :]
+    for k, (_, _, _, count, row) in enumerate(entries):
+        values = packed[k // 2 * BLOCK : (k // 2 + 1) * BLOCK, :]
+        if k % 2:
+            values = pltpu.roll(values, 64, 1)
+        if k < len(entries) - 1:
+            values = jnp.where(lane == 64, pltpu.roll(last, 128 - k, 1) if k else last, values)
+        flat[row : row + count + COLS, :] = values[4 - count :]
+
+
 def pack_near_planes(*refs):
-    tiles, (left, up, down) = refs[:4], refs[4:]
+    tiles, (left, up, down, flat_up, flat_down) = refs[:4], refs[4:]
 
     def load(_, field, plane):
         return tiles[field][pl.ds(plane, COLS, stride=PLANES), :]
 
-    pack_planes(NEAR_BELOW, up, PLANES, load, left)
-    pack_planes(NEAR_ABOVE, down, -PLANES, load, left)
+    pack_planes(NEAR_BELOW, flat_up, PLANES, load, [left])
+    pack_planes(NEAR_ABOVE, flat_down, -PLANES, load, [left])
+    squeeze(NEAR_BELOW, flat_up, up)
+    squeeze(NEAR_ABOVE, flat_down, down)
 
 
 def pack_far_planes(*refs):
-    fields, (left, up, down, *tiles, semaphores) = refs[:4], refs[4:]
+    fields, left, (up, down, *tiles, semaphores) = refs[:4], refs[4:6], refs[6:]
     pairs = []
     for field, tile in zip(fields, tiles):
-        for k in range(1, TILES):
-            pairs.append((field.at[:, pl.ds(k * 128, 128)], tile.at[pl.ds((k - 1) * ROWS, ROWS), :]))
+        for k in range(TILES):
+            pairs.append((field.at[:, pl.ds(k * 128, 128)], tile.at[pl.ds(k * ROWS, ROWS), :]))
     for copy in copy_all(pairs, semaphores):
         copy.wait()
 
     def load(tile, field, plane):
-        return tiles[field][pl.ds((tile - 1) * ROWS + plane, COLS, stride=PLANES), :]
+        return tiles[field][pl.ds(tile * ROWS + plane, COLS, stride=PLANES), :]
 
     pack_planes(FAR_BELOW, up, PLANES, load, left)
     pack_planes(FAR_ABOVE, down, -PLANES, load, left)
@@ -223,9 +256,12 @@
 
 
 def near_kernel(*refs):
-    fields, (below, above, left, crossing, out), halos, swept = refs[:4], refs[4:9], refs[9:13], refs[13]
-    fill_halos(halos, NEAR_BELOW, below)
-    fill_halos(halos, NEAR_ABOVE, above)
+    fields, (below, above, left, crossing, out), halos = refs[:4], refs[4:9], refs[9:13]
+    swept, flat_below, flat_above = refs[13:]
+    unfold(NEAR_BELOW, below, flat_below)
+    unfold(NEAR_ABOVE, above, flat_above)
+    fill_halos(halos, NEAR_BELOW, flat_below)
+    fill_halos(halos, NEAR_ABOVE, flat_above)
 
     def store(column, values):
         swept[row_slice(column + 2), :] = values
@@ -238,14 +274,14 @@
     out[pl.ds(3, R_AX, stride=4), :] = crossing[R_AX:, :]
 
 
-def fill_far_halos(halos, near_below, near_above, below, above):
-    for entries, source in ((NEAR_BELOW, near_below), (NEAR_ABOVE, near_above), (FAR_BELOW, below), (FAR_ABOVE, above)):
-        fill_halos(halos, entries, source)
+def fill_far_halos(halos, below, above):
+    fill_halos(halos, FAR_BELOW, below)
+    fill_halos(halos, FAR_ABOVE, above)
 
 
 def far_first_kernel(*refs):
-    sources, planes, left, out, halos = refs[:4], refs[4:8], refs[8:10], refs[10], refs[11:15]
-    fields, semaphores = refs[15:19], refs[19]
+    sources, planes, left, out, halos = refs[:4], refs[4:6], refs[6:8], refs[8], refs[9:13]
+    fields, semaphores = refs[13:17], refs[17]
     copies = copy_all([(f.at[pl.ds(0, 16), :], held) for f, held in zip(sources, fields)], semaphores)
     fill_far_halos(halos, *planes)
     for copy in copies:
@@ -258,8 +294,8 @@
 
 
 def far_kernel(*refs):
-    sources, planes, left, (result, first_tile), halos = refs[:4], refs[4:8], refs[8:10], refs[10:12], refs[12:16]
-    fields, (out, semaphores) = refs[16:20], refs[20:]
+    sources, planes, left, (result, first_tile), halos = refs[:4], refs[4:6], refs[6:8], refs[8:10], refs[10:14]
+    fields, (out, semaphores) = refs[14:18], refs[18:]
     arrive = [(0, 80), (80, 144), (144, 208), (208, 256)]
     leave = [(0, 64), (64, 128), (128, 192), (192, KEPT)]
     incoming = [
@@ -505,10 +541,12 @@
         [DMA((8,))],
     )
     far_left = lax.ppermute(far_right, "az", higher_az)
+    flat = [VMEM((NEAR_BELOW_ROWS, 128), F32), VMEM((NEAR_ABOVE_ROWS, 128), F32)]
     near_up, near_down = call(
         pack_near_planes,
         [*near_tiles, near_left],
-        [VMEM((NEAR_BELOW_ROWS, 128), F32), VMEM((NEAR_ABOVE_ROWS, 128), F32)],
+        [VMEM((UP_ROWS, 128), F32), VMEM((DOWN_ROWS, 128), F32)],
+        flat,
     )
     tables = filter_tables()
     crossing, volume, *held_tables = call(
@@ -523,21 +561,21 @@
     near_above = lax.ppermute(near_down, "ax", lower_ax)
     far_up, far_down = call(
         pack_far_planes,
-        [*fields, far_left],
+        [*fields, near_left, far_left],
         [VMEM((FAR_BELOW_ROWS, 128), F32), VMEM((FAR_ABOVE_ROWS, 128), F32)],
-        [VMEM(((TILES - 1) * ROWS, 128), F32)] * 4 + [DMA((4 * (TILES - 1),))],
+        [VMEM((TILES * ROWS, 128), F32)] * 4 + [DMA((4 * TILES,))],
     )
     (send,) = call(
         near_kernel,
         [*near_tiles, near_below, near_above, near_left, crossing],
         [free(4 * R_AX, 128)],
-        [VMEM((1, 36 * 8, 128), F32)] * 4 + [VMEM((ROWS, 128), F32)],
+        [VMEM((1, 36 * 8, 128), F32)] * 4 + [VMEM((ROWS, 128), F32)] + flat,
     )
     got = lax.all_to_all(send.reshape(R_AX, 4, 128), "az", 0, 0, tiled=True).reshape(4 * R_AX, 128)
 
     far_below = lax.ppermute(far_up, "ax", higher_ax)
     far_above = lax.ppermute(far_down, "ax", lower_ax)
-    far_inputs = [*fields, near_below, near_above, far_below, far_above, near_left, far_left]
+    far_inputs = [*fields, far_below, far_above, near_left, far_left]
     far_halos = [VMEM((TILES, 36 * 8, 128), F32)] * 4
     (first_columns,) = call(
         far_first_kernel, far_inputs, [VMEM((16, NR), F32)], far_halos + [VMEM((16, NR), F32)] * 4 + [DMA((4,))]

time: 54 us -> 63.6 us (1.18)
  blocking collectives: 0 us -> 27 us
  starting transfers between devices: 28.9 us -> 13.1 us
  waiting for transfers between devices: 10.5 us -> 9.23 us
    all_to_all x0 -> x1, blocking collectives: none -> 27 us  [local(): lax.all_to_all(send.reshape(R_AX, 4, 128), 'az', 0, 0, tiled=True)]
    all_to_all x1 -> x0, starting transfers between devices: 14.5 us -> none  [local(): lax.all_to_all(send.reshape(R_AX, 4, 128), 'az', 0, 0, tiled=True)]
    all_to_all x1 -> x0, waiting for transfers between devices: 5.87 us -> none  [local(): lax.all_to_all(send.reshape(R_AX, 4, 128), 'az', 0, 0, tiled=True)]
    ppermute x1, waiting for transfers between devices: 0.15 us -> 3.34 us  [local(): near_below = lax.ppermute(near_up, 'ax', higher_ax)]
    ppermute x1, starting transfers between devices: 3.1 us -> 0.1 us  [local(): near_left = lax.ppermute(near_right, 'az', higher_az)]
    ppermute x1, starting transfers between devices: 0.1 us -> 3.1 us  [local(): far_left = lax.ppermute(far_right, 'az', higher_az)]
    ppermute x1, waiting for transfers between devices: 0.02 us -> 2.25 us  [local(): near_left = lax.ppermute(near_right, 'az', higher_az)]
    ppermute x1, starting transfers between devices: 1.39 us -> 0.32 us  [local(): far_above = lax.ppermute(far_down, 'ax', lower_ax)]
  transfers between devices with their start and end apart: 9 -> 8, of which waited for: 4 -> 3; matrix products, arithmetic and copies ran while one was open for 0% -> 0% of each run, Pallas kernels for 23% -> 16%
where the time goes in v9:
time: 63.6 us; the launch traced here: 63.2 us
  blocking collectives  27 us (42%)
  Pallas kernels  13.8 us (22%)
  starting transfers between devices  13.1 us (21%)
  waiting for transfers between devices  9.23 us (15%)
    all_to_all x1, blocking collectives, local(): lax.all_to_all(send.reshape(R_AX, 4, 128), 'az', 0, 0, tiled=True)  27 us
    pallas_call x11, Pallas kernels, call(): pl.pallas_call(kernel, in_specs=specs, out_specs=out_specs, out_shape=lis...  13.8 us
    all_to_all x1, starting transfers between devices, local(): lax.all_to_all(back.reshape(R_AX, 2, 128), 'az', 0, 0, tiled=True)  4.88 us
    all_to_all x1, waiting for transfers between devices, local(): lax.all_to_all(back.reshape(R_AX, 2, 128), 'az', 0, 0, tiled=True)  3.63 us
    ppermute x1, waiting for transfers between devices, local(): near_below = lax.ppermute(near_up, 'ax', higher_ax)  3.34 us
    ppermute x1, starting transfers between devices, local(): far_left = lax.ppermute(far_right, 'az', higher_az)  3.1 us
    ppermute x1, waiting for transfers between devices, local(): near_left = lax.ppermute(near_right, 'az', higher_az)  2.25 us
    ppermute x1, starting transfers between devices, local(): near_above = lax.ppermute(near_down, 'ax', lower_ax)  1.38 us
  transfers between devices with their start and end apart: 8, of which 3 were waited for; matrix products, arithmetic and copies ran while one was open for 0% of the time, Pallas kernels for 16%

profile of v9, /device:TPU:1, one launch (start us, length us, event | category | flops | bytes accessed | tf_op | source)
XLA Modules:
  0.0 63.2 jit_solution(17594496766064795816)
XLA Ops:
  0.0 1.2 %shard_map.145 = (f32[256,128]{1,0:T(8,128)S(1)}, f32[256,128]{1,0:T(8,128)S(1)}, f32[256,128]{1,0:T(8,128)S(1)}, f32[256,128]{1,0:T(8,128)S(1)}, f32[120,384]{1,0:T(8,128)S(1)}) custom-call(f32[256,512]{1,0:T(8,128)} %bitcast.17, f32[256,512]{1,0:T(8,128)} %bitcast.22, f32[256,512]{1,0:T(8,128)} %bitcast.27, f32[256,512]{1,0:T(8,128)} %bitcast.32), custom_call_target="tpu_custom_call" | custom-call | flops 1000000 | bytes 3000000 | tf_op jit(solution)/shard_map/pallas_call | solution.py:503
  1.2 3.1 %collective-permute-start.3 = (f32[120,384]{1,0:T(8,128)S(1)}, f32[120,384]{1,0:T(8,128)S(1)}, u32[]{:S(2)}, u32[]{:S(2)}) collective-permute-start(f32[120,384]{1,0:T(8,128)S(1)} %get-tuple-element.40), channel_id=1, source_target_pairs={{0,1},{1,2},{2,3},{3,4},{4,5},{5,6},{6,7},{7,8},{8,9},{9,10},{10,1... | collective-permute-start | bytes 552968 | tf_op jit(solution)/shard_map/ppermute | solution.py:543
  4.3 0.8 %shard_map.146 = f32[120,128]{1,0:T(8,128)S(1)} custom-call(f32[256,512]{1,0:T(8,128)} %bitcast.18, f32[256,512]{1,0:T(8,128)} %bitcast.23, f32[256,512]{1,0:T(8,128)} %bitcast.28, f32[256,512]{1,0:T(8,128)} %bitcast.33), custom_call_target="tpu_custom_call" | custom-call | flops 1000000 | bytes 3000000 | tf_op jit(solution)/shard_map/pallas_call | solution.py:503
  5.1 0.1 collective-permute-start
  5.2 2.2 %collective-permute-done.refs_4_.refs_6_ = f32[120,128]{1,0:T(8,128)S(1)} collective-permute-done((f32[120,128]{1,0:T(8,128)S(1)}, f32[120,128]{1,0:T(8,128)S(1)}, u32[]{:S(2)}, u32[]{:S(2)}) %collective-permute-start) | collective-permute-done | bytes 61472 | tf_op jit(solution)/shard_map/ppermute | solution.py:535
  7.4 2.0 %shard_map.152 = (f32[864,128]{1,0:T(8,128)S(1)}, f32[720,128]{1,0:T(8,128)S(1)}) custom-call(f32[256,512]{1,0:T(8,128)} %bitcast.19, f32[256,512]{1,0:T(8,128)} %bitcast.24, f32[256,512]{1,0:T(8,128)} %bitcast.29, f32[256,512]{1,0:T(8,128)} %bitcast.34, f32[120,128]{1,0:T(8,128)S(1)} %collective-permute-done.refs_4_.refs_6_, ...), custom_call_target="tpu_custom_call" | custom-call | flops 1000000 | bytes 3000000 | tf_op jit(solution)/shard_map/pallas_call | solution.py:503
  9.4 1.4 %collective-permute-start.4 = (f32[864,128]{1,0:T(8,128)S(1)}, f32[864,128]{1,0:T(8,128)S(1)}, u32[]{:S(2)}, u32[]{:S(2)}) collective-permute-start(f32[864,128]{1,0:T(8,128)S(1)} %get-tuple-element.41), channel_id=1, source_target_pairs={{0,64},{64,128},{128,192},{192,0},{1,65},{65,129},{129,193},{193,1... | collective-permute-start | bytes 1327112 | tf_op jit(solution)/shard_map/ppermute | solution.py:576
  10.8 0.1 shard_map.147
  10.9 1.4 %collective-permute-start.1 = (f32[144,128]{1,0:T(8,128)S(1)}, f32[144,128]{1,0:T(8,128)S(1)}, u32[]{:S(2)}, u32[]{:S(2)}) collective-permute-start(f32[144,128]{1,0:T(8,128)S(1)} %get-tuple-element.29.refs_11_), channel_id=1, source_target_pairs={{0,64},{64,128},{128,192},{192,0},{1,65},{65,129},{129,193},{193,1... | collective-permute-start | bytes 221192 | tf_op jit(solution)/shard_map/ppermute | solution.py:560
  12.3 1.4 %collective-permute-start.2 = (f32[112,128]{1,0:T(8,128)S(1)}, f32[112,128]{1,0:T(8,128)S(1)}, u32[]{:S(2)}, u32[]{:S(2)}) collective-permute-start(f32[112,128]{1,0:T(8,128)S(1)} %get-tuple-element.30), channel_id=1, source_target_pairs={{64,0},{128,64},{192,128},{0,192},{65,1},{129,65},{193,129},{1,193... | collective-permute-start | bytes 172040 | tf_op jit(solution)/shard_map/ppermute | solution.py:561
  13.7 0.3 collective-permute-start.5
  14.0 1.3 %shard_map.148 = (f32[128,128]{1,0:T(8,128)S(1)}, f32[16,256]{1,0:T(8,128)S(1)}, bf16[80,64]{1,0:T(8,128)(2,1)S(1)}, bf16[80,64]{1,0:T(8,128)(2,1)S(1)}, bf16[25...) custom-call(s32[32,128]{1,0:T(8,128)S(1)} %copy-done, ...), custom_call_target="tpu_custom_call" | custom-call | flops 1000000 | bytes 3000000 | tf_op jit(solution)/shard_map/pallas_call | solution.py:503
  15.3 0.0 collective-permute-done.2.refs_5_
  15.3 3.3 %collective-permute-done.1.refs_4_ = f32[144,128]{1,0:T(8,128)S(1)} collective-permute-done((f32[144,128]{1,0:T(8,128)S(1)}, f32[144,128]{1,0:T(8,128)S(1)}, u32[]{:S(2)}, u32[]{:S(2)}) %collective-permute-start.1) | collective-permute-done | bytes 73760 | tf_op jit(solution)/shard_map/ppermute | solution.py:560
  18.7 0.6 shard_map.149
  19.3 27.0 %all_to_all.10 = f32[64,4,128]{2,1,0:T(4,128)S(1)} all-to-all(f32[64,4,128]{2,1,0:T(4,128)S(1)} %bitcast.13), channel_id=1, replica_groups=mesh['ax'=4,'az'=64] {'az'}, dimensions={0} | all-to-all | bytes 262144 | tf_op jit(solution)/shard_map/all_to_all | solution.py:574
  46.2 1.5 %shard_map.150 = f32[128,128]{1,0:T(8,128)} custom-call(f32[256,128]{1,0:T(8,128)S(1)} %bitcast.11, bf16[80,64]{1,0:T(8,128)(2,1)S(1)} %get-tuple-element.32.first_h, bf16[80,64]{1,0:T(8,128)(2,1)S(1)} %get-tuple-element.33.first_l, bf16[256,512]{1,0:T(8,128)(2,1)S(1)} %get-tuple-element.34.block_h, bf16[256,512]{1,0:T(8,128)(2,1)S(1)} %get-tuple-element.35.block_l, ...), custom_call_target="tpu_custom_call" | custom-call | flops 1000000 | bytes 3000000 | tf_op jit(solution)/shard_map/pallas_call | solution.py:503
  47.7 4.9 %all-to-all-start.1 = ((f32[64,2,128]{2,1,0:T(2,128)}), f32[64,2,128]{2,1,0:T(2,128)S(1)}, u32[]{:S(2)}, u32[]{:S(2)}) async-start(f32[64,2,128]{2,1,0:T(2,128)} %bitcast.8), calls=%async_computation.1 | async-start | bytes 131072 | tf_op jit(solution)/shard_map/all_to_all | solution.py:593
  52.6 1.1 %shard_map.154 = f32[16,512]{1,0:T(8,128)S(1)} custom-call(f32[256,512]{1,0:T(8,128)} %bitcast.20, f32[256,512]{1,0:T(8,128)} %bitcast.25, f32[256,512]{1,0:T(8,128)} %bitcast.30, f32[256,512]{1,0:T(8,128)} %bitcast.35, f32[864,128]{1,0:T(8,128)S(1)} %collective-permute-done.4.refs_4_, f32[720,128]{1,0:T(8,128)S(1)} %collective-permute-done.5.refs_5_, ...), custom_call_target="tpu_custom_call" | custom-call | flops 1000000 | bytes 3000000 | tf_op jit(solution)/shard_map/pallas_call | solution.py:503
  53.8 0.5 collective-permute-start.6
  54.3 0.4 shard_map.151.delta
  54.6 4.1 %shard_map.153 = (f32[256,512]{1,0:T(8,128)}, f32[240,128]{1,0:T(8,128)S(1)}) custom-call(f32[256,512]{1,0:T(8,128)} %bitcast.21, f32[256,512]{1,0:T(8,128)} %bitcast.26, f32[256,512]{1,0:T(8,128)} %bitcast.31, f32[256,512]{1,0:T(8,128)} %bitcast.36, f32[864,128]{1,0:T(8,128)S(1)} %collective-permute-done.4.refs_4_, ...), custom_call_target="tpu_custom_call" | custom-call | flops 4000000 | bytes 12000000 | tf_op jit(solution)/shard_map/pallas_call | solution.py:503
  58.8 3.6 %all-to-all-done.1 = f32[64,2,128]{2,1,0:T(2,128)S(1)} async-done(((f32[64,2,128]{2,1,0:T(2,128)}), f32[64,2,128]{2,1,0:T(2,128)S(1)}, u32[]{:S(2)}, u32[]{:S(2)}) %all-to-all-start.1) | async-done | bytes 65568 | tf_op jit(solution)/shard_map/all_to_all | solution.py:593
  62.4 0.8 %shard_map.155 = f32[256,512]{1,0:T(8,128)} custom-call(f32[128,128]{1,0:T(8,128)S(1)} %bitcast.14, f32[16,256]{1,0:T(8,128)S(1)} %shard_map.151.delta, f32[240,128]{1,0:T(8,128)S(1)} %get-tuple-element.43.swept, f32[16,512]{1,0:T(8,128)S(1)} %collective-permute-done.6.last, f32[256,512]{1,0:T(8,128)} %get-tuple-element.44._), custom_call_target="tpu_custom_call", output_to_operand_aliasing={{}: (4, {})} | custom-call | flops 1000000 | bytes 3000000 | tf_op jit(solution)/shard_map/pallas_call | solution.py:503
  (12 shorter events, 0.0 us)
Async XLA Ops:
  1.2 6.2 %collective-permute-start.3 = (f32[120,384]{1,0:T(8,128)S(1)}, f32[120,384]{1,0:T(8,128)S(1)}, u32[]{:S(2)}, u32[]{:S(2)}) collective-permute-start(f32[120,384]{1,0:T(8,128)S(1)} %get-tuple-element.40), channel_id=1, source_target_pairs={{0,1},{1,2},{2,3},{3,4},{4,5},{5,6},{6,7},{7,8},{8,9},{9,10},{10,1... | collective-permute-start | bytes 552968 | tf_op jit(solution)/shard_map/ppermute | solution.py:543
  5.1 2.3 %collective-permute-start = (f32[120,128]{1,0:T(8,128)S(1)}, f32[120,128]{1,0:T(8,128)S(1)}, u32[]{:S(2)}, u32[]{:S(2)}) collective-permute-start(f32[120,128]{1,0:T(8,128)S(1)} %shard_map.146), channel_id=1, source_target_pairs={{0,1},{1,2},{2,3},{3,4},{4,5},{5,6},{6,7},{7,8},{8,9},{9,10},{10,1... | collective-permute-start | bytes 184328 | tf_op jit(solution)/shard_map/ppermute | solution.py:535
  9.4 43.2 %collective-permute-start.4 = (f32[864,128]{1,0:T(8,128)S(1)}, f32[864,128]{1,0:T(8,128)S(1)}, u32[]{:S(2)}, u32[]{:S(2)}) collective-permute-start(f32[864,128]{1,0:T(8,128)S(1)} %get-tuple-element.41), channel_id=1, source_target_pairs={{0,64},{64,128},{128,192},{192,0},{1,65},{65,129},{129,193},{193,1... | collective-permute-start | bytes 1327112 | tf_op jit(solution)/shard_map/ppermute | solution.py:576
  10.8 3.3 %copy-start = (s32[32,128]{1,0:T(8,128)S(1)}, s32[32,128]{1,0:T(8,128)}, u32[]{:S(2)}) copy-start(s32[32,128]{1,0:T(8,128)} %refs_0_.1) | copy-start | bytes 49156
  10.8 3.3 %copy-start.1 = (f32[32,128]{1,0:T(8,128)S(1)}, f32[32,128]{1,0:T(8,128)}, u32[]{:S(2)}) copy-start(f32[32,128]{1,0:T(8,128)} %refs_1_.1) | copy-start | bytes 49156
  10.9 3.1 %copy-start.3 = (s32[32,8]{0,1:T(8,128)S(1)}, s32[32,8]{0,1:T(8,128)}, u32[]{:S(2)}) copy-start(s32[32,8]{0,1:T(8,128)} %param.22) | copy-start | bytes 3076
  10.9 3.1 %copy-start.2 = (s32[32,8]{0,1:T(8,128)S(1)}, s32[32,8]{0,1:T(8,128)}, u32[]{:S(2)}) copy-start(s32[32,8]{0,1:T(8,128)} %param.21) | copy-start | bytes 3076
  10.9 7.7 %collective-permute-start.1 = (f32[144,128]{1,0:T(8,128)S(1)}, f32[144,128]{1,0:T(8,128)S(1)}, u32[]{:S(2)}, u32[]{:S(2)}) collective-permute-start(f32[144,128]{1,0:T(8,128)S(1)} %get-tuple-element.29.refs_11_), channel_id=1, source_target_pairs={{0,64},{64,128},{128,192},{192,0},{1,65},{65,129},{129,193},{193,1... | collective-permute-start | bytes 221192 | tf_op jit(solution)/shard_map/ppermute | solution.py:560
  12.3 3.0 %collective-permute-start.2 = (f32[112,128]{1,0:T(8,128)S(1)}, f32[112,128]{1,0:T(8,128)S(1)}, u32[]{:S(2)}, u32[]{:S(2)}) collective-permute-start(f32[112,128]{1,0:T(8,128)S(1)} %get-tuple-element.30), channel_id=1, source_target_pairs={{64,0},{128,64},{192,128},{0,192},{65,1},{129,65},{193,129},{1,193... | collective-permute-start | bytes 172040 | tf_op jit(solution)/shard_map/ppermute | solution.py:561
  13.7 38.9 %collective-permute-start.5 = (f32[720,128]{1,0:T(8,128)S(1)}, f32[720,128]{1,0:T(8,128)S(1)}, u32[]{:S(2)}, u32[]{:S(2)}) collective-permute-start(f32[720,128]{1,0:T(8,128)S(1)} %get-tuple-element.42), channel_id=1, source_target_pairs={{64,0},{128,64},{192,128},{0,192},{65,1},{129,65},{193,129},{1,193... | collective-permute-start | bytes 1105928 | tf_op jit(solution)/shard_map/ppermute | solution.py:577
  47.7 14.7 %all-to-all-start.1 = ((f32[64,2,128]{2,1,0:T(2,128)}), f32[64,2,128]{2,1,0:T(2,128)S(1)}, u32[]{:S(2)}, u32[]{:S(2)}) async-start(f32[64,2,128]{2,1,0:T(2,128)} %bitcast.8), calls=%async_computation.1 | async-start | bytes 131072 | tf_op jit(solution)/shard_map/all_to_all | solution.py:593
  53.8 8.6 %collective-permute-start.6 = (f32[16,512]{1,0:T(8,128)S(1)}, f32[16,512]{1,0:T(8,128)S(1)}, u32[]{:S(2)}, u32[]{:S(2)}) collective-permute-start(f32[16,512]{1,0:T(8,128)S(1)} %shard_map.154), channel_id=1, source_target_pairs={{1,0},{2,1},{3,2},{4,3},{5,4},{6,5},{7,6},{8,7},{9,8},{10,9},{11,1... | collective-permute-start | bytes 98312 | tf_op jit(solution)/shard_map/ppermute | solution.py:583

commit v10 on v8

--- a/solution.py
+++ b/solution.py
@@ -404,6 +404,8 @@
 
 def dot3(a, b):
     (ah, al), (bh, bl) = a, b
+    if ah.shape[1] % 128 == 0:
+        return mm(jnp.concatenate([ah, al, ah], axis=1), jnp.concatenate([bh, bh, bl], axis=0))
     rows = ah.shape[0]
     both = mm(jnp.concatenate([ah, al], axis=0), bh)
     return both[:rows] + (both[rows:] + mm(ah, bl))

time: 54 us -> 53.9 us (level)
  no operation moved by 1% of the time
where the time goes in v10:
time: 53.9 us; the launch traced here: 53.5 us
  starting transfers between devices  28.9 us (54%)
  Pallas kernels  13.9 us (26%)
  waiting for transfers between devices  10.5 us (19%)
    all_to_all x1, starting transfers between devices, local(): lax.all_to_all(send.reshape(R_AX, 4, 128), 'az', 0, 0, tiled=True)  14.5 us
    pallas_call x11, Pallas kernels, call(): pl.pallas_call(kernel, in_specs=specs, out_specs=out_specs, out_shape=lis...  13.9 us
    all_to_all x1, waiting for transfers between devices, local(): lax.all_to_all(send.reshape(R_AX, 4, 128), 'az', 0, 0, tiled=True)  5.87 us
    all_to_all x1, starting transfers between devices, local(): lax.all_to_all(back.reshape(R_AX, 2, 128), 'az', 0, 0, tiled=True)  5.01 us
    all_to_all x1, waiting for transfers between devices, local(): lax.all_to_all(back.reshape(R_AX, 2, 128), 'az', 0, 0, tiled=True)  3.61 us
    ppermute x1, starting transfers between devices, local(): near_left = lax.ppermute(near_right, 'az', higher_az)  3.1 us
    ppermute x1, starting transfers between devices, local(): near_above = lax.ppermute(near_down, 'ax', lower_ax)  1.53 us
    ppermute x1, starting transfers between devices, local(): far_above = lax.ppermute(far_down, 'ax', lower_ax)  1.39 us
  transfers between devices with their start and end apart: 9, of which 4 were waited for; matrix products, arithmetic and copies ran while one was open for 0% of the time, Pallas kernels for 23%

profile of v10, /device:TPU:1, one launch (start us, length us, event | category | flops | bytes accessed | tf_op | source)
XLA Modules:
  0.0 53.5 jit_solution(11902281049081857785)
XLA Ops:
  0.0 0.8 %shard_map.146 = f32[120,128]{1,0:T(8,128)S(1)} custom-call(f32[256,512]{1,0:T(8,128)} %bitcast.16, f32[256,512]{1,0:T(8,128)} %bitcast.21, f32[256,512]{1,0:T(8,128)} %bitcast.26, f32[256,512]{1,0:T(8,128)} %bitcast.31), custom_call_target="tpu_custom_call" | custom-call | flops 1000000 | bytes 3000000 | tf_op jit(solution)/shard_map/pallas_call | solution.py:469
  0.8 3.1 %collective-permute-start = (f32[120,128]{1,0:T(8,128)S(1)}, f32[120,128]{1,0:T(8,128)S(1)}, u32[]{:S(2)}, u32[]{:S(2)}) collective-permute-start(f32[120,128]{1,0:T(8,128)S(1)} %shard_map.146), channel_id=1, source_target_pairs={{0,1},{1,2},{2,3},{3,4},{4,5},{5,6},{6,7},{7,8},{8,9},{9,10},{10,1... | collective-permute-start | bytes 184328 | tf_op jit(solution)/shard_map/ppermute | solution.py:501
  3.9 1.2 %shard_map.145 = (f32[256,128]{1,0:T(8,128)S(1)}, f32[256,128]{1,0:T(8,128)S(1)}, f32[256,128]{1,0:T(8,128)S(1)}, f32[256,128]{1,0:T(8,128)S(1)}, f32[120,384]{1,0:T(8,128)S(1)}) custom-call(f32[256,512]{1,0:T(8,128)} %bitcast.17, f32[256,512]{1,0:T(8,128)} %bitcast.22, f32[256,512]{1,0:T(8,128)} %bitcast.27, f32[256,512]{1,0:T(8,128)} %bitcast.32), custom_call_target="tpu_custom_call" | custom-call | flops 1000000 | bytes 3000000 | tf_op jit(solution)/shard_map/pallas_call | solution.py:469
  5.1 0.1 collective-permute-start.3
  5.2 0.1 shard_map.147
  5.3 1.4 %collective-permute-start.1 = (f32[216,128]{1,0:T(8,128)S(1)}, f32[216,128]{1,0:T(8,128)S(1)}, u32[]{:S(2)}, u32[]{:S(2)}) collective-permute-start(f32[216,128]{1,0:T(8,128)S(1)} %get-tuple-element.29.refs_11_), channel_id=1, source_target_pairs={{0,64},{64,128},{128,192},{192,0},{1,65},{65,129},{129,193},{193,1... | collective-permute-start | bytes 331784 | tf_op jit(solution)/shard_map/ppermute | solution.py:524
  6.7 1.5 %collective-permute-start.2 = (f32[184,128]{1,0:T(8,128)S(1)}, f32[184,128]{1,0:T(8,128)S(1)}, u32[]{:S(2)}, u32[]{:S(2)}) collective-permute-start(f32[184,128]{1,0:T(8,128)S(1)} %get-tuple-element.30), channel_id=1, source_target_pairs={{64,0},{128,64},{192,128},{0,192},{65,1},{129,65},{193,129},{1,193... | collective-permute-start | bytes 282632 | tf_op jit(solution)/shard_map/ppermute | solution.py:525
  8.2 1.3 %shard_map.148 = (f32[128,128]{1,0:T(8,128)S(1)}, f32[16,256]{1,0:T(8,128)S(1)}, bf16[80,64]{1,0:T(8,128)(2,1)S(1)}, bf16[80,64]{1,0:T(8,128)(2,1)S(1)}, bf16[25...) custom-call(s32[32,128]{1,0:T(8,128)S(1)} %copy-done, ...), custom_call_target="tpu_custom_call" | custom-call | flops 1000000 | bytes 3000000 | tf_op jit(solution)/shard_map/pallas_call | solution.py:469
  9.5 0.9 %collective-permute-done.2.refs_5_ = f32[184,128]{1,0:T(8,128)S(1)} collective-permute-done((f32[184,128]{1,0:T(8,128)S(1)}, f32[184,128]{1,0:T(8,128)S(1)}, u32[]{:S(2)}, u32[]{:S(2)}) %collective-permute-start.2) | collective-permute-done | bytes 94240 | tf_op jit(solution)/shard_map/ppermute | solution.py:525
  10.4 0.2 collective-permute-done.1.refs_4_
  10.5 1.1 %shard_map.149 = f32[256,128]{1,0:T(8,128)} custom-call(f32[256,128]{1,0:T(8,128)S(1)} %get-tuple-element.25.refs_0_, f32[256,128]{1,0:T(8,128)S(1)} %get-tuple-element.26.refs_1_, f32[256,128]{1,0:T(8,128)S(1)} %get-tuple-element.27.refs_2_, f32[256,128]{1,0:T(8,128)S(1)} %get-tuple-element.28.refs_3_, f32[216,128]{1,0:T(8,128)S(1)} %collective-permute-done.1.refs_4_, ...), custom_call_target="tpu_custom_call" | custom-call | flops 1000000 | bytes 3000000 | tf_op jit(solution)/shard_map/pallas_call | solution.py:469
  11.6 14.5 %all-to-all-start = ((f32[64,4,128]{2,1,0:T(4,128)}), f32[64,4,128]{2,1,0:T(4,128)S(1)}, u32[]{:S(2)}, u32[]{:S(2)}) async-start(f32[64,4,128]{2,1,0:T(4,128)} %bitcast.6), calls=%async_computation | async-start | bytes 262144 | tf_op jit(solution)/shard_map/all_to_all | solution.py:538
  26.1 1.7 %shard_map.152 = (f32[648,128]{1,0:T(8,128)S(1)}, f32[544,128]{1,0:T(8,128)S(1)}) custom-call(f32[256,512]{1,0:T(8,128)} %bitcast.18, f32[256,512]{1,0:T(8,128)} %bitcast.23, f32[256,512]{1,0:T(8,128)} %bitcast.28, f32[256,512]{1,0:T(8,128)} %bitcast.33, f32[120,384]{1,0:T(8,128)S(1)} %collective-permute-done.3.refs_4_.refs_9_), custom_call_target="tpu_custom_call" | custom-call | flops 1000000 | bytes 3000000 | tf_op jit(solution)/shard_map/pallas_call | solution.py:469
  27.9 1.4 %collective-permute-start.4 = (f32[648,128]{1,0:T(8,128)S(1)}, f32[648,128]{1,0:T(8,128)S(1)}, u32[]{:S(2)}, u32[]{:S(2)}) collective-permute-start(f32[648,128]{1,0:T(8,128)S(1)} %get-tuple-element.41), channel_id=1, source_target_pairs={{0,64},{64,128},{128,192},{192,0},{1,65},{65,129},{129,193},{193,1... | collective-permute-start | bytes 995336 | tf_op jit(solution)/shard_map/ppermute | solution.py:540
  29.2 1.4 %collective-permute-start.5 = (f32[544,128]{1,0:T(8,128)S(1)}, f32[544,128]{1,0:T(8,128)S(1)}, u32[]{:S(2)}, u32[]{:S(2)}) collective-permute-start(f32[544,128]{1,0:T(8,128)S(1)} %get-tuple-element.42), channel_id=1, source_target_pairs={{64,0},{128,64},{192,128},{0,192},{65,1},{129,65},{193,129},{1,193... | collective-permute-start | bytes 835592 | tf_op jit(solution)/shard_map/ppermute | solution.py:541
  30.6 5.9 %all-to-all-done = f32[64,4,128]{2,1,0:T(4,128)S(1)} async-done(((f32[64,4,128]{2,1,0:T(4,128)}), f32[64,4,128]{2,1,0:T(4,128)S(1)}, u32[]{:S(2)}, u32[]{:S(2)}) %all-to-all-start) | async-done | bytes 131104 | tf_op jit(solution)/shard_map/all_to_all | solution.py:538
  36.5 1.5 %shard_map.150 = f32[128,128]{1,0:T(8,128)} custom-call(f32[256,128]{1,0:T(8,128)S(1)} %bitcast.11, bf16[80,64]{1,0:T(8,128)(2,1)S(1)} %get-tuple-element.32.first_h, bf16[80,64]{1,0:T(8,128)(2,1)S(1)} %get-tuple-element.33.first_l, bf16[256,512]{1,0:T(8,128)(2,1)S(1)} %get-tuple-element.34.block_h, bf16[256,512]{1,0:T(8,128)(2,1)S(1)} %get-tuple-element.35.block_l, ...), custom_call_target="tpu_custom_call" | custom-call | flops 1000000 | bytes 3000000 | tf_op jit(solution)/shard_map/pallas_call | solution.py:469
  37.9 5.0 %all-to-all-start.1 = ((f32[64,2,128]{2,1,0:T(2,128)}), f32[64,2,128]{2,1,0:T(2,128)S(1)}, u32[]{:S(2)}, u32[]{:S(2)}) async-start(f32[64,2,128]{2,1,0:T(2,128)} %bitcast.8), calls=%async_computation.1 | async-start | bytes 131072 | tf_op jit(solution)/shard_map/all_to_all | solution.py:557
  43.0 1.1 %shard_map.154 = f32[16,512]{1,0:T(8,128)S(1)} custom-call(f32[256,512]{1,0:T(8,128)} %bitcast.19, f32[256,512]{1,0:T(8,128)} %bitcast.24, f32[256,512]{1,0:T(8,128)} %bitcast.29, f32[256,512]{1,0:T(8,128)} %bitcast.34, f32[216,128]{1,0:T(8,128)S(1)} %collective-permute-done.1.refs_4_, f32[184,128]{1,0:T(8,128)S(1)} %collective-permute-done.2.refs_5_, ...), custom_call_target="tpu_custom_call" | custom-call | flops 1000000 | bytes 3000000 | tf_op jit(solution)/shard_map/pallas_call | solution.py:469
  44.1 0.5 collective-permute-start.6
  44.6 0.4 shard_map.151.delta
  45.0 4.1 %shard_map.153 = (f32[256,512]{1,0:T(8,128)}, f32[240,128]{1,0:T(8,128)S(1)}) custom-call(f32[256,512]{1,0:T(8,128)} %bitcast.20, f32[256,512]{1,0:T(8,128)} %bitcast.25, f32[256,512]{1,0:T(8,128)} %bitcast.30, f32[256,512]{1,0:T(8,128)} %bitcast.35, f32[216,128]{1,0:T(8,128)S(1)} %collective-permute-done.1.refs_4_, ...), custom_call_target="tpu_custom_call" | custom-call | flops 4000000 | bytes 12000000 | tf_op jit(solution)/shard_map/pallas_call | solution.py:469
  49.1 3.6 %all-to-all-done.1 = f32[64,2,128]{2,1,0:T(2,128)S(1)} async-done(((f32[64,2,128]{2,1,0:T(2,128)}), f32[64,2,128]{2,1,0:T(2,128)S(1)}, u32[]{:S(2)}, u32[]{:S(2)}) %all-to-all-start.1) | async-done | bytes 65568 | tf_op jit(solution)/shard_map/all_to_all | solution.py:557
  52.7 0.8 %shard_map.155 = f32[256,512]{1,0:T(8,128)} custom-call(f32[128,128]{1,0:T(8,128)S(1)} %bitcast.13, f32[16,256]{1,0:T(8,128)S(1)} %shard_map.151.delta, f32[240,128]{1,0:T(8,128)S(1)} %get-tuple-element.43.swept, f32[16,512]{1,0:T(8,128)S(1)} %collective-permute-done.6.last, f32[256,512]{1,0:T(8,128)} %get-tuple-element.44._), custom_call_target="tpu_custom_call", output_to_operand_aliasing={{}: (4, {})} | custom-call | flops 1000000 | bytes 3000000 | tf_op jit(solution)/shard_map/pallas_call | solution.py:469
  (13 shorter events, 0.0 us)
Async XLA Ops:
  0.8 4.4 %collective-permute-start = (f32[120,128]{1,0:T(8,128)S(1)}, f32[120,128]{1,0:T(8,128)S(1)}, u32[]{:S(2)}, u32[]{:S(2)}) collective-permute-start(f32[120,128]{1,0:T(8,128)S(1)} %shard_map.146), channel_id=1, source_target_pairs={{0,1},{1,2},{2,3},{3,4},{4,5},{5,6},{6,7},{7,8},{8,9},{9,10},{10,1... | collective-permute-start | bytes 184328 | tf_op jit(solution)/shard_map/ppermute | solution.py:501
  5.1 21.0 %collective-permute-start.3 = (f32[120,384]{1,0:T(8,128)S(1)}, f32[120,384]{1,0:T(8,128)S(1)}, u32[]{:S(2)}, u32[]{:S(2)}) collective-permute-start(f32[120,384]{1,0:T(8,128)S(1)} %get-tuple-element.40), channel_id=1, source_target_pairs={{0,1},{1,2},{2,3},{3,4},{4,5},{5,6},{6,7},{7,8},{8,9},{9,10},{10,1... | collective-permute-start | bytes 552968 | tf_op jit(solution)/shard_map/ppermute | solution.py:509
  5.2 3.0 %copy-start = (s32[32,128]{1,0:T(8,128)S(1)}, s32[32,128]{1,0:T(8,128)}, u32[]{:S(2)}) copy-start(s32[32,128]{1,0:T(8,128)} %refs_0_.1) | copy-start | bytes 49156
  5.2 3.0 %copy-start.1 = (f32[32,128]{1,0:T(8,128)S(1)}, f32[32,128]{1,0:T(8,128)}, u32[]{:S(2)}) copy-start(f32[32,128]{1,0:T(8,128)} %refs_1_.1) | copy-start | bytes 49156
  5.2 3.0 %copy-start.3 = (s32[32,8]{0,1:T(8,128)S(1)}, s32[32,8]{0,1:T(8,128)}, u32[]{:S(2)}) copy-start(s32[32,8]{0,1:T(8,128)} %param.22) | copy-start | bytes 3076
  5.3 2.9 %copy-start.2 = (s32[32,8]{0,1:T(8,128)S(1)}, s32[32,8]{0,1:T(8,128)}, u32[]{:S(2)}) copy-start(s32[32,8]{0,1:T(8,128)} %param.21) | copy-start | bytes 3076
  5.3 5.2 %collective-permute-start.1 = (f32[216,128]{1,0:T(8,128)S(1)}, f32[216,128]{1,0:T(8,128)S(1)}, u32[]{:S(2)}, u32[]{:S(2)}) collective-permute-start(f32[216,128]{1,0:T(8,128)S(1)} %get-tuple-element.29.refs_11_), channel_id=1, source_target_pairs={{0,64},{64,128},{128,192},{192,0},{1,65},{65,129},{129,193},{193,1... | collective-permute-start | bytes 331784 | tf_op jit(solution)/shard_map/ppermute | solution.py:524
  6.7 3.7 %collective-permute-start.2 = (f32[184,128]{1,0:T(8,128)S(1)}, f32[184,128]{1,0:T(8,128)S(1)}, u32[]{:S(2)}, u32[]{:S(2)}) collective-permute-start(f32[184,128]{1,0:T(8,128)S(1)} %get-tuple-element.30), channel_id=1, source_target_pairs={{64,0},{128,64},{192,128},{0,192},{65,1},{129,65},{193,129},{1,193... | collective-permute-start | bytes 282632 | tf_op jit(solution)/shard_map/ppermute | solution.py:525
  11.6 24.9 %all-to-all-start = ((f32[64,4,128]{2,1,0:T(4,128)}), f32[64,4,128]{2,1,0:T(4,128)S(1)}, u32[]{:S(2)}, u32[]{:S(2)}) async-start(f32[64,4,128]{2,1,0:T(4,128)} %bitcast.6), calls=%async_computation | async-start | bytes 262144 | tf_op jit(solution)/shard_map/all_to_all | solution.py:538
  27.9 15.1 %collective-permute-start.4 = (f32[648,128]{1,0:T(8,128)S(1)}, f32[648,128]{1,0:T(8,128)S(1)}, u32[]{:S(2)}, u32[]{:S(2)}) collective-permute-start(f32[648,128]{1,0:T(8,128)S(1)} %get-tuple-element.41), channel_id=1, source_target_pairs={{0,64},{64,128},{128,192},{192,0},{1,65},{65,129},{129,193},{193,1... | collective-permute-start | bytes 995336 | tf_op jit(solution)/shard_map/ppermute | solution.py:540
  29.2 13.7 %collective-permute-start.5 = (f32[544,128]{1,0:T(8,128)S(1)}, f32[544,128]{1,0:T(8,128)S(1)}, u32[]{:S(2)}, u32[]{:S(2)}) collective-permute-start(f32[544,128]{1,0:T(8,128)S(1)} %get-tuple-element.42), channel_id=1, source_target_pairs={{64,0},{128,64},{192,128},{0,192},{65,1},{129,65},{193,129},{1,193... | collective-permute-start | bytes 835592 | tf_op jit(solution)/shard_map/ppermute | solution.py:541
  37.9 14.8 %all-to-all-start.1 = ((f32[64,2,128]{2,1,0:T(2,128)}), f32[64,2,128]{2,1,0:T(2,128)S(1)}, u32[]{:S(2)}, u32[]{:S(2)}) async-start(f32[64,2,128]{2,1,0:T(2,128)} %bitcast.8), calls=%async_computation.1 | async-start | bytes 131072 | tf_op jit(solution)/shard_map/all_to_all | solution.py:557
  44.1 5.0 %collective-permute-start.6 = (f32[16,512]{1,0:T(8,128)S(1)}, f32[16,512]{1,0:T(8,128)S(1)}, u32[]{:S(2)}, u32[]{:S(2)}) collective-permute-start(f32[16,512]{1,0:T(8,128)S(1)} %shard_map.154), channel_id=1, source_target_pairs={{1,0},{2,1},{3,2},{4,3},{5,4},{6,5},{7,6},{8,7},{9,8},{10,9},{11,1... | collective-permute-start | bytes 98312 | tf_op jit(solution)/shard_map/ppermute | solution.py:547
